TPU v7x, 32 devices: a whole 2x2x4 slice. The times are simulated.
32 devices in a mesh: expert: 4 (over x, core), shard: 8 (over z, y).
Axes of the slice: x: 2, y: 2, z: 4, core: 2. Of those that a mesh axis runs over, the one named last changes fastest.
Arguments:
- tokens: bfloat16 [8, 1024, 1536], P('shard', 'expert'), may hold values from -6 to 6
- segment_ids: int32 [8, 1024], P('shard', 'expert'), may hold values from 0 to 3, never falling along the last dimension, each value on 1 to 769 neighbouring positions
- routes: int32 [8, 1024, 8], P('shard', 'expert'), may hold values from 0 to 19, all different within a row; in each aligned block of 256 rows (0 to 255, 256 to 511, ..., all dimensions but the last counted through in order) at most 184 rows name the same one
- gain_attn: bfloat16 [1536], P('shard'), may hold values from 0.5 to 1.5
- w_query: bfloat16 [1536, 1536], P('shard'), may hold values from -0.15625 to 0.15625
- key_weight: bfloat16 [1536, 512], P('shard'), may hold values from -0.15625 to 0.15625
- value_weight: bfloat16 [1536, 512], P('shard'), may hold values from -0.15625 to 0.15625
- w_out: bfloat16 [1536, 1536], P('shard'), may hold values from -0.625 to 0.625
- gain_ffn: bfloat16 [1536], P('shard'), may hold values from 0.5 to 1.5
- w_router: bfloat16 [1536, 20], P('shard'), may hold values from -0.078125 to 0.078125
- w_gate_up: bfloat16 [1536, 20, 1024], P('shard', 'expert'), may hold values from -0.3125 to 0.3125
- w_down: bfloat16 [1536, 20, 512], P('shard', 'expert'), may hold values from -0.3125 to 0.3125
- cotangent: bfloat16 [8, 1024, 1536], P('shard', 'expert'), may hold values from -6 to 6
Outputs:
- mixed: bfloat16 [8, 1024, 1536], P('shard', 'expert')
- grad_tokens: bfloat16 [8, 1024, 1536], P('shard', 'expert')
- grad_gain_attn: float32 [1536], P(('expert', 'shard'))
- grad_query: float32 [1536, 1536], P(('expert', 'shard'))
- grad_key: float32 [1536, 512], P(('expert', 'shard'))
- grad_value: float32 [1536, 512], P(('expert', 'shard'))
- grad_out: float32 [1536, 1536], P(('expert', 'shard'))
- grad_gain_ffn: float32 [1536], P(('expert', 'shard'))
- grad_router: float32 [1536, 20], P(('expert', 'shard'))
- grad_gate_up: float32 [1536, 20, 1024], P('shard', 'expert')
- grad_down: float32 [1536, 20, 512], P('shard', 'expert')
Inputs may be any that keep to these rules, and one draw needn't show every extreme that they name: `routes`: each token names 8 different experts. Among the 256 token rows of one device no expert is named more than 184 times, and in every draw some device's rows name some expert exactly 184 times. `segment_ids`: document numbers never fall along a sequence; every document has at most 769 positions, and one of each sequence has exactly that many.
All inputs are finite; a program needn't handle non-finite values.
Results may differ from a plain program's by a relative error of at most 0.019.
Values may be sent and summed in bfloat16 or wider, within the bound.
No kernel may reach another device: no remote copies, remote signals or barrier semaphores. Data moves between devices by JAX's collectives and lax.ppermute only.
A program may use at most 448 MiB of HBM per device.

v0:
```python
import jax
import jax.numpy as jnp
from jax import lax
from jax.sharding import PartitionSpec as P

QUERY_HEADS = 24
KEY_VALUE_HEADS = 8
HEAD_SIZE = 64
FF = 512
TOP = 8
EXP_DEV = 5


epsilon = 1e-06


def normalize(vector):
    return vector * lax.rsqrt(jnp.mean(vector * vector, axis=-1, keepdims=True) + epsilon)


def norm_back(grad_normed, normed, source):
    inverse_rms = lax.rsqrt(jnp.mean(source * source, axis=-1, keepdims=True) + epsilon)
    return inverse_rms * (
        grad_normed - normed * jnp.mean(grad_normed * normed, axis=-1, keepdims=True)
    )


def rope_tables(positions):
    freqs = 10000.0 ** (-(jnp.arange(HEAD_SIZE // 2, dtype=jnp.float32) * 2.0 / HEAD_SIZE))
    angles = positions.astype(jnp.float32)[:, None] * freqs[None, :]
    return (jnp.cos(angles), jnp.sin(angles))


def apply_rotary(vector, cosine_lookup, sine_lookup):
    half_size = HEAD_SIZE // 2
    front_half = vector[..., :half_size]
    back_half = vector[..., half_size:]
    cosine_wide = cosine_lookup[:, None, :]
    sine_wide = sine_lookup[:, None, :]
    return jnp.concatenate(
        [
            front_half * cosine_wide - back_half * sine_wide,
            back_half * cosine_wide + front_half * sine_wide,
        ],
        -1,
    )


def inner(operand, other):
    return lax.dot_general(
        operand, other, (((0,), (0,)), ((), ())), preferred_element_type=jnp.float32
    )


def contract_fold(source, weight_piece):
    return jnp.einsum("erd,def->erf", source, weight_piece, preferred_element_type=jnp.float32)


def project_with(operand, weight_piece):
    return jnp.einsum("erf,def->erd", operand, weight_piece, preferred_element_type=jnp.float32)


def body(
    tokens,
    segment_ids,
    routes,
    gain_attn,
    w_query,
    key_weight,
    value_weight,
    w_out,
    gain_ffn,
    w_router,
    w_gate_up,
    w_down,
    cotangent,
):
    inputs = tokens[0].astype(jnp.float32)
    token_length = inputs.shape[0]
    model_width = inputs.shape[1]
    expert_count = lax.axis_size("expert")
    expert_place = lax.axis_index("expert")
    expert_total = EXP_DEV * expert_count
    capacity = (7 * token_length * TOP // (4 * expert_total) + 7) // 8 * 8
    query_group_width = QUERY_HEADS // KEY_VALUE_HEADS
    score_scale = HEAD_SIZE ** (-0.5)
    full_query, full_key, full_value, full_out, full_router, gain_one, gain_two = (
        lax.all_gather(w_query, "shard", axis=0, tiled=True),
        lax.all_gather(key_weight, "shard", axis=0, tiled=True),
        lax.all_gather(value_weight, "shard", axis=0, tiled=True),
        lax.all_gather(w_out, "shard", axis=0, tiled=True),
        lax.all_gather(w_router, "shard", axis=0, tiled=True),
        lax.all_gather(gain_attn, "shard", axis=0, tiled=True),
        lax.all_gather(gain_ffn, "shard", axis=0, tiled=True),
    )
    gain_one = gain_one.astype(jnp.float32)
    gain_two = gain_two.astype(jnp.float32)
    normed_one = normalize(inputs)
    normed_input_first = (normed_one * gain_one).astype(jnp.bfloat16)
    queries_raw = jnp.dot(
        normed_input_first, full_query, preferred_element_type=jnp.float32
    ).reshape(token_length, QUERY_HEADS, HEAD_SIZE)
    unrotated_keys = jnp.dot(
        normed_input_first, full_key, preferred_element_type=jnp.float32
    ).reshape(token_length, KEY_VALUE_HEADS, HEAD_SIZE)
    values_low = jnp.dot(normed_input_first, full_value, preferred_element_type=jnp.float32).astype(
        jnp.bfloat16
    )
    positions = expert_place * token_length + jnp.arange(token_length, dtype=jnp.int32)
    cosine_lookup, sine_lookup = rope_tables(positions)
    query_rows_reduced = apply_rotary(queries_raw, cosine_lookup, sine_lookup).astype(jnp.bfloat16)
    keys_low = (
        apply_rotary(unrotated_keys, cosine_lookup, sine_lookup)
        .astype(jnp.bfloat16)
        .reshape(token_length, KEY_VALUE_HEADS * HEAD_SIZE)
    )
    seg_local = segment_ids[0]
    gathered_keys, gathered_values, seg_all = (
        lax.all_gather(keys_low, "expert", axis=0, tiled=True),
        lax.all_gather(values_low, "expert", axis=0, tiled=True),
        lax.all_gather(seg_local.astype(jnp.bfloat16), "expert", axis=0, tiled=True),
    )
    key_count_total = gathered_keys.shape[0]
    seg_keys = seg_all.astype(jnp.int32)
    key_pos = jnp.arange(key_count_total, dtype=jnp.int32)
    allowed = (key_pos[None, :] <= positions[:, None]) & (seg_keys[None, :] == seg_local[:, None])
    query_head_rows = jnp.transpose(
        query_rows_reduced.reshape(token_length, KEY_VALUE_HEADS, query_group_width, HEAD_SIZE),
        (1, 0, 2, 3),
    )
    key_head_rows = jnp.transpose(
        gathered_keys.reshape(key_count_total, KEY_VALUE_HEADS, HEAD_SIZE), (1, 0, 2)
    )
    value_head_rows = jnp.transpose(
        gathered_values.reshape(key_count_total, KEY_VALUE_HEADS, HEAD_SIZE), (1, 0, 2)
    )

    def scores_of(query_one, key_one):
        scores = (
            jnp.einsum("tgd,sd->tgs", query_one, key_one, preferred_element_type=jnp.float32)
            * score_scale
        )
        return jnp.where(allowed[:, None, :], scores, -1e30)

    def forward_head(operands):
        query_one, key_one, value_one = operands
        scores = scores_of(query_one, key_one)
        row_peak = jnp.max(scores, axis=-1, keepdims=True)
        exponent = jnp.exp(scores - row_peak)
        summed = jnp.sum(exponent, axis=-1, keepdims=True)
        probabilities = exponent / summed
        result = jnp.einsum(
            "tgs,sd->tgd",
            probabilities.astype(jnp.bfloat16),
            value_one,
            preferred_element_type=jnp.float32,
        )
        return (result, row_peak[..., 0] + jnp.log(summed[..., 0]))

    attended_heads, logsum = lax.map(
        forward_head, (query_head_rows, key_head_rows, value_head_rows)
    )
    attended = (
        jnp.transpose(attended_heads, (1, 0, 2, 3))
        .reshape(token_length, QUERY_HEADS * HEAD_SIZE)
        .astype(jnp.bfloat16)
    )
    hidden_one = inputs + jnp.dot(attended, full_out, preferred_element_type=jnp.float32)
    normed_two = normalize(hidden_one)
    xn_two = (normed_two * gain_two).astype(jnp.bfloat16)
    logits = jnp.dot(xn_two, full_router, preferred_element_type=jnp.float32)
    route_ids = routes[0]
    choose = (
        route_ids[:, :, None] == jnp.arange(expert_total, dtype=jnp.int32)[None, None, :]
    ).astype(jnp.float32)
    chosen = jnp.sum(choose * logits[:, None, :], axis=2)
    gate_weights = jax.nn.softmax(chosen, axis=-1)
    flat_ids = route_ids.reshape(token_length * TOP)
    onehot = (flat_ids[:, None] == jnp.arange(expert_total, dtype=jnp.int32)[None, :]).astype(
        jnp.int32
    )
    earlier = jnp.cumsum(onehot, axis=0) - onehot
    slot_ranks = jnp.sum(earlier * onehot, axis=1)
    owners = flat_ids // EXP_DEV
    local_ids = flat_ids % EXP_DEV
    slot_index = local_ids * (expert_count * capacity) + owners * capacity + slot_ranks
    buffer_rows = EXP_DEV * expert_count * capacity

    def place(route_rows):
        filled = jnp.zeros((buffer_rows, model_width), jnp.bfloat16).at[slot_index].set(route_rows)
        return filled.reshape(EXP_DEV, expert_count * capacity, model_width)

    def pick(buffer):
        return buffer.reshape(buffer_rows, model_width)[slot_index].reshape(
            token_length, TOP, model_width
        )

    received = lax.all_to_all(
        place(jnp.repeat(xn_two, TOP, axis=0)), "expert", split_axis=1, concat_axis=1, tiled=True
    )
    gate_up = contract_fold(received, lax.all_gather(w_gate_up, "shard", axis=0, tiled=True))
    gate_part = gate_up[..., :FF]
    up_part = gate_up[..., FF:]
    sigmoid_part = jax.nn.sigmoid(gate_part)
    activated = (gate_part * sigmoid_part * up_part).astype(jnp.bfloat16)
    expert_out = project_with(activated, lax.all_gather(w_down, "shard", axis=0, tiled=True))
    returned = lax.all_to_all(
        expert_out.astype(jnp.bfloat16), "expert", split_axis=1, concat_axis=1, tiled=True
    )
    routed = pick(returned)
    expert_sum = jnp.sum(gate_weights[:, :, None] * routed.astype(jnp.float32), axis=1)
    mixed = (hidden_one + expert_sum).astype(jnp.bfloat16)[None]
    grad_y = cotangent[0].astype(jnp.float32)
    grad_gates = jnp.sum(grad_y[:, None, :] * routed.astype(jnp.float32), axis=2)
    grad_routed = (
        (gate_weights[:, :, None] * grad_y[:, None, :])
        .astype(jnp.bfloat16)
        .reshape(token_length * TOP, model_width)
    )
    grad_received = lax.all_to_all(
        place(grad_routed), "expert", split_axis=1, concat_axis=1, tiled=True
    )
    grad_act = contract_fold(grad_received, lax.all_gather(w_down, "shard", axis=0, tiled=True))
    grad_act = lax.optimization_barrier(grad_act.astype(jnp.bfloat16)).astype(jnp.float32)
    grad_gate = grad_act * up_part * sigmoid_part * (1.0 + gate_part * (1.0 - sigmoid_part))
    grad_up = grad_act * gate_part * sigmoid_part
    grad_gate_rows = jnp.concatenate([grad_gate, grad_up], axis=-1).astype(jnp.bfloat16)
    grad_input_rows = project_with(
        grad_gate_rows, lax.all_gather(w_gate_up, "shard", axis=0, tiled=True)
    )
    first_term = jnp.einsum(
        "erd,erf->def", received, grad_gate_rows, preferred_element_type=jnp.float32
    )
    second_term = jnp.einsum(
        "erd,erf->def", grad_received, activated, preferred_element_type=jnp.float32
    )
    expert_grads = lax.psum_scatter(
        jnp.concatenate([first_term, second_term], axis=2).astype(jnp.bfloat16),
        "shard",
        scatter_dimension=0,
        tiled=True,
    ).astype(jnp.float32)
    grad_returned = lax.all_to_all(
        grad_input_rows.astype(jnp.bfloat16), "expert", split_axis=1, concat_axis=1, tiled=True
    )
    grad_xn_two = jnp.sum(pick(grad_returned).astype(jnp.float32), axis=1)
    mean_term = jnp.sum(gate_weights * grad_gates, axis=-1, keepdims=True)
    grad_chosen = gate_weights * (grad_gates - mean_term)
    grad_logits = jnp.sum(choose * grad_chosen[:, :, None], axis=1).astype(jnp.bfloat16)
    grad_xn_two = grad_xn_two + jnp.dot(
        grad_logits, full_router.T, preferred_element_type=jnp.float32
    )
    grad_gain_two = jnp.sum(grad_xn_two * normed_two, axis=0)
    grad_hidden = grad_y + norm_back(grad_xn_two * gain_two, normed_two, hidden_one)
    grad_attn = grad_hidden.astype(jnp.bfloat16)
    gradient_attended = jnp.dot(grad_attn, full_out.T, preferred_element_type=jnp.float32).astype(
        jnp.bfloat16
    )
    gradient_heads = jnp.transpose(
        gradient_attended.reshape(token_length, KEY_VALUE_HEADS, query_group_width, HEAD_SIZE),
        (1, 0, 2, 3),
    )

    def backward_head(operands):
        query_one, key_one, value_one, grad_one, logsum_one = operands
        scores = scores_of(query_one, key_one)
        probabilities = jnp.exp(scores - logsum_one[..., None])
        grad_probs = jnp.einsum(
            "tgd,sd->tgs", grad_one, value_one, preferred_element_type=jnp.float32
        )
        grad_value_one = jnp.einsum(
            "tgs,tgd->sd",
            probabilities.astype(jnp.bfloat16),
            grad_one,
            preferred_element_type=jnp.float32,
        )
        grad_scores = probabilities * (
            grad_probs - jnp.sum(probabilities * grad_probs, axis=-1, keepdims=True)
        )
        grad_scores = grad_scores.astype(jnp.bfloat16)
        grad_query_one = (
            jnp.einsum("tgs,sd->tgd", grad_scores, key_one, preferred_element_type=jnp.float32)
            * score_scale
        )
        grad_key_one = (
            jnp.einsum("tgs,tgd->sd", grad_scores, query_one, preferred_element_type=jnp.float32)
            * score_scale
        )
        return (grad_query_one, grad_key_one, grad_value_one)

    grad_query_heads, gradient_key_heads, gradient_value_heads = lax.map(
        backward_head, (query_head_rows, key_head_rows, value_head_rows, gradient_heads, logsum)
    )
    gradient_key_total = jnp.transpose(gradient_key_heads, (1, 0, 2)).reshape(
        key_count_total, KEY_VALUE_HEADS * HEAD_SIZE
    )
    gradient_value_total = jnp.transpose(gradient_value_heads, (1, 0, 2)).reshape(
        key_count_total, KEY_VALUE_HEADS * HEAD_SIZE
    )
    gradient_key_local, grad_value_mine = (
        lax.psum_scatter(
            gradient_key_total.astype(jnp.bfloat16), "expert", scatter_dimension=0, tiled=True
        ).astype(jnp.float32),
        lax.psum_scatter(
            gradient_value_total.astype(jnp.bfloat16), "expert", scatter_dimension=0, tiled=True
        ).astype(jnp.float32),
    )
    grad_query_rot = jnp.transpose(grad_query_heads, (1, 0, 2, 3)).reshape(
        token_length, QUERY_HEADS, HEAD_SIZE
    )
    grad_query_low = (
        apply_rotary(grad_query_rot, cosine_lookup, -sine_lookup)
        .reshape(token_length, QUERY_HEADS * HEAD_SIZE)
        .astype(jnp.bfloat16)
    )
    grad_key_low = (
        apply_rotary(
            gradient_key_local.reshape(token_length, KEY_VALUE_HEADS, HEAD_SIZE),
            cosine_lookup,
            -sine_lookup,
        )
        .reshape(token_length, KEY_VALUE_HEADS * HEAD_SIZE)
        .astype(jnp.bfloat16)
    )
    grad_value_low = grad_value_mine.astype(jnp.bfloat16)
    grad_xn_one = jnp.dot(grad_query_low, full_query.T, preferred_element_type=jnp.float32)
    grad_xn_one = grad_xn_one + jnp.dot(
        grad_key_low, full_key.T, preferred_element_type=jnp.float32
    )
    grad_xn_one = grad_xn_one + jnp.dot(
        grad_value_low, full_value.T, preferred_element_type=jnp.float32
    )
    grad_gain_one = jnp.sum(grad_xn_one * normed_one, axis=0)
    grad_inputs = grad_hidden + norm_back(grad_xn_one * gain_one, normed_one, inputs)
    grad_projections = jnp.concatenate([grad_query_low, grad_key_low, grad_value_low], axis=1)
    gain_grads = jnp.stack([grad_gain_one, grad_gain_two], axis=1)
    packed = lax.psum_scatter(
        jnp.concatenate(
            [
                inner(normed_input_first, grad_projections),
                inner(attended, grad_attn),
                inner(xn_two, grad_logits),
                gain_grads,
            ],
            axis=1,
        ),
        ("expert", "shard"),
        scatter_dimension=0,
        tiled=True,
    )
    query_cols = QUERY_HEADS * HEAD_SIZE
    key_columns = KEY_VALUE_HEADS * HEAD_SIZE
    start_out = query_cols + 2 * key_columns
    start_router = start_out + model_width
    start_gains = start_router + expert_total
    return (
        mixed,
        grad_inputs.astype(jnp.bfloat16)[None],
        packed[:, start_gains],
        packed[:, :query_cols],
        packed[:, query_cols : query_cols + key_columns],
        packed[:, query_cols + key_columns : start_out],
        packed[:, start_out:start_router],
        packed[:, start_gains + 1],
        packed[:, start_router:start_gains],
        expert_grads[:, :, : 2 * FF],
        expert_grads[:, :, 2 * FF :],
    )


def solution(mesh):
    in_specs = (
        P("shard", "expert", None),
        P("shard", "expert"),
        P("shard", "expert", None),
        P("shard"),
        P("shard", None),
        P("shard", None),
        P("shard", None),
        P("shard", None),
        P("shard"),
        P("shard", None),
        P("shard", "expert", None),
        P("shard", "expert", None),
        P("shard", "expert", None),
    )
    out_specs = (
        P("shard", "expert", None),
        P("shard", "expert", None),
        P(("expert", "shard")),
        P(("expert", "shard"), None),
        P(("expert", "shard"), None),
        P(("expert", "shard"), None),
        P(("expert", "shard"), None),
        P(("expert", "shard")),
        P(("expert", "shard"), None),
        P("shard", "expert", None),
        P("shard", "expert", None),
    )
    return jax.shard_map(body, mesh=mesh, in_specs=in_specs, out_specs=out_specs, check_vma=False)
```

profile of v0, /device:TPU:0, one launch (start us, length us, event | category | flops | bytes accessed | tf_op | source)
XLA Modules:
  0.0 2144.6 jit_solution(15213039239234732598)
XLA Ops:
  12.3 23.4 %all-reduce.2 = (bf16[1536]{0:T(1024)(128)(2,1)S(1)}, bf16[1536]{0:T(1024)(128)(2,1)S(1)}) all-reduce(bf16[1536]{0:T(1024)(128)(2,1)S(1)} %dynamic-update-slice, bf16[1536]{0:T(1024)(128)(2,1)S(1)} %dynamic-update-slice.1), channel_id=1, replica_groups=mesh['expert'=4,'shard'=8] {'shard'}, use_global_device_ids=true, to_apply=%add | all-reduce | flops 3072 | bytes 12288
  37.2 19.7 all-gather.17.cloned.1.call-done
  61.3 40.7 %all-gather.13.cloned.1.call-done = bf16[1536,512]{1,0:T(8,128)(2,1)} async-done(((bf16[192,512]{1,0:T(8,128)(2,1)}), bf16[1536,512]{1,0:T(8,128)(2,1)}) %all-gather.13.cloned.1.call-update) | async-done | bytes 1572880 | tf_op jit(solution)/shard_map/all_gather | solution.py:89
  120.3 31.0 %all-gather.1 = bf16[8,192,20]{1,2,0:T(8,128)(2,1)S(1)} all-gather(bf16[1,192,20]{1,2,0:T(8,128)(2,1)S(1)} %bitcast.326), channel_id=1, replica_groups=mesh['expert'=4,'shard'=8] {'shard'}, dimensions={0}, use_global_device_ids=true | all-gather | bytes 69120 | tf_op jit(solution)/shard_map/all_gather | solution.py:92
  155.6 46.6 %all-gather.11.cloned.1.call-done = bf16[1536,1536]{1,0:T(8,128)(2,1)} async-done(((bf16[192,1536]{1,0:T(8,128)(2,1)}), bf16[1536,1536]{1,0:T(8,128)(2,1)}) %all-gather.11.cloned.1.call-update) | async-done | bytes 4718608 | tf_op jit(solution)/shard_map/all_gather | solution.py:88
  219.2 44.5 %while.30 = (s32[]{:T(128)}, bf16[8,256,3,64]{1,3,2,0:T(8,128)(2,1)S(1)}, f32[8,256,3]{1,2,0:T(4,128)}, bf16[8,256,3,64]{1,3,2,0:T(8,128)(2,1)}, bf16[8,1024,64]...) while((s32[]{:T(128)}, ...), condition=%wide.region_4.5_spmd.clone.clone, body=%wide.region_1.4_spmd.clone.sunk.clone | while | flops 211549440 | bytes 11079261 | solution.py:160
  263.7 37.5 %all-gather.21.cloned.1.call-done = bf16[1536,1536]{1,0:T(8,128)(2,1)} async-done(((bf16[192,1536]{1,0:T(8,128)(2,1)}), bf16[1536,1536]{1,0:T(8,128)(2,1)}) %all-gather.21.cloned.1.call-update) | async-done | bytes 4718608 | tf_op jit(solution)/shard_map/all_gather | solution.py:91
  308.3 17.7 scatter_custom_fusion.1
  326.0 34.1 %copy.164 = bf16[5,736,1536]{2,0,1:T(8,128)(2,1)} copy(bf16[5,736,1536]{2,1,0:T(8,128)(2,1)} %bitcast.286) | data formatting | bytes 22609920 | tf_op jit(solution)/shard_map/reshape | solution.py:191
  367.3 16.6 scatter_custom_fusion
  383.9 34.0 %copy.159 = bf16[5,736,1536]{2,0,1:T(8,128)(2,1)} copy(bf16[5,736,1536]{2,1,0:T(8,128)(2,1)} %bitcast.287) | data formatting | bytes 22609920 | tf_op jit(solution)/shard_map/reshape | solution.py:191
  417.9 146.5 %all-to-all-done.2 = bf16[5,736,1536]{2,0,1:T(8,128)(2,1)} async-done(((bf16[5,736,1536]{2,0,1:T(8,128)(2,1)}), bf16[5,736,1536]{2,0,1:T(8,128)(2,1)}, u32[]{:S(2)}, u32[]{:S(2)}) %all-to-all-start.2) | async-done | bytes 11304992 | tf_op jit(solution)/shard_map/all_to_all | solution.py:220
  571.8 18.1 fusion.81
  589.9 179.0 %all-to-all-done = bf16[5,736,1536]{2,0,1:T(8,128)(2,1)} async-done(((bf16[5,736,1536]{2,0,1:T(8,128)(2,1)}), bf16[5,736,1536]{2,0,1:T(8,128)(2,1)}, u32[]{:S(2)}, u32[]{:S(2)}) %all-to-all-start) | async-done | bytes 11304992 | tf_op jit(solution)/shard_map/all_to_all | solution.py:198
  768.9 28.6 %fusion.68 = f32[5,736,1024]{2,1,0:T(8,128)} fusion(bf16[1536,5,1024]{2,0,1:T(8,128)(2,1)} %all-gather.23.cloned.1.call-done, bf16[5,736,1536]{2,0,1:T(8,128)(2,1)} %all-to-all-done), kind=kOutput, calls=%fused_computation.92 | convolution fusion | flops 11576279040 | bytes 42106880 | tf_op jit(solution)/shard_map/erd,def->erf/dot_general | solution.py:56
  821.6 34.0 %copy.161 = bf16[5,736,1536]{2,0,1:T(8,128)(2,1)} copy(bf16[5,736,1536]{2,1,0:T(8,128)(2,1)} %convolution_convert_fusion) | data formatting | bytes 22609920 | tf_op jit(solution)/shard_map/convert_element_type | solution.py:208
  862.9 22.4 %convolution_convert_fusion.1 = bf16[5,736,1536]{2,1,0:T(8,128)(2,1)} fusion(bf16[1536,5,1024]{2,0,1:T(8,128)(2,1)} %all-gather.23.cloned.1.call-done, bf16[5,736,512]{2,1,0:T(8,128)(2,1)} %get-tuple-element.283, bf16[5,736,512]{2,1,0:T(8,128)(2,1)} %get-tuple-element.282), kind=kOutput, calls=%fused_computation.70 | convolution fusion | flops 11597004800 | bytes 34570240 | tf_op jit(solution)/shard_map/erf,def->erd/dot_general | solution.py:60
  885.3 34.0 %copy.166 = bf16[5,736,1536]{2,0,1:T(8,128)(2,1)} copy(bf16[5,736,1536]{2,1,0:T(8,128)(2,1)} %convolution_convert_fusion.1) | data formatting | bytes 22609920 | tf_op jit(solution)/shard_map/convert_element_type | solution.py:244
  919.3 140.7 %all-to-all-done.1 = bf16[5,736,1536]{2,0,1:T(8,128)(2,1)} async-done(((bf16[5,736,1536]{2,0,1:T(8,128)(2,1)}), bf16[5,736,1536]{2,0,1:T(8,128)(2,1)}, u32[]{:S(2)}, u32[]{:S(2)}) %all-to-all-start.1) | async-done | bytes 11304992 | tf_op jit(solution)/shard_map/all_to_all | solution.py:207
  1067.4 14.5 copy.162
  1081.9 19.1 gather_fusion
  1110.7 153.7 %all-to-all-done.3 = bf16[5,736,1536]{2,0,1:T(8,128)(2,1)} async-done(((bf16[5,736,1536]{2,0,1:T(8,128)(2,1)}), bf16[5,736,1536]{2,0,1:T(8,128)(2,1)}, u32[]{:S(2)}, u32[]{:S(2)}) %all-to-all-start.3) | async-done | bytes 11304992 | tf_op jit(solution)/shard_map/all_to_all | solution.py:243
  1278.6 19.3 gather_fusion.1
  1309.7 82.0 %while.31 = (s32[]{:T(128)}, f32[8,256,3,64]{1,3,2,0:T(8,128)}, bf16[8,1024,64]{1,2,0:T(8,128)(2,1)}, bf16[8,1024,64]{1,2,0:T(8,128)(2,1)}, bf16[8,256,3,64]{1,3...) while((s32[]{:T(128)}, f32[8,256,3,64]{1,3,2,0:T(8,128)}, ...), condition=%wide.region_22.23_spmd.clone.clone, body=%wide.region_20.22_spmd.clone.sunk.clone | while | flops 511294720 | bytes 25651320 | solution.py:291
  1418.7 22.8 %reduce-scatter.9.cloned.1.call-done = bf16[256,512]{0,1:T(8,128)(2,1)} async-done(((bf16[1024,512]{0,1:T(8,128)(2,1)}), bf16[256,512]{0,1:T(8,128)(2,1)}) %reduce-scatter.9.cloned.1.call-update) | async-done | bytes 262160 | tf_op jit(solution)/shard_map/reduce_scatter | solution.py:304
  1454.6 27.9 %concatenate.43 = f32[1536,4118]{1,0:T(8,128)} concatenate(f32[1536,2560]{1,0:T(8,128)} %fusion.100, f32[1536,1536]{1,0:T(8,128)} %fusion.109, f32[1536,20]{1,0:T(8,128)} %fusion.138, f32[1536,1]{1,0:T(8,128)} %stack.8, f32[1536,1]{1,0:T(8,128)} %stack.9), dimensions={1} | concatenate | bytes 50601984 | tf_op jit(solution)/shard_map/concatenate | solution.py:338
  1482.6 16.2 convert_bitcast_fusion.1
  1498.8 42.6 %convert_bitcast_fusion = bf16[1536,5,1024]{0,2,1:T(8,128)(2,1)} fusion(bf16[5,736,1536]{2,0,1:T(8,128)(2,1)} %all-to-all-done, bf16[5,736,512]{2,1,0:T(8,128)(2,1)} %get-tuple-element.283, bf16[5,736,512]{2,1,0:T(8,128)(2,1)} %get-tuple-element.282), kind=kOutput, calls=%fused_computation.68 | convolution fusion | flops 11599216640 | bytes 34570240 | tf_op jit(solution)/shard_map/erd,erf->def/dot_general | solution.py:231
  1541.4 20.0 pad_maximum_fusion
  1561.4 30.3 %copy.185 = bf16[1536,7680]{1,0:T(8,128)(2,1)} copy(bf16[1536,7680]{0,1:T(8,128)(2,1)} %bitcast.285) | data formatting | bytes 47185920
  1594.5 140.5 %reduce-scatter.11.cloned.1.call-done = f32[48,4118]{1,0:T(8,128)} async-done(((f32[1536,4118]{1,0:T(8,128)}), f32[48,4118]{1,0:T(8,128)}) %reduce-scatter.11.cloned.1.call-update) | async-done | bytes 790672 | tf_op jit(solution)/shard_map/reduce_scatter | solution.py:337
  1741.4 378.0 %reduce-scatter.13.cloned.1.call-done = bf16[192,7680]{1,0:T(8,128)(2,1)} async-done(((bf16[1536,7680]{1,0:T(8,128)(2,1)}), bf16[192,7680]{1,0:T(8,128)(2,1)}) %reduce-scatter.13.cloned.1.call-update) | async-done | bytes 2949136
  (340 shorter events, 338.7 us)
Async XLA Ops:
  7.2 49.7 %all-gather.17.cloned.1.call-start = ((), (), s32[]{:S(2)}) async-start(), calls=%async_computation.11 | async-start | bytes 1769472 | tf_op jit(solution)/shard_map/all_gather | solution.py:90
  7.9 94.1 %all-gather.13.cloned.1.call-start = ((), (), s32[]{:S(2)}) async-start(), calls=%async_computation.9 | async-start | bytes 1769472 | tf_op jit(solution)/shard_map/all_gather | solution.py:89
  8.7 144.3 %all-gather.19.cloned.1.call-start = ((), (), s32[]{:S(2)}) async-start(), calls=%async_computation.12 | async-start | bytes 1310720 | tf_op jit(solution)/shard_map/all_gather | solution.py:120
  35.8 173.1 %copy-start.24 = (f32[1536]{0:T(1024)}, f32[1536]{0:T(1024)S(1)}, u32[]{:S(2)}) copy-start(f32[1536]{0:T(1024)S(1)} %convert_element_type.177) | copy-start | bytes 18436
  37.2 171.7 %copy-start.37 = (f32[256]{0:T(256)}, f32[256]{0:T(256)S(1)}, u32[]{:S(2)}) copy-start(f32[256]{0:T(256)S(1)} %add_rsqrt_fusion.1) | copy-start | bytes 3076
  37.2 66.6 %copy-start.3 = (bf16[1,256,1536]{2,1,0:T(8,128)(2,1)S(1)}, bf16[1,256,1536]{2,1,0:T(8,128)(2,1)}, u32[]{:S(2)}) copy-start(bf16[1,256,1536]{2,1,0:T(8,128)(2,1)} %param.17) | copy-start | bytes 2359300
  59.8 142.4 %all-gather.11.cloned.1.call-start = ((), (), s32[]{:S(2)}) async-start(), calls=%async_computation.8 | async-start | bytes 5308416 | tf_op jit(solution)/shard_map/all_gather | solution.py:88
  60.4 158.8 %all-gather.15.cloned.1.call-start = ((), (), s32[]{:S(2)}) async-start(), calls=%async_computation.10 | async-start | bytes 1310720 | tf_op jit(solution)/shard_map/all_gather | solution.py:119
  61.3 151.6 %copy-start.18 = (f32[256,32]{0,1:T(8,128)}, f32[256,32]{0,1:T(8,128)S(1)}, u32[]{:S(2)}) copy-start(f32[256,32]{0,1:T(8,128)S(1)} %get-tuple-element.303) | copy-start | bytes 98308
  105.3 195.9 %all-gather.21.cloned.1.call-start = ((), (), s32[]{:S(2)}) async-start(), calls=%async_computation.13 | async-start | bytes 5308416 | tf_op jit(solution)/shard_map/all_gather | solution.py:91
  105.9 465.9 %all-gather.25.cloned.1.call-start = ((), (), s32[]{:S(2)}) async-start(), calls=%async_computation.15 | async-start | bytes 8847360 | tf_op jit(solution)/shard_map/all_gather | solution.py:206
  106.7 662.2 %all-gather.23.cloned.1.call-start = ((), (), s32[]{:S(2)}) async-start(), calls=%async_computation.14 | async-start | bytes 17694720 | tf_op jit(solution)/shard_map/all_gather | solution.py:201
  113.0 192.1 %copy-start.31 = (f32[1536]{0:T(1024)}, f32[1536]{0:T(1024)S(1)}, u32[]{:S(2)}) copy-start(f32[1536]{0:T(1024)S(1)} %convert_element_type.187) | copy-start | bytes 18436
  151.4 155.0 %copy-start.20 = (bf16[1536,20]{0,1:T(8,128)(2,1)}, bf16[1536,20]{0,1:T(8,128)(2,1)S(1)}, u32[]{:S(2)}) copy-start(bf16[1536,20]{0,1:T(8,128)(2,1)S(1)} %reshape.524) | copy-start | bytes 184324
  152.8 155.5 %copy-start.5 = (f32[256,1536]{1,0:T(8,128)}, f32[256,1536]{1,0:T(8,128)S(1)}, u32[]{:S(2)}) copy-start(f32[256,1536]{1,0:T(8,128)S(1)} %bitcast_convert_fusion) | copy-start | bytes 4718596
  263.7 41.4 %copy-start.7 = (bf16[8,256,3,64]{1,3,2,0:T(8,128)(2,1)}, bf16[8,256,3,64]{1,3,2,0:T(8,128)(2,1)S(1)}, u32[]{:S(2)}) copy-start(bf16[8,256,3,64]{1,3,2,0:T(8,128)(2,1)S(1)} %get-tuple-element.103) | copy-start | bytes 2359300
  263.7 41.4 %copy-start.22 = (s32[1024]{0:T(1024)}, s32[1024]{0:T(1024)S(1)}, u32[]{:S(2)}) copy-start(s32[1024]{0:T(1024)S(1)} %get-tuple-element.607) | copy-start | bytes 12292
  263.7 41.4 %copy-start.35 = (s32[256]{0:T(256)}, s32[256]{0:T(256)S(1)}, u32[]{:S(2)}) copy-start(s32[256]{0:T(256)S(1)} %get-tuple-element.616) | copy-start | bytes 3076
  306.4 60.9 %copy-start.9 = (bf16[256,1536]{1,0:T(8,128)(2,1)}, bf16[256,1536]{1,0:T(8,128)(2,1)S(1)}, u32[]{:S(2)}) copy-start(bf16[256,1536]{1,0:T(8,128)(2,1)S(1)} %multiply_convert_fusion.2) | copy-start | bytes 2359300
  360.1 204.3 %all-to-all-start.2 = ((bf16[5,736,1536]{2,0,1:T(8,128)(2,1)}), bf16[5,736,1536]{2,0,1:T(8,128)(2,1)}, u32[]{:S(2)}, u32[]{:S(2)}) async-start(bf16[5,736,1536]{2,0,1:T(8,128)(2,1)} %copy.164), calls=%async_computation.2 | async-start | bytes 36175872 | tf_op jit(solution)/shard_map/all_to_all | solution.py:220
  564.4 204.4 %all-to-all-start = ((bf16[5,736,1536]{2,0,1:T(8,128)(2,1)}), bf16[5,736,1536]{2,0,1:T(8,128)(2,1)}, u32[]{:S(2)}, u32[]{:S(2)}) async-start(bf16[5,736,1536]{2,0,1:T(8,128)(2,1)} %copy.159), calls=%async_computation | async-start | bytes 36175872 | tf_op jit(solution)/shard_map/all_to_all | solution.py:198
  855.6 204.5 %all-to-all-start.1 = ((bf16[5,736,1536]{2,0,1:T(8,128)(2,1)}), bf16[5,736,1536]{2,0,1:T(8,128)(2,1)}, u32[]{:S(2)}, u32[]{:S(2)}) async-start(bf16[5,736,1536]{2,0,1:T(8,128)(2,1)} %copy.161), calls=%async_computation.1 | async-start | bytes 36175872 | tf_op jit(solution)/shard_map/all_to_all | solution.py:207
  1060.0 204.3 %all-to-all-start.3 = ((bf16[5,736,1536]{2,0,1:T(8,128)(2,1)}), bf16[5,736,1536]{2,0,1:T(8,128)(2,1)}, u32[]{:S(2)}, u32[]{:S(2)}) async-start(bf16[5,736,1536]{2,0,1:T(8,128)(2,1)} %copy.166), calls=%async_computation.3 | async-start | bytes 36175872 | tf_op jit(solution)/shard_map/all_to_all | solution.py:243
  1067.3 346.7 %reduce-scatter.7.cloned.1.call-start = ((), (), s32[]{:S(2)}) async-start(), calls=%async_computation.16 | async-start | bytes 1310720 | tf_op jit(solution)/shard_map/reduce_scatter | solution.py:301
  1309.7 82.9 %copy-start.19 = (f32[256,32]{0,1:T(8,128)S(1)}, f32[256,32]{0,1:T(8,128)}, u32[]{:S(2)}) copy-start(f32[256,32]{0,1:T(8,128)} %copy-done.18) | copy-start | bytes 98308
  1309.7 82.9 %copy-start.26 = (f32[256,32]{0,1:T(8,128)S(1)}, f32[256,32]{0,1:T(8,128)}, u32[]{:S(2)}) copy-start(f32[256,32]{0,1:T(8,128)} %get-tuple-element.301) | copy-start | bytes 98308
  1391.7 49.7 %reduce-scatter.9.cloned.1.call-start = ((), (), s32[]{:S(2)}) async-start(), calls=%async_computation.17 | async-start | bytes 1310720 | tf_op jit(solution)/shard_map/reduce_scatter | solution.py:304
  1392.3 342.7 %reduce-scatter.11.cloned.1.call-start = ((), (), s32[]{:S(2)}) async-start(), calls=%async_computation.18 | async-start | bytes 26763264 | tf_op jit(solution)/shard_map/reduce_scatter | solution.py:337
  1415.1 26.4 %copy-start.4 = (bf16[1,256,1536]{2,1,0:T(8,128)(2,1)S(1)}, bf16[1,256,1536]{2,1,0:T(8,128)(2,1)}, u32[]{:S(2)}) copy-start(bf16[1,256,1536]{2,1,0:T(8,128)(2,1)} %param.17) | copy-start | bytes 2359300
  1415.1 26.4 %copy-start.25 = (f32[1536]{0:T(1024)S(1)}, f32[1536]{0:T(1024)}, u32[]{:S(2)}) copy-start(f32[1536]{0:T(1024)} %copy-done.24) | copy-start | bytes 18436
  1415.1 26.3 %copy-start.38 = (f32[256]{0:T(256)S(1)}, f32[256]{0:T(256)}, u32[]{:S(2)}) copy-start(f32[256]{0:T(256)} %copy-done.37) | copy-start | bytes 3076
  1482.6 636.8 %reduce-scatter.13.cloned.1.call-start = ((), (), s32[]{:S(2)}) async-start(), calls=%async_computation.19 | async-start | bytes 26542080
  (32 other events, 206.7 us)
Sparse Core Ops, SparseCore 0:
  10.2 46.6 all-gather.16
  59.0 42.9 all-gather.12
  104.2 15.5 all-gather.18
  121.8 80.3 all-gather.10
  204.2 14.9 all-gather.14
  221.2 79.9 all-gather.20
  303.4 116.5 all-gather.24
  422.2 212.9 all-gather.22
  1391.8 22.1 reduce-scatter.6
  1416.5 24.8 reduce-scatter.8
  1482.7 252.1 reduce-scatter.10
  1738.7 380.6 reduce-scatter.12
where the time goes:
time: 2150 us; the launch traced here: 2140 us
  waiting for transfers between devices  1320 us (61%)
  local copies, waits for them, and re-layouts  330 us (15%)
  matrix products  283 us (13%)
  other arithmetic  104 us (5%)
  blocking collectives  59.5 us (3%)
  starting transfers between devices  29.8 us (1%)
    unnamed x13, waiting for transfers between devices  382 us
    all_to_all x1, waiting for transfers between devices, body(): lax.all_to_all(place(jnp.repeat(xn_two, TOP, axis=0)), 'expert', split_ax...  179 us
    all_to_all x1, waiting for transfers between devices, body(): lax.all_to_all(grad_input_rows.astype(jnp.bfloat16), 'expert', split_axis...  154 us
    all_to_all x1, waiting for transfers between devices, body(): lax.all_to_all(place(grad_routed), 'expert', split_axis=1, concat_axis=1,...  147 us
    all_to_all x1, waiting for transfers between devices, body(): lax.all_to_all(expert_out.astype(jnp.bfloat16), 'expert', split_axis=1, c...  141 us
    reduce_scatter x1, waiting for transfers between devices, body(): lax.psum_scatter(jnp.concatenate([inner(normed_input_first, grad_projecti...  141 us
    reshape x2, local copies, waits for them, and re-layouts, place(): return filled.reshape(EXP_DEV, expert_count * capacity, model_width)  68.1 us
    unnamed x111, local copies, waits for them, and re-layouts  50.4 us
  transfers between devices with their start and end apart: 16, of which 13 were waited for; matrix products, arithmetic and copies ran while one was open for 21% of the time, Pallas kernels for 0%

commit v1 on v0

v1 whole, which is shorter than its diff:
```python
import functools

import jax
import jax.numpy as jnp
from jax import lax
from jax.experimental import pallas as pl
from jax.experimental.pallas import tpu as pltpu
from jax.sharding import PartitionSpec as P

QUERY_HEADS = 24
KEY_VALUE_HEADS = 8
GROUP = QUERY_HEADS // KEY_VALUE_HEADS
HEAD_SIZE = 64
HALF = HEAD_SIZE // 2
FF = 512
TOP = 8
EXP_DEV = 5
BLOCK = 256
MASKED = -1e30
epsilon = 1e-06


def dot(a, b, ca, cb):
    return lax.dot_general(a, b, (((ca,), (cb,)), ((), ())), preferred_element_type=jnp.float32)


def inverse_rms(v):
    return lax.rsqrt(jnp.mean(v * v, axis=-1, keepdims=True) + epsilon)


def allowed_tile(seg_col, seg_row, qi, ki):
    keys = seg_col[pl.ds(ki * BLOCK, BLOCK), :]
    queries = seg_row[:, pl.ds(qi * BLOCK, BLOCK)]
    ok = keys == queries
    if qi == ki:
        kpos = lax.broadcasted_iota(jnp.int32, (BLOCK, BLOCK), 0)
        qpos = lax.broadcasted_iota(jnp.int32, (BLOCK, BLOCK), 1)
        ok = ok & (kpos <= qpos)
    return ok


def attention_forward_kernel(blocks, q_ref, k_ref, v_ref, seg_col, seg_row, o_ref, lse_ref):
    keys = k_ref[0].astype(jnp.float32).T.astype(jnp.bfloat16)
    for qi in range(blocks):
        qs = slice(qi * BLOCK, (qi + 1) * BLOCK)
        q = q_ref[0, :, qs]
        top = total = acc = None
        for ki in range(qi, -1, -1):
            ks = slice(ki * BLOCK, (ki + 1) * BLOCK)
            s = dot(keys[ks, :], q, 1, 0)
            s = jnp.where(allowed_tile(seg_col, seg_row, qi, ki), s, MASKED)
            peak = jnp.max(s, axis=0, keepdims=True)
            if top is None:
                top = peak
                e = jnp.exp(s - top)
                total = jnp.sum(e, axis=0, keepdims=True)
                acc = dot(v_ref[0, :, ks], e.astype(jnp.bfloat16), 1, 0)
            else:
                new = jnp.maximum(top, peak)
                scale = jnp.exp(top - new)
                e = jnp.exp(s - new)
                total = total * scale + jnp.sum(e, axis=0, keepdims=True)
                acc = acc * scale + dot(v_ref[0, :, ks], e.astype(jnp.bfloat16), 1, 0)
                top = new
        o_ref[0, :, qs] = (acc / total).astype(jnp.bfloat16)
        lse_ref[0, :, qs] = top + jnp.log(total)


def attention_forward(q, k, v, seg):
    heads, _, length = q.shape
    blocks = length // BLOCK
    full = pl.BlockSpec((1, HEAD_SIZE, length), lambda h: (h, 0, 0))
    shared = pl.BlockSpec((1, HEAD_SIZE, length), lambda h: (h // GROUP, 0, 0))
    return pl.pallas_call(
        functools.partial(attention_forward_kernel, blocks),
        grid=(heads,),
        in_specs=[
            full,
            shared,
            shared,
            pl.BlockSpec((length, 1), lambda h: (0, 0)),
            pl.BlockSpec((1, length), lambda h: (0, 0)),
        ],
        out_specs=[full, pl.BlockSpec((1, 1, length), lambda h: (h, 0, 0))],
        out_shape=[
            jax.ShapeDtypeStruct((heads, HEAD_SIZE, length), jnp.bfloat16),
            jax.ShapeDtypeStruct((heads, 1, length), jnp.float32),
        ],
        compiler_params=pltpu.CompilerParams(vmem_limit_bytes=48 * 1024 * 1024),
        cost_estimate=pl.CostEstimate(
            flops=4 * heads * length * length * HEAD_SIZE,
            bytes_accessed=6 * heads * length * HEAD_SIZE,
            transcendentals=heads * length * length // 2,
        ),
        name="attention_forward",
    )(q, k, v, seg[:, None], seg[None, :])


def attention_backward_kernel(
    blocks, q_ref, k_ref, v_ref, o_ref, g_ref, lse_ref, seg_col, seg_row, dq_ref, dk_ref, dv_ref, dk_acc, dv_acc
):
    member = pl.program_id(1)

    @pl.when(member == 0)
    def _():
        dk_acc[...] = jnp.zeros_like(dk_acc)
        dv_acc[...] = jnp.zeros_like(dv_acc)

    keys_t = k_ref[0]
    keys = keys_t.astype(jnp.float32).T.astype(jnp.bfloat16)
    values = v_ref[0].astype(jnp.float32).T.astype(jnp.bfloat16)
    for qi in range(blocks):
        qs = slice(qi * BLOCK, (qi + 1) * BLOCK)
        q = q_ref[0, :, qs]
        g = g_ref[0, :, qs]
        g32 = g.astype(jnp.float32)
        delta = jnp.sum(g32 * o_ref[0, :, qs].astype(jnp.float32), axis=0, keepdims=True)
        lse = lse_ref[0, :, qs]
        q_rows = q.astype(jnp.float32).T.astype(jnp.bfloat16)
        g_rows = g32.T.astype(jnp.bfloat16)
        dq = jnp.zeros((HEAD_SIZE, BLOCK), jnp.float32)
        for ki in range(qi + 1):
            ks = slice(ki * BLOCK, (ki + 1) * BLOCK)
            s = dot(keys[ks, :], q, 1, 0)
            p = jnp.where(allowed_tile(seg_col, seg_row, qi, ki), jnp.exp(s - lse), 0.0)
            dp = dot(values[ks, :], g, 1, 0)
            ds = (p * (dp - delta)).astype(jnp.bfloat16)
            dv_acc[ks, :] += dot(p.astype(jnp.bfloat16), g_rows, 1, 0)
            dk_acc[ks, :] += dot(ds, q_rows, 1, 0)
            dq = dq + dot(keys_t[:, ks], ds, 1, 0)
        dq_ref[0, :, qs] = dq

    @pl.when(member == GROUP - 1)
    def _():
        dk_ref[0] = dk_acc[...].T
        dv_ref[0] = dv_acc[...].T


def attention_backward(q, k, v, o, g, lse, seg):
    heads, _, length = q.shape
    blocks = length // BLOCK
    full = pl.BlockSpec((1, HEAD_SIZE, length), lambda j, m: (j * GROUP + m, 0, 0))
    shared = pl.BlockSpec((1, HEAD_SIZE, length), lambda j, m: (j, 0, 0))
    return pl.pallas_call(
        functools.partial(attention_backward_kernel, blocks),
        grid=(heads // GROUP, GROUP),
        in_specs=[
            full,
            shared,
            shared,
            full,
            full,
            pl.BlockSpec((1, 1, length), lambda j, m: (j * GROUP + m, 0, 0)),
            pl.BlockSpec((length, 1), lambda j, m: (0, 0)),
            pl.BlockSpec((1, length), lambda j, m: (0, 0)),
        ],
        out_specs=[full, shared, shared],
        out_shape=[
            jax.ShapeDtypeStruct((heads, HEAD_SIZE, length), jnp.float32),
            jax.ShapeDtypeStruct((heads // GROUP, HEAD_SIZE, length), jnp.float32),
            jax.ShapeDtypeStruct((heads // GROUP, HEAD_SIZE, length), jnp.float32),
        ],
        scratch_shapes=[
            pltpu.VMEM((length, HEAD_SIZE), jnp.float32),
            pltpu.VMEM((length, HEAD_SIZE), jnp.float32),
        ],
        compiler_params=pltpu.CompilerParams(vmem_limit_bytes=48 * 1024 * 1024),
        cost_estimate=pl.CostEstimate(
            flops=10 * heads * length * length * HEAD_SIZE,
            bytes_accessed=16 * heads * length * HEAD_SIZE,
            transcendentals=heads * length * length // 2,
        ),
        name="attention_backward",
    )(q, k, v, o, g, lse, seg[:, None], seg[None, :])


def rope_tables(length):
    freqs = 10000.0 ** (-(jnp.arange(HALF, dtype=jnp.float32) * 2.0 / HEAD_SIZE))
    angles = freqs[:, None] * jnp.arange(length, dtype=jnp.float32)[None, :]
    return jnp.cos(angles)[None], jnp.sin(angles)[None]


def rotate(v, cosine, sine):
    a, b = v[:, :HALF, :], v[:, HALF:, :]
    return jnp.concatenate([a * cosine - b * sine, b * cosine + a * sine], axis=1)


def gather_expert(v):
    return lax.all_gather(v, "expert", axis=0, tiled=True)


def scatter_expert(v):
    return lax.psum_scatter(v, "expert", scatter_dimension=0, tiled=True)


def gather_shard(v):
    return lax.all_gather(v, "shard", axis=0, tiled=True)


def scatter_shard(v):
    return lax.psum_scatter(v, "shard", scatter_dimension=0, tiled=True)


def body(
    tokens,
    segment_ids,
    routes,
    gain_attn,
    w_query,
    key_weight,
    value_weight,
    w_out,
    gain_ffn,
    w_router,
    w_gate_up,
    w_down,
    cotangent,
):
    bf16, f32 = jnp.bfloat16, jnp.float32
    members = lax.axis_size("expert")
    shards = lax.axis_size("shard")
    me = lax.axis_index("expert")
    rows, width = tokens.shape[1:]
    length = rows * members
    shard_rows = w_query.shape[0]
    experts = EXP_DEV * members
    q_cols = QUERY_HEADS * HEAD_SIZE // members
    k_cols = KEY_VALUE_HEADS * HEAD_SIZE // members
    heads, kv_heads = q_cols // HEAD_SIZE, k_cols // HEAD_SIZE
    out_rows = width // (members * shards)

    def cols(w, n):
        return lax.dynamic_slice_in_dim(w, me * n, n, axis=1)

    first = jnp.concatenate(
        [cols(w_query, q_cols), cols(key_weight, k_cols), cols(value_weight, k_cols)], axis=1
    )
    small = jnp.concatenate([w_router, gain_attn[:, None], gain_ffn[:, None]], axis=1)
    full_small = gather_shard(small)
    full_qkv = gather_shard(first)
    full_router = full_small[:, :experts]
    gain_one = full_small[:, experts].astype(f32)
    gain_two = full_small[:, experts + 1].astype(f32)
    out_piece = cols(w_out, q_cols)
    full_out = jnp.concatenate(
        [
            lax.all_gather(gather_shard(out_piece), "expert", axis=0)[i]
            for i in range(members)
        ],
        axis=1,
    )
    pieces = [
        gather_shard(jnp.concatenate([w_gate_up[:, j, :], w_down[:, j, :]], axis=1))
        for j in range(EXP_DEV)
    ]

    all_tokens = gather_expert(tokens[0])
    meta = gather_expert(jnp.concatenate([segment_ids[0][:, None], routes[0]], axis=1))
    seg = meta[:, 0]
    route_ids = meta[:, 1:]
    all_grad = gather_expert(cotangent[0])

    inputs = all_tokens.astype(f32)
    normed_one = inputs * inverse_rms(inputs)
    xn_one = (normed_one * gain_one).astype(bf16)
    qkv = dot(full_qkv, xn_one, 0, 1).reshape(heads + 2 * kv_heads, HEAD_SIZE, length)
    cosine, sine = rope_tables(length)
    rotated = rotate(qkv[: heads + kv_heads], cosine, sine).astype(bf16)
    queries = rotated[:heads] * jnp.asarray(HEAD_SIZE**-0.5, bf16)
    keys = rotated[heads:]
    values = qkv[heads + kv_heads :].astype(bf16)
    attended, lse = attention_forward(queries, keys, values, seg)
    attended_rows = attended.reshape(q_cols, length)
    attended_all = gather_expert(attended_rows)

    hidden = inputs + dot(attended_all, full_out, 0, 0)
    normed_two = hidden * inverse_rms(hidden)
    xn_two = (normed_two * gain_two).astype(bf16)

    logits = jnp.dot(xn_two, full_router, preferred_element_type=f32)
    named = jnp.any(
        route_ids[:, :, None] == jnp.arange(experts, dtype=jnp.int32)[None, None, :], axis=1
    )
    peak = jnp.max(jnp.where(named, logits, -jnp.inf), axis=1, keepdims=True)
    exps = jnp.where(named, jnp.exp(jnp.minimum(logits - peak, 0.0)), 0.0)
    gates = exps / jnp.sum(exps, axis=1, keepdims=True)
    my_gates = lax.dynamic_slice_in_dim(gates, me * EXP_DEV, EXP_DEV, axis=1)

    xn_t, grad_t = xn_two.T, all_grad.T
    mix = jnp.zeros((length, width), f32)
    grad_in = jnp.zeros((length, width), f32)
    gate_grads, expert_grads = [], []
    for j in range(EXP_DEV):
        w_in, w_back = pieces[j][:, : 2 * FF], pieces[j][:, 2 * FF :]
        gate_up = dot(xn_two, w_in, 1, 0)
        through = dot(all_grad, w_back, 1, 0)
        gate, up = gate_up[:, :FF], gate_up[:, FF:]
        weight = my_gates[:, j : j + 1]
        sig = jax.nn.sigmoid(gate)
        act = gate * sig * up
        gate_grads.append(jnp.sum(act * through, axis=1, keepdims=True))
        scaled = (weight * act).astype(bf16)
        grad_act = weight * through
        back = jnp.concatenate(
            [grad_act * up * sig * (1.0 + gate * (1.0 - sig)), grad_act * gate * sig], axis=1
        ).astype(bf16)
        mix = mix + dot(scaled, w_back, 1, 1)
        grad_in = grad_in + dot(back, w_in, 1, 1)
        grads = jnp.concatenate([dot(xn_t, back, 1, 0), dot(grad_t, scaled, 1, 0)], axis=1)
        expert_grads.append(scatter_shard(grads.astype(bf16)))

    def mine(v):
        return lax.dynamic_slice_in_dim(v, me * rows, rows, axis=0)

    grad_gates = gather_expert(jnp.concatenate(gate_grads, axis=1).T).T
    grad_chosen = gates * (grad_gates - jnp.sum(gates * grad_gates, axis=1, keepdims=True))
    grad_logits = grad_chosen.astype(bf16)
    grad_xn_two = scatter_expert(grad_in.astype(bf16)).astype(f32)
    grad_xn_two = grad_xn_two + dot(mine(grad_logits), full_router, 1, 1)
    my_hidden = mine(hidden)
    mixed = (my_hidden + scatter_expert(mix.astype(bf16)).astype(f32)).astype(bf16)

    my_scale = inverse_rms(my_hidden)
    my_normed = my_hidden * my_scale
    grad_gain_two = jnp.sum(grad_xn_two * my_normed, axis=0)
    g = grad_xn_two * gain_two
    grad_hidden = cotangent[0].astype(f32) + my_scale * (
        g - my_normed * jnp.mean(g * my_normed, axis=-1, keepdims=True)
    )
    grad_attn = gather_expert(grad_hidden.astype(bf16))
    out_mine = lax.dynamic_slice_in_dim(full_out, me * q_cols, q_cols, axis=0)
    grad_attended = dot(out_mine, grad_attn, 1, 1).astype(bf16).reshape(heads, HEAD_SIZE, length)
    grad_out = jnp.dot(attended_rows, grad_attn, preferred_element_type=f32)
    grad_router = dot(cols(xn_two, q_cols), grad_logits, 0, 0)
    out_grads = scatter_shard(
        jnp.concatenate([grad_out, grad_router], axis=1).astype(bf16)
    ).astype(f32)

    dq, dk, dv = attention_backward(queries, keys, values, attended, grad_attended, lse, seg)
    dq = rotate(dq, cosine, -sine) * HEAD_SIZE**-0.5
    dk = rotate(dk, cosine, -sine)
    grad_qkv = jnp.concatenate([dq, dk, dv], axis=0).astype(bf16).reshape(-1, length)
    grad_first = dot(xn_one, grad_qkv, 0, 1)
    grad_xn_one = dot(grad_qkv, full_qkv, 0, 1)
    grad_xn_one = scatter_expert(grad_xn_one.astype(bf16)).astype(f32)
    my_inputs = tokens[0].astype(f32)
    scale_one = inverse_rms(my_inputs)
    normed = my_inputs * scale_one
    grad_gain_one = jnp.sum(grad_xn_one * normed, axis=0)
    h = grad_xn_one * gain_one
    grad_tokens = grad_hidden + scale_one * (h - normed * jnp.mean(h * normed, axis=-1, keepdims=True))

    total_cols = q_cols + 2 * k_cols
    grad_first = jnp.transpose(
        grad_first.astype(bf16).reshape(members, shards, out_rows, total_cols), (1, 0, 2, 3)
    ).reshape(width, total_cols)
    grad_first = scatter_shard(grad_first).reshape(members, out_rows, total_cols)
    grad_first = lax.all_to_all(grad_first, "expert", split_axis=0, concat_axis=0, tiled=True)
    grad_first = jnp.transpose(grad_first, (1, 0, 2)).astype(f32)
    gains = lax.psum_scatter(
        jnp.stack([grad_gain_one, grad_gain_two], axis=1),
        ("expert", "shard"),
        scatter_dimension=0,
        tiled=True,
    )
    expert_grads = jnp.stack(expert_grads, axis=1).astype(f32)
    return (
        mixed[None],
        grad_tokens.astype(bf16)[None],
        gains[:, 0],
        grad_first[:, :, :q_cols].reshape(out_rows, -1),
        grad_first[:, :, q_cols : q_cols + k_cols].reshape(out_rows, -1),
        grad_first[:, :, q_cols + k_cols :].reshape(out_rows, -1),
        out_grads[:, :width],
        gains[:, 1],
        out_grads[:, width:],
        expert_grads[:, :, : 2 * FF],
        expert_grads[:, :, 2 * FF :],
    )


def solution(mesh):
    in_specs = (
        P("shard", "expert", None),
        P("shard", "expert"),
        P("shard", "expert", None),
        P("shard"),
        P("shard", None),
        P("shard", None),
        P("shard", None),
        P("shard", None),
        P("shard"),
        P("shard", None),
        P("shard", "expert", None),
        P("shard", "expert", None),
        P("shard", "expert", None),
    )
    out_specs = (
        P("shard", "expert", None),
        P("shard", "expert", None),
        P(("expert", "shard")),
        P(("expert", "shard"), None),
        P(("expert", "shard"), None),
        P(("expert", "shard"), None),
        P(("expert", "shard"), None),
        P(("expert", "shard")),
        P(("expert", "shard"), None),
        P("shard", "expert", None),
        P("shard", "expert", None),
    )
    return jax.shard_map(body, mesh=mesh, in_specs=in_specs, out_specs=out_specs, check_vma=False)
```

time: 2150 us -> 1620 us (0.75)
  local copies, waits for them, and re-layouts: 330 us -> 110 us
  waiting for transfers between devices: 1320 us -> 1140 us
  matrix products: 283 us -> 208 us
  other arithmetic: 104 us -> 50.1 us
  Pallas kernels: 0 us -> 34.7 us
  starting transfers between devices: 29.8 us -> 4.94 us
    all_to_all x4 -> x1, waiting for transfers between devices: 620 us -> 0.01 us  [body(): lax.all_to_all(grad_first, 'expert', split_axis=0, concat_axis=0, tiled=T...]
    all_gather x8 -> x12, waiting for transfers between devices: 150 us -> 484 us  [the longest x7 434 us: gather_shard(): return lax.all_gather(v, 'shard', axis=0, tiled=True)]
    dot_general x75 -> x39, matrix products: 283 us -> 208 us  [the longest x37 203 us: dot(): lax.dot_general(a, b, (((ca,), (cb,)), ((), ())), preferred_element_type=...]
    convert_element_type x3 -> x0, local copies, waits for them, and re-layouts: 68.2 us -> none  [the longest x1 34 us: body(): grad_input_rows.astype(jnp.bfloat16)]
    reshape x2 -> x4, local copies, waits for them, and re-layouts: 68.1 us -> 3.51 us  [the longest x1 1.47 us: body(): grad_first.astype(bf16).reshape(members, shards, out_rows, total_cols)]
    unnamed x13 -> x29, waiting for transfers between devices: 382 us -> 443 us
    reduce_scatter x3 -> x5, waiting for transfers between devices: 170 us -> 216 us  [the longest x3 108 us: scatter_expert(): return lax.psum_scatter(v, 'expert', scatter_dimension=0, tiled=True)]
    gather x2 -> x0, local copies, waits for them, and re-layouts: 38.4 us -> none  [pick(): buffer.reshape(buffer_rows, model_width)[slot_index]]
  transfers between devices with their start and end apart: 16 -> 24, of which waited for: 13 -> 20; matrix products, arithmetic and copies ran while one was open for 21% -> 17% of each run, Pallas kernels for 0% -> 2%
where the time goes in v1:
time: 1620 us; the launch traced here: 1610 us
  waiting for transfers between devices  1140 us (70%)
  matrix products  208 us (13%)
  local copies, waits for them, and re-layouts  110 us (7%)
  other arithmetic  50.1 us (3%)
  blocking collectives  43.1 us (3%)
  Pallas kernels  34.7 us (2%)
    unnamed x29, waiting for transfers between devices  443 us
    all_gather x7, waiting for transfers between devices, gather_shard(): return lax.all_gather(v, 'shard', axis=0, tiled=True)  434 us
    dot_general x37, matrix products, dot(): lax.dot_general(a, b, (((ca,), (cb,)), ((), ())), preferred_element_type=...  203 us
    reduce_scatter x3, waiting for transfers between devices, scatter_expert(): return lax.psum_scatter(v, 'expert', scatter_dimension=0, tiled=True)  108 us
    reduce_scatter x2, waiting for transfers between devices, scatter_shard(): return lax.psum_scatter(v, 'shard', scatter_dimension=0, tiled=True)  107 us
    unnamed x224, local copies, waits for them, and re-layouts  83.7 us
    all_gather x4, waiting for transfers between devices, gather_expert(): return lax.all_gather(v, 'expert', axis=0, tiled=True)  46.1 us
  transfers between devices with their start and end apart: 24, of which 20 were waited for; matrix products, arithmetic and copies ran while one was open for 17% of the time, Pallas kernels for 2%

profile of v1, /device:TPU:0, one launch (start us, length us, event | category | flops | bytes accessed | tf_op | source)
XLA Modules:
  0.0 1608.8 jit_solution(9450134947506000504)
XLA Ops:
  12.3 42.3 %all-gather.22.cloned.1.call-done = bf16[1536,384]{1,0:T(8,128)(2,1)} async-done(((bf16[192,384]{1,0:T(8,128)(2,1)}), bf16[1536,384]{1,0:T(8,128)(2,1)}) %all-gather.22.cloned.1.call-update) | async-done | bytes 1179664 | tf_op jit(solution)/shard_map/all_gather | solution.py:197
  54.8 30.6 %all-gather.3 = bf16[8,192,22]{1,2,0:T(8,128)(2,1)S(1)} all-gather(bf16[1,192,22]{1,2,0:T(8,128)(2,1)S(1)} %maximum_bitcast_fusion), channel_id=1, replica_groups=mesh['expert'=4,'shard'=8] {'shard'}, dimensions={0}, use_global_device_ids=true | all-gather | bytes 76032 | tf_op jit(solution)/shard_map/all_gather | solution.py:197
  85.6 7.1 all_gather.60
  97.1 36.7 %all-gather.18.cloned.1.call-done = bf16[1536,640]{1,0:T(8,128)(2,1)} async-done(((bf16[192,640]{1,0:T(8,128)(2,1)}), bf16[1536,640]{1,0:T(8,128)(2,1)}) %all-gather.18.cloned.1.call-update) | async-done | bytes 1966096 | tf_op jit(solution)/shard_map/all_gather | solution.py:197
  139.5 17.8 %attention_forward.1 = (bf16[6,64,1024]{2,1,0:T(8,128)(2,1)}, f32[6,1,1024]{2,1,0:T(1,128)S(1)}) custom-call(bf16[6,64,1024]{2,1,0:T(8,128)(2,1)S(1)} %fusion.107.q_ref, bf16[2,64,1024]{2,1,0:T(8,128)(2,1)S(1)} %pad_maximum_fusion.28.k_ref, bf16[2,64,1024]{2,1,0:T(8,128)(2,1)S(1)} %bitcast.242, s32[1024,1]{1,0:T(8,128)S(1)} %get-tuple-element.138.seg_col, ...), custom_call_target="tpu_custom_call" | custom-call | flops 1610612736 | bytes 2359296 | tf_op jit(solution)/shard_map/attention_forward/pallas_call | solution.py:74
  176.0 26.4 %all-gather.20.cloned.1.call-done = bf16[1536,1024]{1,0:T(8,128)(2,1)} async-done(((bf16[384,1024]{1,0:T(8,128)(2,1)}), bf16[1536,1024]{1,0:T(8,128)(2,1)}) %all-gather.20.cloned.1.call-update) | async-done | bytes 3145744 | tf_op jit(solution)/shard_map/all_gather | solution.py:189
  202.4 9.0 multiply_reduce_fusion
  216.6 67.7 %all-gather.32.cloned.1.call-done = bf16[1536,1536]{1,0:T(8,128)(2,1)} async-done(((bf16[192,1536]{1,0:T(8,128)(2,1)}), bf16[1536,1536]{1,0:T(8,128)(2,1)}) %all-gather.32.cloned.1.call-update) | async-done | bytes 4718608 | tf_op jit(solution)/shard_map/all_gather | solution.py:197
  284.4 8.3 fusion.39
  292.7 71.9 %all-gather.30.cloned.1.call-done = bf16[1536,1536]{1,0:T(8,128)(2,1)} async-done(((bf16[192,1536]{1,0:T(8,128)(2,1)}), bf16[1536,1536]{1,0:T(8,128)(2,1)}) %all-gather.30.cloned.1.call-update) | async-done | bytes 4718608 | tf_op jit(solution)/shard_map/all_gather | solution.py:197
  364.6 8.7 fusion.43
  373.3 71.5 %all-gather.28.cloned.1.call-done = bf16[1536,1536]{1,0:T(8,128)(2,1)} async-done(((bf16[192,1536]{1,0:T(8,128)(2,1)}), bf16[1536,1536]{1,0:T(8,128)(2,1)}) %all-gather.28.cloned.1.call-update) | async-done | bytes 4718608 | tf_op jit(solution)/shard_map/all_gather | solution.py:197
  444.8 8.4 fusion.47
  453.2 71.8 %all-gather.26.cloned.1.call-done = bf16[1536,1536]{1,0:T(8,128)(2,1)} async-done(((bf16[192,1536]{1,0:T(8,128)(2,1)}), bf16[1536,1536]{1,0:T(8,128)(2,1)}) %all-gather.26.cloned.1.call-update) | async-done | bytes 4718608 | tf_op jit(solution)/shard_map/all_gather | solution.py:197
  525.1 8.3 fusion.51
  533.4 71.8 %all-gather.24.cloned.1.call-done = bf16[1536,1536]{1,0:T(8,128)(2,1)} async-done(((bf16[192,1536]{1,0:T(8,128)(2,1)}), bf16[1536,1536]{1,0:T(8,128)(2,1)}) %all-gather.24.cloned.1.call-update) | async-done | bytes 4718608 | tf_op jit(solution)/shard_map/all_gather | solution.py:197
  605.2 8.6 fusion.55
  613.8 19.6 %all-gather.40.cloned.1.call-done = bf16[1,1024,1536]{2,1,0:T(8,128)(2,1)} async-done(((bf16[1,256,1536]{2,1,0:T(8,128)(2,1)}), bf16[1,1024,1536]{2,1,0:T(8,128)(2,1)}) %all-gather.40.cloned.1.call-update) | async-done | bytes 3145744 | tf_op jit(solution)/shard_map/all_gather | solution.py:189
  633.5 7.8 fusion.76
  702.3 12.4 add_convert_fusion
  716.4 36.4 %reduce-scatter.26.cloned.1.call-done = bf16[256,1536]{1,0:T(8,128)(2,1)} async-done(((bf16[1024,1536]{1,0:T(8,128)(2,1)}), bf16[256,1536]{1,0:T(8,128)(2,1)}) %reduce-scatter.26.cloned.1.call-update) | async-done | bytes 786448 | tf_op jit(solution)/shard_map/reduce_scatter | solution.py:193
  864.6 16.9 %attention_backward.1 = (f32[6,64,1024]{2,1,0:T(8,128)S(1)}, f32[2,64,1024]{2,1,0:T(8,128)S(1)}, f32[2,64,1024]{2,1,0:T(8,128)S(1)}) custom-call(bf16[6,64,1024]{2,1,0:T(8,128)(2,1)S(1)} %copy-done.3, bf16[2,64,1024]{2,1,0:T(8,128)(2,1)S(1)} %copy-done.7, bf16[2,64,1024]{2,1,0:T(8,128)(2,1)S(1)} %bitcast.243, bf16[6,64,1024]{2,1,0:T(8,128)(2,1)} %get-tuple-element.16.o_ref, ...), custom_call_target="tpu_custom_call" | custom-call | flops 4026531840 | bytes 6291456 | tf_op jit(solution)/shard_map/attention_backward/pallas_call | solution.py:144
  920.7 9.8 add_convert_fusion.1
  933.3 53.1 %reduce-scatter.40.cloned.1.call-done = bf16[192,1536]{1,0:T(8,128)(2,1)} async-done(((bf16[1536,1536]{1,0:T(8,128)(2,1)}), bf16[192,1536]{1,0:T(8,128)(2,1)}) %reduce-scatter.40.cloned.1.call-update) | async-done | bytes 589840
  987.7 97.8 %reduce-scatter.38.cloned.1.call-done = bf16[192,1536]{1,0:T(8,128)(2,1)} async-done(((bf16[1536,1536]{1,0:T(8,128)(2,1)}), bf16[192,1536]{1,0:T(8,128)(2,1)}) %reduce-scatter.38.cloned.1.call-update) | async-done | bytes 589840
  1087.7 96.9 %reduce-scatter.42.cloned.1.call-done = bf16[192,1536]{1,0:T(8,128)(2,1)} async-done(((bf16[1536,1536]{1,0:T(8,128)(2,1)}), bf16[192,1536]{1,0:T(8,128)(2,1)}) %reduce-scatter.42.cloned.1.call-update) | async-done | bytes 589840
  1186.9 96.9 %reduce-scatter.36.cloned.1.call-done = bf16[192,1536]{1,0:T(8,128)(2,1)} async-done(((bf16[1536,1536]{1,0:T(8,128)(2,1)}), bf16[192,1536]{1,0:T(8,128)(2,1)}) %reduce-scatter.36.cloned.1.call-update) | async-done | bytes 589840
  1290.9 63.7 %reduce-scatter.30.cloned.1.call-done = bf16[192,640]{1,0:T(8,128)(2,1)} async-done(((bf16[1536,640]{1,0:T(8,128)(2,1)}), bf16[192,640]{1,0:T(8,128)(2,1)}) %reduce-scatter.30.cloned.1.call-update) | async-done | bytes 245776 | tf_op jit(solution)/shard_map/reduce_scatter | solution.py:201
  1375.5 43.8 %reduce-scatter.32.cloned.1.call-done = bf16[48,1556]{1,0:T(8,128)(2,1)} async-done(((bf16[384,1556]{1,0:T(8,128)(2,1)}), bf16[48,1556]{1,0:T(8,128)(2,1)}) %reduce-scatter.32.cloned.1.call-update) | async-done | bytes 149392 | tf_op jit(solution)/shard_map/reduce_scatter | solution.py:201
  1424.4 34.2 %reduce-scatter.28.cloned.1.call-done = bf16[256,1536]{1,0:T(8,128)(2,1)} async-done(((bf16[1024,1536]{1,0:T(8,128)(2,1)}), bf16[256,1536]{1,0:T(8,128)(2,1)}) %reduce-scatter.28.cloned.1.call-update) | async-done | bytes 786448 | tf_op jit(solution)/shard_map/reduce_scatter | solution.py:193
  1461.7 37.6 %reduce-scatter.24.cloned.1.call-done = bf16[256,1536]{1,0:T(8,128)(2,1)} async-done(((bf16[1024,1536]{1,0:T(8,128)(2,1)}), bf16[256,1536]{1,0:T(8,128)(2,1)}) %reduce-scatter.24.cloned.1.call-update) | async-done | bytes 786448 | tf_op jit(solution)/shard_map/reduce_scatter | solution.py:193
  1503.4 96.6 %reduce-scatter.34.cloned.1.call-done = f32[48,2]{1,0:T(8,128)} async-done(((f32[1536,2]{1,0:T(8,128)}), f32[48,2]{1,0:T(8,128)}) %reduce-scatter.34.cloned.1.call-update) | async-done | bytes 400
  (395 shorter events, 302.5 us)
Async XLA Ops:
  7.2 47.5 %copy-start.82 = (bf16[192]{0:T(256)(128)(2,1)S(1)}, bf16[192]{0:T(256)(128)(2,1)}, u32[]{:S(2)}) copy-start(bf16[192]{0:T(256)(128)(2,1)} %param.16) | copy-start | bytes 1156
  7.2 47.5 %copy-start.83 = (bf16[192]{0:T(256)(128)(2,1)S(1)}, bf16[192]{0:T(256)(128)(2,1)}, u32[]{:S(2)}) copy-start(bf16[192]{0:T(256)(128)(2,1)} %param.21) | copy-start | bytes 1156
  7.2 47.5 %copy-start.76 = (bf16[192,20]{0,1:T(8,128)(2,1)S(1)}, bf16[192,20]{0,1:T(8,128)(2,1)}, u32[]{:S(2)}) copy-start(bf16[192,20]{0,1:T(8,128)(2,1)} %param.22) | copy-start | bytes 23044
  7.2 78.3 %copy-start.77 = (s32[1,256,8]{1,2,0:T(8,128)S(1)}, s32[1,256,8]{1,2,0:T(8,128)}, u32[]{:S(2)}) copy-start(s32[1,256,8]{1,2,0:T(8,128)} %param.15) | copy-start | bytes 24580
  7.2 78.3 %copy-start.80 = (s32[1,256]{1,0:T(1,128)S(1)}, s32[1,256]{1,0:T(1,128)}, u32[]{:S(2)}) copy-start(s32[1,256]{1,0:T(1,128)} %param.14) | copy-start | bytes 3076
  7.2 47.4 %all-gather.22.cloned.1.call-start = ((), (), s32[]{:S(2)}) async-start(), calls=%async_computation.14 | async-start | bytes 1327104 | tf_op jit(solution)/shard_map/all_gather | solution.py:197
  9.0 85.4 %all-gather.36.cloned.1.call-start = ((), (), s32[]{:S(2)}) async-start(), calls=%async_computation.26 | async-start | bytes 3932160 | tf_op jit(solution)/shard_map/all_gather | solution.py:189
  9.7 124.1 %all-gather.18.cloned.1.call-start = ((), (), s32[]{:S(2)}) async-start(), calls=%async_computation.12 | async-start | bytes 2211840 | tf_op jit(solution)/shard_map/all_gather | solution.py:197
  12.3 159.6 %all-gather.38.cloned.1.call-start = ((), (), s32[]{:S(2)}) async-start(), calls=%async_computation.27 | async-start | bytes 5898240 | tf_op jit(solution)/shard_map/all_gather | solution.py:247
  54.7 147.8 %all-gather.20.cloned.1.call-start = ((), (), s32[]{:S(2)}) async-start(), calls=%async_computation.13 | async-start | bytes 3932160 | tf_op jit(solution)/shard_map/all_gather | solution.py:189
  94.3 45.2 %copy-start.4 = (s32[1024,1]{1,0:T(8,128)}, s32[1024,1]{1,0:T(8,128)S(1)}, u32[]{:S(2)}) copy-start(s32[1024,1]{1,0:T(8,128)S(1)} %get-tuple-element.138.seg_col) | copy-start | bytes 12292
  157.4 127.0 %all-gather.32.cloned.1.call-start = ((), (), s32[]{:S(2)}) async-start(), calls=%async_computation.19 | async-start | bytes 5308416 | tf_op jit(solution)/shard_map/all_gather | solution.py:197
  161.7 202.9 %all-gather.30.cloned.1.call-start = ((), (), s32[]{:S(2)}) async-start(), calls=%async_computation.18 | async-start | bytes 5308416 | tf_op jit(solution)/shard_map/all_gather | solution.py:197
  163.8 281.1 %all-gather.28.cloned.1.call-start = ((), (), s32[]{:S(2)}) async-start(), calls=%async_computation.17 | async-start | bytes 5308416 | tf_op jit(solution)/shard_map/all_gather | solution.py:197
  164.7 360.3 %all-gather.26.cloned.1.call-start = ((), (), s32[]{:S(2)}) async-start(), calls=%async_computation.16 | async-start | bytes 5308416 | tf_op jit(solution)/shard_map/all_gather | solution.py:197
  165.7 439.5 %all-gather.24.cloned.1.call-start = ((), (), s32[]{:S(2)}) async-start(), calls=%async_computation.15 | async-start | bytes 5308416 | tf_op jit(solution)/shard_map/all_gather | solution.py:197
  166.6 466.8 %all-gather.40.cloned.1.call-start = ((), (), s32[]{:S(2)}) async-start(), calls=%async_computation.28 | async-start | bytes 3932160 | tf_op jit(solution)/shard_map/all_gather | solution.py:189
  167.4 585.5 %reduce-scatter.26.cloned.1.call-start = ((), (), s32[]{:S(2)}) async-start(), calls=%async_computation.21 | async-start | bytes 3932160 | tf_op jit(solution)/shard_map/reduce_scatter | solution.py:193
  714.7 146.0 %all-gather.34.cloned.1.call-start = ((), (), s32[]{:S(2)}) async-start(), calls=%async_computation.22 | async-start | bytes 3932160 | tf_op jit(solution)/shard_map/all_gather | solution.py:189
  759.1 172.8 %reduce-scatter.44.cloned.1.call-start = ((), (), s32[]{:S(2)}) async-start(), calls=%async_computation.34 | async-start | bytes 5308416
  777.6 208.8 %reduce-scatter.40.cloned.1.call-start = ((), (), s32[]{:S(2)}) async-start(), calls=%async_computation.32 | async-start | bytes 5308416
  796.7 288.8 %reduce-scatter.38.cloned.1.call-start = ((), (), s32[]{:S(2)}) async-start(), calls=%async_computation.31 | async-start | bytes 5308416
  816.1 368.5 %reduce-scatter.42.cloned.1.call-start = ((), (), s32[]{:S(2)}) async-start(), calls=%async_computation.33 | async-start | bytes 5308416
  835.7 448.1 %reduce-scatter.36.cloned.1.call-start = ((), (), s32[]{:S(2)}) async-start(), calls=%async_computation.30 | async-start | bytes 5308416
  854.8 499.8 %reduce-scatter.30.cloned.1.call-start = ((), (), s32[]{:S(2)}) async-start(), calls=%async_computation.24 | async-start | bytes 2211840 | tf_op jit(solution)/shard_map/reduce_scatter | solution.py:201
  888.3 530.9 %reduce-scatter.32.cloned.1.call-start = ((), (), s32[]{:S(2)}) async-start(), calls=%async_computation.25 | async-start | bytes 1437696 | tf_op jit(solution)/shard_map/reduce_scatter | solution.py:201
  894.5 564.1 %reduce-scatter.28.cloned.1.call-start = ((), (), s32[]{:S(2)}) async-start(), calls=%async_computation.23 | async-start | bytes 3932160 | tf_op jit(solution)/shard_map/reduce_scatter | solution.py:193
  900.3 599.1 %reduce-scatter.24.cloned.1.call-start = ((), (), s32[]{:S(2)}) async-start(), calls=%async_computation.20 | async-start | bytes 3932160 | tf_op jit(solution)/shard_map/reduce_scatter | solution.py:193
  1354.6 67.7 %all-to-all-start = ((bf16[4,48,640]{2,1,0:T(8,128)(2,1)}), bf16[4,48,640]{2,1,0:T(8,128)(2,1)S(1)}, u32[]{:S(2)}, u32[]{:S(2)}) async-start(bf16[4,48,640]{2,1,0:T(8,128)(2,1)} %bitcast.269), calls=%async_computation.4 | async-start | bytes 491520 | tf_op jit(solution)/shard_map/all_to_all | solution.py:358
  1358.0 241.9 %reduce-scatter.34.cloned.1.call-start = ((), (), s32[]{:S(2)}) async-start(), calls=%async_computation.29 | async-start | bytes 811008
  1423.1 76.2 %copy-start.20 = (f32[256,1536]{1,0:T(8,128)S(1)}, f32[256,1536]{1,0:T(8,128)}, u32[]{:S(2)}) copy-start(f32[256,1536]{1,0:T(8,128)} %copy-done.19) | copy-start | bytes 4718596
  1461.7 140.4 %copy-start.1 = (bf16[192,1536]{1,0:T(8,128)(2,1)S(1)}, bf16[192,1536]{1,0:T(8,128)(2,1)}, u32[]{:S(2)}) copy-start(bf16[192,1536]{1,0:T(8,128)(2,1)} %param.20) | copy-start | bytes 1769476
  (92 other events, 779.0 us)
Sparse Core Ops, SparseCore 0:
  10.8 43.7 all-gather.21
  56.2 27.2 all-gather.35
  86.3 47.5 all-gather.17
  135.3 36.5 all-gather.37
  173.8 28.5 all-gather.19
  204.4 79.8 all-gather.31
  286.6 78.0 all-gather.29
  366.8 78.0 all-gather.27
  447.0 78.0 all-gather.25
  527.1 78.0 all-gather.23
  606.7 26.6 all-gather.39
  714.8 37.9 reduce-scatter.25
  759.3 28.5 all-gather.33
  791.8 95.4 reduce-scatter.43
  891.2 95.1 reduce-scatter.39
  990.3 95.1 reduce-scatter.37
  1089.5 95.1 reduce-scatter.41
  1188.6 95.1 reduce-scatter.35
  1288.2 66.3 reduce-scatter.29
  1357.9 61.2 reduce-scatter.31
  1421.8 36.8 reduce-scatter.27
  1461.3 37.9 reduce-scatter.23
  1504.4 95.5 reduce-scatter.33

commit v2 on v1

v2 whole, which is shorter than its diff:
```python
import functools

import jax
import jax.numpy as jnp
from jax import lax
from jax.experimental import pallas as pl
from jax.experimental.pallas import tpu as pltpu
from jax.sharding import PartitionSpec as P

QUERY_HEADS = 24
KEY_VALUE_HEADS = 8
GROUP = QUERY_HEADS // KEY_VALUE_HEADS
HEAD_SIZE = 64
HALF = HEAD_SIZE // 2
FF = 512
TOP = 8
EXP_DEV = 5
BLOCK = 256
CHUNKS = ((0, 1), (2, 3), (4,))
MASKED = -1e30
epsilon = 1e-06


def dot(a, b, ca, cb):
    return lax.dot_general(a, b, (((ca,), (cb,)), ((), ())), preferred_element_type=jnp.float32)


def inverse_rms(v):
    return lax.rsqrt(jnp.mean(v * v, axis=-1, keepdims=True) + epsilon)


def place_of(block, mine, members):
    r = block ^ mine
    return (r & 1) * (members // 2) + (r >> 1)


def spans(me_ref, blocks):
    return [pl.multiple_of(place_of(a, me_ref[0], blocks) * BLOCK, BLOCK) for a in range(blocks)]


def allowed_tile(seg_col, seg_row, at, qi, ki):
    ok = seg_col[pl.ds(at[ki], BLOCK), :] == seg_row[:, pl.ds(at[qi], BLOCK)]
    if qi == ki:
        kpos = lax.broadcasted_iota(jnp.int32, (BLOCK, BLOCK), 0)
        qpos = lax.broadcasted_iota(jnp.int32, (BLOCK, BLOCK), 1)
        ok = ok & (kpos <= qpos)
    return ok


def attention_forward_kernel(blocks, me_ref, q_ref, k_ref, v_ref, seg_col, seg_row, o_ref, lse_ref, keys):
    at = spans(me_ref, blocks)
    keys[...] = k_ref[0].astype(jnp.float32).T.astype(jnp.bfloat16)
    for qi in range(blocks):
        qs = pl.ds(at[qi], BLOCK)
        q = q_ref[0, :, qs]
        top = total = acc = None
        for ki in range(qi, -1, -1):
            ks = pl.ds(at[ki], BLOCK)
            s = dot(keys[ks, :], q, 1, 0)
            s = jnp.where(allowed_tile(seg_col, seg_row, at, qi, ki), s, MASKED)
            peak = jnp.max(s, axis=0, keepdims=True)
            if top is None:
                top = peak
                e = jnp.exp(s - top)
                total = jnp.sum(e, axis=0, keepdims=True)
                acc = dot(v_ref[0, :, ks], e.astype(jnp.bfloat16), 1, 0)
            else:
                new = jnp.maximum(top, peak)
                scale = jnp.exp(top - new)
                e = jnp.exp(s - new)
                total = total * scale + jnp.sum(e, axis=0, keepdims=True)
                acc = acc * scale + dot(v_ref[0, :, ks], e.astype(jnp.bfloat16), 1, 0)
                top = new
        o_ref[0, :, qs] = (acc / total).astype(jnp.bfloat16)
        lse_ref[0, :, qs] = top + jnp.log(total)


def attention_forward(me, q, k, v, seg):
    heads, _, length = q.shape
    blocks = length // BLOCK
    full = pl.BlockSpec((1, HEAD_SIZE, length), lambda h, me: (h, 0, 0))
    shared = pl.BlockSpec((1, HEAD_SIZE, length), lambda h, me: (h // GROUP, 0, 0))
    return pl.pallas_call(
        functools.partial(attention_forward_kernel, blocks),
        grid_spec=pltpu.PrefetchScalarGridSpec(
            num_scalar_prefetch=1,
            grid=(heads,),
            in_specs=[
                full,
                shared,
                shared,
                pl.BlockSpec((length, 1), lambda h, me: (0, 0)),
                pl.BlockSpec((1, length), lambda h, me: (0, 0)),
            ],
            out_specs=[full, pl.BlockSpec((1, 1, length), lambda h, me: (h, 0, 0))],
            scratch_shapes=[pltpu.VMEM((length, HEAD_SIZE), jnp.bfloat16)],
        ),
        out_shape=[
            jax.ShapeDtypeStruct((heads, HEAD_SIZE, length), jnp.bfloat16),
            jax.ShapeDtypeStruct((heads, 1, length), jnp.float32),
        ],
        compiler_params=pltpu.CompilerParams(vmem_limit_bytes=48 * 1024 * 1024),
        cost_estimate=pl.CostEstimate(
            flops=4 * heads * length * length * HEAD_SIZE,
            bytes_accessed=6 * heads * length * HEAD_SIZE,
            transcendentals=heads * length * length // 2,
        ),
        name="attention_forward",
    )(me, q, k, v, seg[:, None], seg[None, :])


def attention_backward_kernel(
    blocks, me_ref, q_ref, k_ref, v_ref, o_ref, g_ref, lse_ref, seg_col, seg_row,
    dq_ref, dk_ref, dv_ref, keys, values, dk_acc, dv_acc,
):
    at = spans(me_ref, blocks)
    member = pl.program_id(1)

    @pl.when(member == 0)
    def _():
        dk_acc[...] = jnp.zeros_like(dk_acc)
        dv_acc[...] = jnp.zeros_like(dv_acc)
        keys[...] = k_ref[0].astype(jnp.float32).T.astype(jnp.bfloat16)
        values[...] = v_ref[0].astype(jnp.float32).T.astype(jnp.bfloat16)

    for qi in range(blocks):
        qs = pl.ds(at[qi], BLOCK)
        q = q_ref[0, :, qs]
        g = g_ref[0, :, qs]
        g32 = g.astype(jnp.float32)
        delta = jnp.sum(g32 * o_ref[0, :, qs].astype(jnp.float32), axis=0, keepdims=True)
        lse = lse_ref[0, :, qs]
        q_rows = q.astype(jnp.float32).T.astype(jnp.bfloat16)
        g_rows = g32.T.astype(jnp.bfloat16)
        dq = jnp.zeros((HEAD_SIZE, BLOCK), jnp.float32)
        for ki in range(qi + 1):
            ks = pl.ds(at[ki], BLOCK)
            s = dot(keys[ks, :], q, 1, 0)
            p = jnp.where(allowed_tile(seg_col, seg_row, at, qi, ki), jnp.exp(s - lse), 0.0)
            dp = dot(values[ks, :], g, 1, 0)
            ds = (p * (dp - delta)).astype(jnp.bfloat16)
            dv_acc[ks, :] += dot(p.astype(jnp.bfloat16), g_rows, 1, 0)
            dk_acc[ks, :] += dot(ds, q_rows, 1, 0)
            dq = dq + dot(k_ref[0, :, ks], ds, 1, 0)
        dq_ref[0, :, qs] = dq

    @pl.when(member == GROUP - 1)
    def _():
        dk_ref[0] = dk_acc[...].T
        dv_ref[0] = dv_acc[...].T


def attention_backward(me, q, k, v, o, g, lse, seg):
    heads, _, length = q.shape
    blocks = length // BLOCK
    full = pl.BlockSpec((1, HEAD_SIZE, length), lambda j, m, me: (j * GROUP + m, 0, 0))
    shared = pl.BlockSpec((1, HEAD_SIZE, length), lambda j, m, me: (j, 0, 0))
    return pl.pallas_call(
        functools.partial(attention_backward_kernel, blocks),
        grid_spec=pltpu.PrefetchScalarGridSpec(
            num_scalar_prefetch=1,
            grid=(heads // GROUP, GROUP),
            in_specs=[
                full,
                shared,
                shared,
                full,
                full,
                pl.BlockSpec((1, 1, length), lambda j, m, me: (j * GROUP + m, 0, 0)),
                pl.BlockSpec((length, 1), lambda j, m, me: (0, 0)),
                pl.BlockSpec((1, length), lambda j, m, me: (0, 0)),
            ],
            out_specs=[full, shared, shared],
            scratch_shapes=[
                pltpu.VMEM((length, HEAD_SIZE), jnp.bfloat16),
                pltpu.VMEM((length, HEAD_SIZE), jnp.bfloat16),
                pltpu.VMEM((length, HEAD_SIZE), jnp.float32),
                pltpu.VMEM((length, HEAD_SIZE), jnp.float32),
            ],
        ),
        out_shape=[
            jax.ShapeDtypeStruct((heads, HEAD_SIZE, length), jnp.float32),
            jax.ShapeDtypeStruct((heads // GROUP, HEAD_SIZE, length), jnp.float32),
            jax.ShapeDtypeStruct((heads // GROUP, HEAD_SIZE, length), jnp.float32),
        ],
        compiler_params=pltpu.CompilerParams(vmem_limit_bytes=48 * 1024 * 1024),
        cost_estimate=pl.CostEstimate(
            flops=10 * heads * length * length * HEAD_SIZE,
            bytes_accessed=16 * heads * length * HEAD_SIZE,
            transcendentals=heads * length * length // 2,
        ),
        name="attention_backward",
    )(me, q, k, v, o, g, lse, seg[:, None], seg[None, :])


def rope_tables(positions):
    freqs = 10000.0 ** (-(jnp.arange(HALF, dtype=jnp.float32) * 2.0 / HEAD_SIZE))
    angles = freqs[:, None] * positions.astype(jnp.float32)[None, :]
    return jnp.cos(angles)[None], jnp.sin(angles)[None]


def rotate(v, cosine, sine):
    a, b = v[:, :HALF, :], v[:, HALF:, :]
    return jnp.concatenate([a * cosine - b * sine, b * cosine + a * sine], axis=1)


def swap_member(v, bit):
    n = lax.axis_size("expert")
    return lax.ppermute(v, "expert", [(i, i ^ bit) for i in range(n)])


def swap_shard(v):
    n = lax.axis_size("shard")
    return lax.ppermute(v, "shard", [(i, i ^ 1) for i in range(n)])


def swap_sequence(v):
    got = swap_shard(v[: v.shape[0] // 2])
    return jnp.concatenate([got, swap_member(got, 1)], axis=0)


def chip_bits():
    n = lax.axis_size("expert")
    return [1 << i for i in range(1, n.bit_length() - 1)]


def gather_members(v, axis=0):
    for bit in chip_bits() + [1]:
        v = jnp.concatenate([v, swap_member(v, bit)], axis=axis)
    return v


def gather_heads(v):
    members = lax.axis_size("expert")
    width = v.shape[1] // members
    for bit in chip_bits() + [1]:
        got = swap_member(v, bit)
        source = [place_of(2 * (p % (members // 2)) + p // (members // 2), bit, members) for p in range(members)]
        got = jnp.concatenate([got[:, p * width : (p + 1) * width] for p in source], axis=1)
        v = jnp.concatenate([v, got], axis=0)
    return v


def halves(v, axis):
    return jnp.split(v, 2, axis=axis)


def add_swapped(keep, sent, swap):
    return keep.astype(jnp.float32) + swap(sent).astype(jnp.float32)


def scatter_members(own, other, axis=0):
    kind = own.dtype
    parts = []
    for v in (own, other):
        keep, sent = halves(v, axis)
        parts.append(add_swapped(keep, sent, lambda u: swap_member(u, 1)).astype(kind))
    own, other = parts
    total = add_swapped(own, other, swap_shard)
    for bit in reversed(chip_bits()):
        keep, sent = halves(total.astype(kind), axis)
        total = add_swapped(keep, sent, lambda u: swap_member(u, bit))
    return total


def turn(first, back=False):
    members, shards = lax.axis_size("expert"), lax.axis_size("shard")
    pairs = []
    for e in range(members):
        for s in range(shards):
            core, low = e & 1, s & 1
            to_core, to_low = (low, core) if first else (1 - low, core)
            target = ((e & ~1) | to_core) * shards + ((s & ~1) | to_low)
            pairs.append((e * shards + s, target))
    if back:
        pairs = [(b, a) for a, b in pairs]
    return pairs


def permute_all(v, pairs):
    return lax.ppermute(v, ("expert", "shard"), pairs)


def shard_lines():
    n = lax.axis_size("shard")
    return [[s for s in range(n) if s & 1 == low] for low in range(2)]


def gather_shard(v):
    return lax.all_gather(v, "shard", axis=0, tiled=True)


def scatter_shard(v):
    return lax.psum_scatter(v, "shard", scatter_dimension=0, tiled=True)


def out_kernel(members, me_ref, slice_ref, out_ref):
    size = slice_ref.shape[2]
    p = pl.program_id(0)
    r = 2 * (p % (members // 2)) + p // (members // 2)
    col = pl.multiple_of((me_ref[0] ^ r) * size, 128)
    for a in range(members):
        row = pl.multiple_of(place_of(a, me_ref[0], members) * size, 16)
        out_ref[pl.ds(row, size), pl.ds(col, size)] = slice_ref[0, a * size : (a + 1) * size, :]


def assemble_out(me, slices):
    members, rows, size = slices.shape
    return pl.pallas_call(
        functools.partial(out_kernel, members),
        grid_spec=pltpu.PrefetchScalarGridSpec(
            num_scalar_prefetch=1,
            grid=(members,),
            in_specs=[pl.BlockSpec((1, rows, size), lambda p, me: (p, 0, 0))],
            out_specs=pl.BlockSpec((rows, size * members), lambda p, me: (0, 0)),
        ),
        out_shape=jax.ShapeDtypeStruct((rows, size * members), slices.dtype),
        compiler_params=pltpu.CompilerParams(vmem_limit_bytes=48 * 1024 * 1024),
        name="assemble_out",
    )(me, slices)


def body(
    tokens,
    segment_ids,
    routes,
    gain_attn,
    w_query,
    key_weight,
    value_weight,
    w_out,
    gain_ffn,
    w_router,
    w_gate_up,
    w_down,
    cotangent,
):
    bf16, f32 = jnp.bfloat16, jnp.float32
    members = lax.axis_size("expert")
    shards = lax.axis_size("shard")
    me = lax.axis_index("expert")
    core = me & 1
    low = lax.axis_index("shard") & 1
    rows, width = tokens.shape[1:]
    length = rows * members
    experts = EXP_DEV * members
    q_cols = QUERY_HEADS * HEAD_SIZE // members
    k_cols = KEY_VALUE_HEADS * HEAD_SIZE // members
    heads, kv_heads = q_cols // HEAD_SIZE, k_cols // HEAD_SIZE
    out_rows = width // (members * shards)
    half = FF // 2
    me_ref = me[None].astype(jnp.int32)

    def cols(w, n):
        return lax.dynamic_slice_in_dim(w, me * n, n, axis=1)

    small = jnp.concatenate([w_router, gain_attn[:, None], gain_ffn[:, None]], axis=1)
    total_cols = q_cols + 2 * k_cols
    first = jnp.concatenate(
        [
            cols(w_query, q_cols),
            cols(key_weight, k_cols),
            cols(value_weight, k_cols),
            cols(w_out, q_cols),
            jnp.pad(small, ((0, 0), (0, 128 - small.shape[1]))),
        ],
        axis=1,
    )
    first = gather_shard(first)
    full_qkv = first[:, :total_cols]
    out_slice = first[:, total_cols : total_cols + q_cols]
    full_small = first[:, total_cols + q_cols :]
    full_router = full_small[:, :experts]
    gain_one = full_small[:, experts].astype(f32)
    gain_two = full_small[:, experts + 1].astype(f32)

    all_tokens = gather_members(tokens[0])
    meta = gather_members(jnp.concatenate([segment_ids[0][:, None], routes[0]], axis=1))
    seg = meta[:, 0]
    my_routes = meta[:, 1:]
    route_ids = jnp.concatenate([my_routes, swap_shard(my_routes)], axis=0)
    my_grad = gather_members(cotangent[0])
    all_grad = jnp.concatenate([my_grad, swap_sequence(my_grad)], axis=0)

    weights = []
    for js in CHUNKS:
        sides = [
            jnp.concatenate(
                [w_gate_up[:, j, h * half : (h + 1) * half] for j in js]
                + [w_gate_up[:, j, FF + h * half : FF + (h + 1) * half] for j in js]
                + [w_down[:, j, h * half : (h + 1) * half] for j in js],
                axis=1,
            )
            for h in range(2)
        ]
        one = permute_all(jnp.where(low == 0, sides[0], sides[1]), turn(True))
        two = permute_all(jnp.where(low == 0, sides[1], sides[0]), turn(False))
        block = jnp.concatenate(
            [jnp.where(core == 0, one, two), jnp.where(core == 0, two, one)], axis=0
        )
        weights.append(
            lax.all_gather(block, "shard", axis=0, tiled=True, axis_index_groups=shard_lines())
        )

    inputs = all_tokens.astype(f32)
    normed_one = inputs * inverse_rms(inputs)
    xn_one = (normed_one * gain_one).astype(bf16)
    qkv = dot(full_qkv, xn_one, 0, 1).reshape(heads + 2 * kv_heads, HEAD_SIZE, length)
    order = jnp.arange(members, dtype=jnp.int32)
    order = me ^ (2 * (order % (members // 2)) + order // (members // 2))
    positions = (order[:, None] * rows + jnp.arange(rows, dtype=jnp.int32)[None, :]).reshape(-1)
    cosine, sine = rope_tables(positions)
    rotated = rotate(qkv[: heads + kv_heads], cosine, sine).astype(bf16)
    queries = rotated[:heads] * jnp.asarray(HEAD_SIZE**-0.5, bf16)
    keys = rotated[heads:]
    values = qkv[heads + kv_heads :].astype(bf16)
    attended, lse = attention_forward(me_ref, queries, keys, values, seg)
    attended_rows = attended.reshape(q_cols, length)
    attended_all = gather_heads(attended_rows)
    full_out = assemble_out(me_ref, gather_members(out_slice[None]))

    hidden = inputs + dot(attended_all, full_out, 0, 0)
    normed_two = hidden * inverse_rms(hidden)
    my_xn_two = (normed_two * gain_two).astype(bf16)
    xn_two = jnp.concatenate([my_xn_two, swap_sequence(my_xn_two)], axis=0)

    logits = jnp.dot(xn_two, full_router, preferred_element_type=f32)
    named = jnp.any(
        route_ids[:, :, None] == jnp.arange(experts, dtype=jnp.int32)[None, None, :], axis=1
    )
    peak = jnp.max(jnp.where(named, logits, -jnp.inf), axis=1, keepdims=True)
    exps = jnp.where(named, jnp.exp(jnp.minimum(logits - peak, 0.0)), 0.0)
    gates = exps / jnp.sum(exps, axis=1, keepdims=True)
    group = (me & ~1) | low
    my_gates = lax.dynamic_slice_in_dim(gates, group * EXP_DEV, EXP_DEV, axis=1)

    count = 2 * length
    mix = jnp.zeros((count, width), f32)
    grad_in = jnp.zeros((count, width), f32)
    gate_grads, expert_grads = [], []
    for js, w in zip(CHUNKS, weights):
        n = len(js) * half
        w_in, w_back = w[:, : 2 * n], w[:, 2 * n :]
        gate_up = dot(xn_two, w_in, 1, 0)
        through = dot(all_grad, w_back, 1, 0)
        gate, up = gate_up[:, :n], gate_up[:, n:]
        weight = jnp.concatenate(
            [jnp.broadcast_to(my_gates[:, j : j + 1], (count, half)) for j in js], axis=1
        )
        sig = jax.nn.sigmoid(gate)
        act = gate * sig * up
        product = act * through
        for i in range(len(js)):
            gate_grads.append(jnp.sum(product[:, i * half : (i + 1) * half], axis=1))
        scaled = (weight * act).astype(bf16)
        grad_act = weight * through
        back = jnp.concatenate(
            [grad_act * up * sig * (1.0 + gate * (1.0 - sig)), grad_act * gate * sig], axis=1
        ).astype(bf16)
        mix = mix + dot(scaled, w_back, 1, 1)
        grad_in = grad_in + dot(back, w_in, 1, 1)
        grads = jnp.concatenate([dot(xn_two, back, 0, 0), dot(all_grad, scaled, 0, 0)], axis=1)
        expert_grads.append(
            lax.psum_scatter(
                grads.astype(bf16),
                "shard",
                scatter_dimension=0,
                tiled=True,
                axis_index_groups=shard_lines(),
            )
        )

    grad_xn_two = scatter_members(grad_in[:length].astype(bf16), grad_in[length:].astype(bf16))
    gate_grads = lax.dynamic_update_slice_in_dim(
        jnp.zeros((experts, count), f32), jnp.stack(gate_grads, axis=0), group * EXP_DEV, axis=0
    )
    grad_gates = scatter_members(gate_grads[:, :length], gate_grads[:, length:], axis=1).T
    own_gates = gates[:rows]
    grad_chosen = own_gates * (grad_gates - jnp.sum(own_gates * grad_gates, axis=1, keepdims=True))
    grad_logits = grad_chosen.astype(bf16)
    grad_xn_two = grad_xn_two + dot(grad_logits, full_router, 1, 1)
    my_hidden = hidden[:rows]

    my_scale = inverse_rms(my_hidden)
    my_normed = my_hidden * my_scale
    grad_gain_two = jnp.sum(grad_xn_two * my_normed, axis=0)
    g = grad_xn_two * gain_two
    grad_hidden = cotangent[0].astype(f32) + my_scale * (
        g - my_normed * jnp.mean(g * my_normed, axis=-1, keepdims=True)
    )
    grad_attn = gather_members(grad_hidden.astype(bf16))
    grad_attended = dot(full_out[:q_cols], grad_attn, 1, 1).astype(bf16)
    grad_attended = grad_attended.reshape(heads, HEAD_SIZE, length)
    grad_out = jnp.dot(attended_rows, grad_attn, preferred_element_type=f32)
    out_grads = scatter_shard(grad_out.astype(bf16)).astype(f32)
    grad_router = dot(xn_two[:rows], grad_logits, 0, 0)

    dq, dk, dv = attention_backward(me_ref, queries, keys, values, attended, grad_attended, lse, seg)
    dq = rotate(dq, cosine, -sine) * HEAD_SIZE**-0.5
    dk = rotate(dk, cosine, -sine)
    grad_qkv = jnp.concatenate([dq, dk, dv], axis=0).astype(bf16).reshape(-1, length)
    grad_first = dot(xn_one, grad_qkv, 0, 1)
    grad_xn_one = dot(grad_qkv, full_qkv, 0, 1)
    grad_gain_one = jnp.sum(grad_xn_one * normed_one, axis=0)
    grad_xn_one = grad_xn_one.astype(bf16)
    for bit in [1] + chip_bits()[::-1]:
        keep, sent = halves(grad_xn_one.astype(bf16), 0)
        grad_xn_one = add_swapped(keep, sent, lambda u: swap_member(u, bit))
    my_inputs = tokens[0].astype(f32)
    scale_one = inverse_rms(my_inputs)
    normed = my_inputs * scale_one
    h = grad_xn_one * gain_one
    grad_tokens = grad_hidden + scale_one * (h - normed * jnp.mean(h * normed, axis=-1, keepdims=True))

    rest = jnp.concatenate([grad_router, grad_gain_one[:, None], grad_gain_two[:, None]], axis=1)
    rest = jnp.pad(rest, ((0, 0), (0, 128 - rest.shape[1])))
    grad_first = jnp.concatenate([grad_first, rest], axis=1).astype(bf16)
    grad_first = jnp.transpose(grad_first.reshape(members, shards, out_rows, -1), (1, 0, 2, 3))
    grad_first = scatter_shard(grad_first.reshape(width, -1)).reshape(members, out_rows, -1)
    grad_first = lax.all_to_all(grad_first, "expert", split_axis=0, concat_axis=0, tiled=True)
    rest = jnp.sum(grad_first[:, :, total_cols:].astype(f32), axis=0)
    grad_first = jnp.transpose(grad_first, (1, 0, 2)).astype(f32)

    mixed = my_hidden + scatter_members(mix[:length].astype(bf16), mix[length:].astype(bf16))

    gate_up_out, down_out = [], []
    for js, v in zip(CHUNKS, expert_grads):
        size = v.shape[0] // 2
        one = permute_all(jnp.where(core == 0, v[:size], v[size:]), turn(True, True))
        two = permute_all(jnp.where(core == 0, v[size:], v[:size]), turn(False, True))
        sides = [jnp.where(low == 0, one, two), jnp.where(low == 0, two, one)]
        n = len(js)
        for i in range(n):
            piece = [
                [sides[h][:, (k * n + i) * half : (k * n + i + 1) * half] for h in range(2)]
                for k in range(3)
            ]
            gate_up_out.append(jnp.concatenate(piece[0] + piece[1], axis=1))
            down_out.append(jnp.concatenate(piece[2], axis=1))
    return (
        mixed.astype(bf16)[None],
        grad_tokens.astype(bf16)[None],
        rest[:, experts],
        grad_first[:, :, :q_cols].reshape(out_rows, -1),
        grad_first[:, :, q_cols : q_cols + k_cols].reshape(out_rows, -1),
        grad_first[:, :, q_cols + k_cols : total_cols].reshape(out_rows, -1),
        out_grads,
        rest[:, experts + 1],
        rest[:, :experts],
        jnp.stack(gate_up_out, axis=1).astype(f32),
        jnp.stack(down_out, axis=1).astype(f32),
    )


def solution(mesh):
    in_specs = (
        P("shard", "expert", None),
        P("shard", "expert"),
        P("shard", "expert", None),
        P("shard"),
        P("shard", None),
        P("shard", None),
        P("shard", None),
        P("shard", None),
        P("shard"),
        P("shard", None),
        P("shard", "expert", None),
        P("shard", "expert", None),
        P("shard", "expert", None),
    )
    out_specs = (
        P("shard", "expert", None),
        P("shard", "expert", None),
        P(("expert", "shard")),
        P(("expert", "shard"), None),
        P(("expert", "shard"), None),
        P(("expert", "shard"), None),
        P(("expert", "shard"), None),
        P(("expert", "shard")),
        P(("expert", "shard"), None),
        P("shard", "expert", None),
        P("shard", "expert", None),
    )
    return jax.shard_map(body, mesh=mesh, in_specs=in_specs, out_specs=out_specs, check_vma=False)
```

time: 1620 us -> 886 us (0.55)
  waiting for transfers between devices: 1140 us -> 398 us
  starting transfers between devices: 4.94 us -> 55.8 us
  blocking collectives: 43.1 us -> 0 us
  local copies, waits for them, and re-layouts: 110 us -> 73.7 us
  other arithmetic: 50.1 us -> 72 us
    unnamed x29 -> x9, waiting for transfers between devices: 443 us -> 0.15 us
    all_gather x7 -> x1, waiting for transfers between devices: 434 us -> 3.26 us  [gather_shard(): return lax.all_gather(v, 'shard', axis=0, tiled=True)]
    ppermute x0 -> x43, waiting for transfers between devices: none -> 239 us  [the longest x25 101 us: swap_member(): return lax.ppermute(v, 'expert', [(i, i ^ bit) for i in range(n)])]
    reduce_scatter x2, waiting for transfers between devices: 107 us -> 52.8 us  [scatter_shard(): return lax.psum_scatter(v, 'shard', scatter_dimension=0, tiled=True)]
    ppermute x0 -> x43, starting transfers between devices: none -> 51.2 us  [the longest x12 28.4 us: permute_all(): return lax.ppermute(v, ('expert', 'shard'), pairs)]
    all_gather x5 -> x3, waiting for transfers between devices: 49.7 us -> 0.06 us  [body(): lax.all_gather(block, 'shard', axis=0, tiled=True, axis_index_groups=shar...]
    all_gather x3 -> x0, blocking collectives: 43.1 us -> none  [the longest x1 30.6 us: gather_shard(): return lax.all_gather(v, 'shard', axis=0, tiled=True)]
    unnamed x224 -> x182, local copies, waits for them, and re-layouts: 83.7 us -> 43 us
  transfers between devices with their start and end apart: 24 -> 53, of which waited for: 20 -> 21; matrix products, arithmetic and copies ran while one was open for 17% -> 38% of each run, Pallas kernels for 2% -> 4%
where the time goes in v2:
time: 886 us; the launch traced here: 876 us
  waiting for transfers between devices  398 us (45%)
  matrix products  224 us (25%)
  local copies, waits for them, and re-layouts  73.7 us (8%)
  other arithmetic  72 us (8%)
  starting transfers between devices  55.8 us (6%)
  Pallas kernels  36.7 us (4%)
  between operations  15.7 us (2%)
    dot_general x25, matrix products, dot(): lax.dot_general(a, b, (((ca,), (cb,)), ((), ())), preferred_element_type=...  215 us
    ppermute x25, waiting for transfers between devices, swap_member(): return lax.ppermute(v, 'expert', [(i, i ^ bit) for i in range(n)])  101 us
    reduce_scatter x3, waiting for transfers between devices, body(): lax.psum_scatter(grads.astype(bf16), 'shard', scatter_dimension=0, tiled=...  99.5 us
    ppermute x6, waiting for transfers between devices, swap_shard(): return lax.ppermute(v, 'shard', [(i, i ^ 1) for i in range(n)])  92.7 us
    reduce_scatter x2, waiting for transfers between devices, scatter_shard(): return lax.psum_scatter(v, 'shard', scatter_dimension=0, tiled=True)  52.8 us
    ppermute x12, waiting for transfers between devices, permute_all(): return lax.ppermute(v, ('expert', 'shard'), pairs)  44.7 us
    unnamed x182, local copies, waits for them, and re-layouts  43 us
    ppermute x12, starting transfers between devices, permute_all(): return lax.ppermute(v, ('expert', 'shard'), pairs)  28.4 us
  transfers between devices with their start and end apart: 53, of which 21 were waited for; matrix products, arithmetic and copies ran while one was open for 38% of the time, Pallas kernels for 4%

profile of v2, /device:TPU:0, one launch (start us, length us, event | category | flops | bytes accessed | tf_op | source)
XLA Modules:
  0.0 875.9 jit_solution(15301554102131835593)
XLA Ops:
  24.3 19.1 %collective-permute-done.14 = bf16[192,1536]{1,0:T(8,128)(2,1)} collective-permute-done((bf16[192,1536]{1,0:T(8,128)(2,1)S(1)}, bf16[192,1536]{1,0:T(8,128)(2,1)}, u32[]{:S(2)}, u32[]{:S(2)}) %collective-permute-start.14) | collective-permute-done | bytes 589856 | tf_op jit(solution)/shard_map/ppermute | solution.py:281
  47.3 16.9 %collective-permute-done = bf16[256,1536]{1,0:T(8,128)(2,1)S(1)} collective-permute-done((bf16[256,1536]{1,0:T(8,128)(2,1)S(1)}, bf16[256,1536]{1,0:T(8,128)(2,1)S(1)}, u32[]{:S(2)}, u32[]{:S(2)}) %collective-permute-start) | collective-permute-done | bytes 786464 | tf_op jit(solution)/shard_map/ppermute | solution.py:209
  92.5 17.6 %attention_forward.1 = (bf16[6,64,1024]{2,1,0:T(8,128)(2,1)S(1)}, f32[6,1,1024]{2,1,0:T(1,128)S(1)}) custom-call(s32[1]{0:T(128)} %bitcast.1.me_ref, bf16[6,64,1024]{2,1,0:T(8,128)(2,1)S(1)} %fusion.60.q_ref, bf16[2,64,1024]{2,1,0:T(8,128)(2,1)S(1)} %pad_maximum_fusion.29.k_ref, bf16[2,64,1024]{2,1,0:T(8,128)(2,1)S(1)} %bitcast.191, ...), custom_call_target="tpu_custom_call" | custom-call | flops 1610612736 | bytes 2359296 | tf_op jit(solution)/shard_map/attention_forward/pallas_call | solution.py:83
  121.2 12.8 %collective-permute-done.4 = bf16[384,1024]{1,0:T(8,128)(2,1)S(1)} collective-permute-done((bf16[384,1024]{1,0:T(8,128)(2,1)S(1)}, bf16[384,1024]{1,0:T(8,128)(2,1)S(1)}, u32[]{:S(2)}, u32[]{:S(2)}) %collective-permute-start.4) | collective-permute-done | bytes 786464 | tf_op jit(solution)/shard_map/ppermute | solution.py:209
  139.2 18.7 %collective-permute-done.21 = bf16[256,1536]{1,0:T(8,128)(2,1)S(1)} collective-permute-done((bf16[256,1536]{1,0:T(8,128)(2,1)}, bf16[256,1536]{1,0:T(8,128)(2,1)S(1)}, u32[]{:S(2)}, u32[]{:S(2)}) %collective-permute-start.21) | collective-permute-done | bytes 786464 | tf_op jit(solution)/shard_map/ppermute | solution.py:209
  169.7 12.6 %multiply_reduce_fusion = (f32[1024]{0:T(1024)S(1)}, f32[1024,1536]{1,0:T(8,128)S(1)}) fusion(bf16[1536,1536]{1,0:T(8,128)(2,1)S(1)} %assemble_out.1, bf16[768,512]{1,0:T(8,128)(2,1)S(1)} %get-tuple-element.144, bf16[768,512]{1,0:T(8,128)(2,1)S(1)} %get-tuple-element.143, bf16[384,256]{1,0:T(8,128)(2,1)S(1)} %get-tuple-element.174, ...), kind=kOutput, calls=%fused_computation.12 | convolution fusion | flops 4868013056 | bytes 17305600 | tf_op jit(solution)/shard_map/dot_general | solution.py:25
  199.1 35.3 %collective-permute-done.8 = s32[1024,8]{0,1:T(8,128)S(1)} collective-permute-done((s32[1024,8]{0,1:T(8,128)}, s32[1024,8]{0,1:T(8,128)S(1)}, u32[]{:S(2)}, u32[]{:S(2)}) %collective-permute-start.8) | collective-permute-done | bytes 32800 | tf_op jit(solution)/shard_map/ppermute | solution.py:214
  262.3 11.9 %fusion.25 = f32[2048,1024]{0,1:T(8,128)} fusion(bf16[1536,1536]{1,0:T(8,128)(2,1)} %all-gather.9.cloned.1.call-done, bf16[512,1536]{1,0:T(8,128)(2,1)} %collective-permute-done.10, bf16[512,1536]{1,0:T(8,128)(2,1)} %collective-permute-done.9, bf16[1024,1536]{1,0:T(8,128)(2,1)S(1)} %multiply_convert_fusion), kind=kOutput, calls=%fused_computation.63 | convolution fusion | flops 6461325312 | bytes 17825792 | tf_op jit(solution)/shard_map/dot_general | solution.py:25
  274.7 12.4 %multiply_convert_fusion.2 = (bf16[2048,512]{0,1:T(8,128)(2,1)}, bf16[2048,512]{0,1:T(8,128)(2,1)}, f32[2048,512]{0,1:T(8,128)S(1)}) fusion(f32[2048,1024]{0,1:T(8,128)} %fusion.25, f32[2048,256]{0,1:T(8,128)S(1)} %broadcast_in_dim.102, f32[2048,256]{0,1:T(8,128)S(1)} %broadcast_in_dim.100, bf16[2048,1536]{1,0:T(8,128)(2,1)} %constant_dynamic-update-slice_fusion.3, ...), kind=kOutput, calls=%fused_computation.27 | convolution fusion | flops 3240099840 | bytes 28835840 | tf_op jit(solution)/shard_map/dot_general | solution.py:25
  287.4 12.2 %fusion.29 = f32[2048,1024]{0,1:T(8,128)} fusion(bf16[1536,1536]{1,0:T(8,128)(2,1)} %all-gather.7.cloned.1.call-done, bf16[512,1536]{1,0:T(8,128)(2,1)} %collective-permute-done.10, bf16[512,1536]{1,0:T(8,128)(2,1)} %collective-permute-done.9, bf16[1024,1536]{1,0:T(8,128)(2,1)S(1)} %multiply_convert_fusion), kind=kOutput, calls=%fused_computation.67 | convolution fusion | flops 6461325312 | bytes 17825792 | tf_op jit(solution)/shard_map/dot_general | solution.py:25
  300.1 12.4 %multiply_convert_fusion.4 = (bf16[2048,512]{0,1:T(8,128)(2,1)}, bf16[2048,512]{0,1:T(8,128)(2,1)}, f32[2048,512]{0,1:T(8,128)S(1)}) fusion(f32[2048,1024]{0,1:T(8,128)} %fusion.29, f32[2048,256]{0,1:T(8,128)S(1)} %broadcast_in_dim.98, f32[2048,256]{0,1:T(8,128)S(1)} %broadcast_in_dim.96, bf16[2048,1536]{1,0:T(8,128)(2,1)} %constant_dynamic-update-slice_fusion.3, ...), kind=kOutput, calls=%fused_computation.29 | convolution fusion | flops 3240099840 | bytes 28835840 | tf_op jit(solution)/shard_map/dot_general | solution.py:25
  312.7 7.3 fusion.45
  320.0 7.9 multiply_convert_fusion.6
  329.1 12.8 %fusion.27 = f32[2048,1536]{1,0:T(8,128)} fusion(bf16[1536,1536]{1,0:T(8,128)(2,1)} %all-gather.7.cloned.1.call-done, bf16[2048,512]{0,1:T(8,128)(2,1)} %get-tuple-element.104, bf16[2048,512]{0,1:T(8,128)(2,1)} %get-tuple-element.103), kind=kOutput, calls=%fused_computation.65 | convolution fusion | flops 6450839552 | bytes 19922944 | tf_op jit(solution)/shard_map/dot_general | solution.py:25
  348.4 15.9 %add_convert_fusion = bf16[2048,1536]{1,0:T(8,128)(2,1)} fusion(f32[2048,1536]{1,0:T(8,128)} %fusion.43, f32[2048,1536]{1,0:T(8,128)} %fusion.27, bf16[1536,1536]{1,0:T(8,128)(2,1)} %all-gather.9.cloned.1.call-done, bf16[2048,512]{0,1:T(8,128)(2,1)} %get-tuple-element.102, bf16[2048,512]{0,1:T(8,128)(2,1)} %get-tuple-element.101), kind=kOutput, calls=%fused_computation | convolution fusion | flops 6460276736 | bytes 38797312 | tf_op jit(solution)/shard_map/dot_general | solution.py:25
  368.6 12.7 %fusion.49 = f32[2048,1536]{1,0:T(8,128)} fusion(bf16[1536,1536]{1,0:T(8,128)(2,1)} %all-gather.9.cloned.1.call-done, f32[2048,256]{0,1:T(8,128)S(1)} %copy-done.30, f32[2048,256]{0,1:T(8,128)S(1)} %copy-done.33, f32[2048,1024]{0,1:T(8,128)} %fusion.25), kind=kOutput, calls=%fused_computation.120 | convolution fusion | flops 3229614080 | bytes 26738688 | tf_op jit(solution)/shard_map/dot_general | solution.py:25
  381.3 12.7 %fusion.53 = f32[2048,1536]{1,0:T(8,128)} fusion(bf16[1536,1536]{1,0:T(8,128)(2,1)} %all-gather.7.cloned.1.call-done, f32[2048,256]{0,1:T(8,128)S(1)} %copy-done.36, f32[2048,256]{0,1:T(8,128)S(1)} %copy-done.39, f32[2048,1024]{0,1:T(8,128)} %fusion.29), kind=kOutput, calls=%fused_computation.124 | convolution fusion | flops 3229614080 | bytes 26738688 | tf_op jit(solution)/shard_map/dot_general | solution.py:25
  394.0 12.5 %add_convert_fusion.1 = bf16[2048,1536]{1,0:T(8,128)(2,1)} fusion(f32[2048,1536]{1,0:T(8,128)} %fusion.53, f32[2048,1536]{1,0:T(8,128)} %fusion.49, bf16[1536,768]{1,0:T(8,128)(2,1)} %all-gather.11.cloned.1.call-done, f32[2048,256]{0,1:T(8,128)S(1)} %copy-done.28, f32[2048]{0:T(1024)S(1)} %bitcast.224), kind=kOutput, calls=%fused_computation.1 | convolution fusion | flops 1621098496 | bytes 34349056 | tf_op jit(solution)/shard_map/dot_general | solution.py:25
  433.2 25.7 %collective-permute-done.27 = bf16[512,1536]{1,0:T(8,128)(2,1)} collective-permute-done((bf16[512,1536]{1,0:T(8,128)(2,1)}, bf16[512,1536]{1,0:T(8,128)(2,1)}, u32[]{:S(2)}, u32[]{:S(2)}) %collective-permute-start.27) | collective-permute-done | bytes 1572896 | tf_op jit(solution)/shard_map/ppermute | solution.py:214
  463.6 27.7 %collective-permute-done.19 = bf16[512,1536]{1,0:T(8,128)(2,1)} collective-permute-done((bf16[512,1536]{1,0:T(8,128)(2,1)}, bf16[512,1536]{1,0:T(8,128)(2,1)}, u32[]{:S(2)}, u32[]{:S(2)}) %collective-permute-start.19) | collective-permute-done | bytes 1572896 | tf_op jit(solution)/shard_map/ppermute | solution.py:214
  498.6 14.3 %collective-permute-done.20 = bf16[256,1536]{1,0:T(8,128)(2,1)S(1)} collective-permute-done((bf16[256,1536]{1,0:T(8,128)(2,1)S(1)}, bf16[256,1536]{1,0:T(8,128)(2,1)S(1)}, u32[]{:S(2)}, u32[]{:S(2)}) %collective-permute-start.20) | collective-permute-done | bytes 786464 | tf_op jit(solution)/shard_map/ppermute | solution.py:209
  516.8 16.0 %collective-permute-done.33 = bf16[256,1536]{1,0:T(8,128)(2,1)S(1)} collective-permute-done((bf16[256,1536]{1,0:T(8,128)(2,1)S(1)}, bf16[256,1536]{1,0:T(8,128)(2,1)S(1)}, u32[]{:S(2)}, u32[]{:S(2)}) %collective-permute-start.33) | collective-permute-done | bytes 786464 | tf_op jit(solution)/shard_map/ppermute | solution.py:209
  540.0 10.8 %convolution_convert_fusion.1 = bf16[1536,1024]{0,1:T(8,128)(2,1)S(1)} fusion(bf16[2048,512]{0,1:T(8,128)(2,1)} %get-tuple-element.104, bf16[2048,512]{0,1:T(8,128)(2,1)} %get-tuple-element.103, bf16[512,1536]{1,0:T(8,128)(2,1)} %collective-permute-done.10, bf16[512,1536]{1,0:T(8,128)(2,1)} %collective-permute-done.9, bf16[1024,1536]{1,0:T(8,128)(2,1)} %copy-done.16), kind=kOutput, calls=%fused_computation.35 | convolution fusion | flops 6471286784 | bytes 13631488 | tf_op jit(solution)/shard_map/dot_general | solution.py:25
  550.8 9.0 %convolution_convert_fusion.4 = bf16[1536,512]{0,1:T(8,128)(2,1)S(1)} fusion(bf16[2048,1536]{1,0:T(8,128)(2,1)} %constant_dynamic-update-slice_fusion.3, f32[2048,256]{0,1:T(8,128)S(1)} %copy-done.37, f32[2048,256]{0,1:T(8,128)S(1)} %copy-done.40, f32[2048,1024]{0,1:T(8,128)} %fusion.29), kind=kOutput, calls=%fused_computation.60 | convolution fusion | flops 3230400512 | bytes 20447232 | tf_op jit(solution)/shard_map/dot_general | solution.py:25
  569.2 10.3 %convolution_convert_fusion = bf16[1536,1024]{0,1:T(8,128)(2,1)S(1)} fusion(bf16[2048,512]{0,1:T(8,128)(2,1)} %get-tuple-element.102, bf16[2048,512]{0,1:T(8,128)(2,1)} %get-tuple-element.101, bf16[512,1536]{1,0:T(8,128)(2,1)} %collective-permute-done.10, bf16[512,1536]{1,0:T(8,128)(2,1)} %collective-permute-done.9, bf16[1024,1536]{1,0:T(8,128)(2,1)} %copy-done.16), kind=kOutput, calls=%fused_computation.34 | convolution fusion | flops 6471286784 | bytes 13631488 | tf_op jit(solution)/shard_map/dot_general | solution.py:25
  579.5 9.0 %convolution_convert_fusion.3 = bf16[1536,512]{0,1:T(8,128)(2,1)S(1)} fusion(bf16[2048,1536]{1,0:T(8,128)(2,1)} %constant_dynamic-update-slice_fusion.3, f32[2048,256]{0,1:T(8,128)S(1)} %copy-done.31, f32[2048,256]{0,1:T(8,128)S(1)} %copy-done.34, f32[2048,1024]{0,1:T(8,128)} %fusion.25), kind=kOutput, calls=%fused_computation.59 | convolution fusion | flops 3230400512 | bytes 20447232 | tf_op jit(solution)/shard_map/dot_general | solution.py:25
  601.5 15.8 %attention_backward.1 = (f32[6,64,1024]{2,1,0:T(8,128)S(1)}, f32[2,64,1024]{2,1,0:T(8,128)S(1)}, f32[2,64,1024]{2,1,0:T(8,128)S(1)}) custom-call(s32[1]{0:T(128)} %bitcast.1.me_ref, bf16[6,64,1024]{2,1,0:T(8,128)(2,1)S(1)} %copy-done.2, bf16[2,64,1024]{2,1,0:T(8,128)(2,1)S(1)} %copy-done.8, bf16[2,64,1024]{2,1,0:T(8,128)(2,1)S(1)} %bitcast.192, ...), custom_call_target="tpu_custom_call" | custom-call | flops 4026531840 | bytes 6291456 | tf_op jit(solution)/shard_map/attention_backward/pallas_call | solution.py:158
  658.3 12.0 %collective-permute-done.36 = bf16[256,1536]{1,0:T(8,128)(2,1)S(1)} collective-permute-done((bf16[256,1536]{1,0:T(8,128)(2,1)}, bf16[256,1536]{1,0:T(8,128)(2,1)S(1)}, u32[]{:S(2)}, u32[]{:S(2)}) %collective-permute-start.36) | collective-permute-done | bytes 786464 | tf_op jit(solution)/shard_map/ppermute | solution.py:209
  670.7 21.3 %reduce-scatter.16.cloned.1.call-done = bf16[384,1536]{1,0:T(8,128)(2,1)} async-done(((bf16[1536,1536]{1,0:T(8,128)(2,1)}), bf16[384,1536]{1,0:T(8,128)(2,1)}) %reduce-scatter.16.cloned.1.call-update) | async-done | bytes 1179664 | tf_op jit(solution)/shard_map/reduce_scatter | solution.py:464
  701.9 78.2 %reduce-scatter.18.cloned.1.call-done = bf16[384,1536]{1,0:T(8,128)(2,1)} async-done(((bf16[1536,1536]{1,0:T(8,128)(2,1)}), bf16[384,1536]{1,0:T(8,128)(2,1)}) %reduce-scatter.18.cloned.1.call-update) | async-done | bytes 1179664 | tf_op jit(solution)/shard_map/reduce_scatter | solution.py:464
  786.4 14.7 %collective-permute-done.40 = bf16[192,1536]{1,0:T(8,128)(2,1)S(1)} collective-permute-done((bf16[192,1536]{1,0:T(8,128)(2,1)S(1)}, bf16[192,1536]{1,0:T(8,128)(2,1)S(1)}, u32[]{:S(2)}, u32[]{:S(2)}) %collective-permute-start.40) | collective-permute-done | bytes 589856 | tf_op jit(solution)/shard_map/ppermute | solution.py:281
  803.1 52.7 %reduce-scatter.12.cloned.1.call-done = bf16[192,768]{1,0:T(8,128)(2,1)} async-done(((bf16[1536,768]{1,0:T(8,128)(2,1)}), bf16[192,768]{1,0:T(8,128)(2,1)}) %reduce-scatter.12.cloned.1.call-update) | async-done | bytes 294928 | tf_op jit(solution)/shard_map/reduce_scatter | solution.py:294
  (425 shorter events, 279.2 us)
Async XLA Ops:
  7.2 75.2 %all-gather.5.cloned.1.call-start = ((), (), s32[]{:S(2)}) async-start(), calls=%async_computation.6 | async-start | bytes 3981312 | tf_op jit(solution)/shard_map/all_gather | solution.py:290
  13.8 248.4 %all-gather.9.cloned.1.call-start = ((), (), s32[]{:S(2)}) async-start(), calls=%async_computation.8 | async-start | bytes 5898240 | tf_op jit(solution)/shard_map/all_gather | solution.py:402
  21.0 22.4 %collective-permute-start.14 = (bf16[192,1536]{1,0:T(8,128)(2,1)S(1)}, bf16[192,1536]{1,0:T(8,128)(2,1)}, u32[]{:S(2)}, u32[]{:S(2)}) collective-permute-start(bf16[192,1536]{1,0:T(8,128)(2,1)S(1)} %get-tuple-element.156), channel_id=1, source_target_pairs={{0,8},{1,0},{2,10},{3,2},{4,12},{5,4},{6,14},{7,6},{8,9},{9,1},{10... | collective-permute-start | bytes 1769480 | tf_op jit(solution)/shard_map/ppermute | solution.py:281
  45.7 241.7 %all-gather.7.cloned.1.call-start = ((), (), s32[]{:S(2)}) async-start(), calls=%async_computation.7 | async-start | bytes 5898240 | tf_op jit(solution)/shard_map/all_gather | solution.py:402
  68.3 42.5 %collective-permute-start.11 = (bf16[192,1536]{1,0:T(8,128)(2,1)}, bf16[192,1536]{1,0:T(8,128)(2,1)}, u32[]{:S(2)}, u32[]{:S(2)}) collective-permute-start(bf16[192,1536]{1,0:T(8,128)(2,1)} %get-tuple-element.159), channel_id=1, source_target_pairs={{0,0},{1,8},{2,2},{3,10},{4,4},{5,12},{6,6},{7,14},{8,1},{9,9},{10... | collective-permute-start | bytes 1769480 | tf_op jit(solution)/shard_map/ppermute | solution.py:281
  74.2 36.5 %collective-permute-start.12 = (bf16[192,1536]{1,0:T(8,128)(2,1)}, bf16[192,1536]{1,0:T(8,128)(2,1)}, u32[]{:S(2)}, u32[]{:S(2)}) collective-permute-start(bf16[192,1536]{1,0:T(8,128)(2,1)} %get-tuple-element.160), channel_id=1, source_target_pairs={{0,8},{1,0},{2,10},{3,2},{4,12},{5,4},{6,14},{7,6},{8,9},{9,1},{10... | collective-permute-start | bytes 1769480 | tf_op jit(solution)/shard_map/ppermute | solution.py:281
  90.4 29.0 %collective-permute-start.6 = (bf16[1,1536,384]{2,1,0:T(8,128)(2,1)S(1)}, bf16[1,1536,384]{2,1,0:T(8,128)(2,1)S(1)}, u32[]{:S(2)}, u32[]{:S(2)}) collective-permute-start(bf16[1,1536,384]{2,1,0:T(8,128)(2,1)S(1)} %slice_bitcast_fusion), channel_id=1, source_target_pairs={{0,16},{8,24},{16,0},{24,8},{1,17},{9,25},{17,1},{25,9},{2,18},{10... | collective-permute-start | bytes 3538952 | tf_op jit(solution)/shard_map/ppermute | solution.py:209
  110.1 23.8 %collective-permute-start.4 = (bf16[384,1024]{1,0:T(8,128)(2,1)S(1)}, bf16[384,1024]{1,0:T(8,128)(2,1)S(1)}, u32[]{:S(2)}, u32[]{:S(2)}) collective-permute-start(bf16[384,1024]{1,0:T(8,128)(2,1)S(1)} %bitcast.187), channel_id=1, source_target_pairs={{0,16},{8,24},{16,0},{24,8},{1,17},{9,25},{17,1},{25,9},{2,18},{10... | collective-permute-start | bytes 2359304 | tf_op jit(solution)/shard_map/ppermute | solution.py:209
  121.2 41.4 %collective-permute-start.7 = (bf16[2,1536,384]{2,1,0:T(8,128)(2,1)}, bf16[2,1536,384]{2,1,0:T(8,128)(2,1)}, u32[]{:S(2)}, u32[]{:S(2)}) collective-permute-start(bf16[2,1536,384]{2,1,0:T(8,128)(2,1)} %pad_maximum_fusion.14), channel_id=1, source_target_pairs={{0,8},{8,0},{16,24},{24,16},{1,9},{9,1},{17,25},{25,17},{2,10},{10... | collective-permute-start | bytes 7077896 | tf_op jit(solution)/shard_map/ppermute | solution.py:209
  136.0 25.1 %collective-permute-start.5 = (bf16[768,1024]{1,0:T(8,128)(2,1)}, bf16[768,1024]{1,0:T(8,128)(2,1)}, u32[]{:S(2)}, u32[]{:S(2)}) collective-permute-start(bf16[768,1024]{1,0:T(8,128)(2,1)} %maximum_maximum_fusion), channel_id=1, source_target_pairs={{0,8},{8,0},{16,24},{24,16},{1,9},{9,1},{17,25},{25,17},{2,10},{10... | collective-permute-start | bytes 4718600 | tf_op jit(solution)/shard_map/ppermute | solution.py:209
  137.1 175.6 %all-gather.11.cloned.1.call-start = ((), (), s32[]{:S(2)}) async-start(), calls=%async_computation.9 | async-start | bytes 2949120 | tf_op jit(solution)/shard_map/all_gather | solution.py:402
  160.5 37.6 %collective-permute-start.23 = (bf16[512,1536]{1,0:T(8,128)(2,1)}, bf16[512,1536]{1,0:T(8,128)(2,1)}, u32[]{:S(2)}, u32[]{:S(2)}) collective-permute-start(bf16[512,1536]{1,0:T(8,128)(2,1)} %pad_maximum_fusion.18), channel_id=1, source_target_pairs={{0,1},{1,0},{2,3},{3,2},{4,5},{5,4},{6,7},{7,6},{8,9},{9,8},{10,11... | collective-permute-start | bytes 4718600 | tf_op jit(solution)/shard_map/ppermute | solution.py:214
  186.2 56.0 %collective-permute-start.9 = (bf16[512,1536]{1,0:T(8,128)(2,1)}, bf16[512,1536]{1,0:T(8,128)(2,1)}, u32[]{:S(2)}, u32[]{:S(2)}) collective-permute-start(bf16[512,1536]{1,0:T(8,128)(2,1)} %slice.547), channel_id=1, source_target_pairs={{0,1},{1,0},{2,3},{3,2},{4,5},{5,4},{6,7},{7,6},{8,9},{9,8},{10,11... | collective-permute-start | bytes 4718600 | tf_op jit(solution)/shard_map/ppermute | solution.py:214
  189.6 46.0 %collective-permute-start.15 = (bf16[192,768]{1,0:T(8,128)(2,1)}, bf16[192,768]{1,0:T(8,128)(2,1)}, u32[]{:S(2)}, u32[]{:S(2)}) collective-permute-start(bf16[192,768]{1,0:T(8,128)(2,1)} %get-tuple-element.209), channel_id=1, source_target_pairs={{0,0},{1,8},{2,2},{3,10},{4,4},{5,12},{6,6},{7,14},{8,1},{9,9},{10... | collective-permute-start | bytes 884744 | tf_op jit(solution)/shard_map/ppermute | solution.py:281
  193.4 52.1 %collective-permute-start.22 = (bf16[512,1536]{1,0:T(8,128)(2,1)}, bf16[512,1536]{1,0:T(8,128)(2,1)}, u32[]{:S(2)}, u32[]{:S(2)}) collective-permute-start(bf16[512,1536]{1,0:T(8,128)(2,1)} %pad_maximum_fusion.18), channel_id=1, source_target_pairs={{0,8},{8,0},{16,24},{24,16},{1,9},{9,1},{17,25},{25,17},{2,10},{10... | collective-permute-start | bytes 4718600 | tf_op jit(solution)/shard_map/ppermute | solution.py:209
  194.0 40.4 %collective-permute-start.8 = (s32[1024,8]{0,1:T(8,128)}, s32[1024,8]{0,1:T(8,128)S(1)}, u32[]{:S(2)}, u32[]{:S(2)}) collective-permute-start(s32[1024,8]{0,1:T(8,128)} %pad_add_fusion.1), channel_id=1, source_target_pairs={{0,1},{1,0},{2,3},{3,2},{4,5},{5,4},{6,7},{7,6},{8,9},{9,8},{10,11... | collective-permute-start | bytes 98312 | tf_op jit(solution)/shard_map/ppermute | solution.py:214
  198.1 52.7 %collective-permute-start.24 = (bf16[512,1536]{1,0:T(8,128)(2,1)}, bf16[512,1536]{1,0:T(8,128)(2,1)}, u32[]{:S(2)}, u32[]{:S(2)}) collective-permute-start(bf16[512,1536]{1,0:T(8,128)(2,1)} %collective-permute-done.23), channel_id=1, source_target_pairs={{0,8},{8,0},{16,24},{24,16},{1,9},{9,1},{17,25},{25,17},{2,10},{10... | collective-permute-start | bytes 4718600 | tf_op jit(solution)/shard_map/ppermute | solution.py:209
  243.2 385.4 %reduce-scatter.20.cloned.1.call-start = ((), (), s32[]{:S(2)}) async-start(), calls=%async_computation.14 | async-start | bytes 2949120 | tf_op jit(solution)/shard_map/reduce_scatter | solution.py:464
  328.5 96.8 %collective-permute-start.29 = (f32[20,512]{1,0:T(8,128)S(1)}, f32[20,512]{1,0:T(8,128)S(1)}, u32[]{:S(2)}, u32[]{:S(2)}) collective-permute-start(f32[20,512]{1,0:T(8,128)S(1)} %get-tuple-element.217), channel_id=1, source_target_pairs={{0,8},{8,0},{16,24},{24,16},{1,9},{9,1},{17,25},{25,17},{2,10},{10... | collective-permute-start | bytes 122888 | tf_op jit(solution)/shard_map/ppermute | solution.py:209
  329.0 86.8 %collective-permute-start.30 = (f32[20,512]{1,0:T(8,128)S(1)}, f32[20,512]{1,0:T(8,128)}, u32[]{:S(2)}, u32[]{:S(2)}) collective-permute-start(f32[20,512]{1,0:T(8,128)S(1)} %get-tuple-element.218), channel_id=1, source_target_pairs={{0,8},{8,0},{16,24},{24,16},{1,9},{9,1},{17,25},{25,17},{2,10},{10... | collective-permute-start | bytes 122888 | tf_op jit(solution)/shard_map/ppermute | solution.py:209
  368.2 48.5 %collective-permute-start.26 = (bf16[512,1536]{1,0:T(8,128)(2,1)}, bf16[512,1536]{1,0:T(8,128)(2,1)}, u32[]{:S(2)}, u32[]{:S(2)}) collective-permute-start(bf16[512,1536]{1,0:T(8,128)(2,1)} %get-tuple-element.113), channel_id=1, source_target_pairs={{0,8},{8,0},{16,24},{24,16},{1,9},{9,1},{17,25},{25,17},{2,10},{10... | collective-permute-start | bytes 4718600 | tf_op jit(solution)/shard_map/ppermute | solution.py:209
  409.9 53.8 %collective-permute-start.17 = (bf16[512,1536]{1,0:T(8,128)(2,1)}, bf16[512,1536]{1,0:T(8,128)(2,1)}, u32[]{:S(2)}, u32[]{:S(2)}) collective-permute-start(bf16[512,1536]{1,0:T(8,128)(2,1)} %get-tuple-element.116), channel_id=1, source_target_pairs={{0,8},{8,0},{16,24},{24,16},{1,9},{9,1},{17,25},{25,17},{2,10},{10... | collective-permute-start | bytes 4718600 | tf_op jit(solution)/shard_map/ppermute | solution.py:209
  421.3 37.6 %collective-permute-start.27 = (bf16[512,1536]{1,0:T(8,128)(2,1)}, bf16[512,1536]{1,0:T(8,128)(2,1)}, u32[]{:S(2)}, u32[]{:S(2)}) collective-permute-start(bf16[512,1536]{1,0:T(8,128)(2,1)} %add_convert_fusion.4), channel_id=1, source_target_pairs={{0,1},{1,0},{2,3},{3,2},{4,5},{5,4},{6,7},{7,6},{8,9},{9,8},{10,11... | collective-permute-start | bytes 4718600 | tf_op jit(solution)/shard_map/ppermute | solution.py:214
  425.2 66.1 %collective-permute-start.19 = (bf16[512,1536]{1,0:T(8,128)(2,1)}, bf16[512,1536]{1,0:T(8,128)(2,1)}, u32[]{:S(2)}, u32[]{:S(2)}) collective-permute-start(bf16[512,1536]{1,0:T(8,128)(2,1)} %add_convert_fusion.7), channel_id=1, source_target_pairs={{0,1},{1,0},{2,3},{3,2},{4,5},{5,4},{6,7},{7,6},{8,9},{9,8},{10,11... | collective-permute-start | bytes 4718600 | tf_op jit(solution)/shard_map/ppermute | solution.py:214
  432.3 224.3 %reduce-scatter.14.cloned.1.call-start = ((), (), s32[]{:S(2)}) async-start(), calls=%async_computation.11 | async-start | bytes 1327104 | tf_op jit(solution)/shard_map/reduce_scatter | solution.py:294
  462.1 34.6 %collective-permute-start.28 = (bf16[256,1536]{1,0:T(8,128)(2,1)S(1)}, bf16[256,1536]{1,0:T(8,128)(2,1)S(1)}, u32[]{:S(2)}, u32[]{:S(2)}) collective-permute-start(bf16[256,1536]{1,0:T(8,128)(2,1)S(1)} %split.99), channel_id=1, source_target_pairs={{0,16},{8,24},{16,0},{24,8},{1,17},{9,25},{17,1},{25,9},{2,18},{10... | collective-permute-start | bytes 2359304 | tf_op jit(solution)/shard_map/ppermute | solution.py:209
  540.0 152.1 %reduce-scatter.16.cloned.1.call-start = ((), (), s32[]{:S(2)}) async-start(), calls=%async_computation.12 | async-start | bytes 5898240 | tf_op jit(solution)/shard_map/reduce_scatter | solution.py:464
  569.1 211.1 %reduce-scatter.18.cloned.1.call-start = ((), (), s32[]{:S(2)}) async-start(), calls=%async_computation.13 | async-start | bytes 5898240 | tf_op jit(solution)/shard_map/reduce_scatter | solution.py:464
  597.7 258.2 %reduce-scatter.12.cloned.1.call-start = ((), (), s32[]{:S(2)}) async-start(), calls=%async_computation.10 | async-start | bytes 2654208 | tf_op jit(solution)/shard_map/reduce_scatter | solution.py:294
  649.9 20.3 %collective-permute-start.36 = (bf16[256,1536]{1,0:T(8,128)(2,1)}, bf16[256,1536]{1,0:T(8,128)(2,1)S(1)}, u32[]{:S(2)}, u32[]{:S(2)}) collective-permute-start(bf16[256,1536]{1,0:T(8,128)(2,1)} %split.109), channel_id=1, source_target_pairs={{0,16},{8,24},{16,0},{24,8},{1,17},{9,25},{17,1},{25,9},{2,18},{10... | collective-permute-start | bytes 2359304 | tf_op jit(solution)/shard_map/ppermute | solution.py:209
  694.5 90.4 %collective-permute-start.37 = (bf16[192,1536]{1,0:T(8,128)(2,1)}, bf16[192,1536]{1,0:T(8,128)(2,1)}, u32[]{:S(2)}, u32[]{:S(2)}) collective-permute-start(bf16[192,1536]{1,0:T(8,128)(2,1)} %get-tuple-element.151), channel_id=1, source_target_pairs={{0,0},{8,1},{2,2},{10,3},{4,4},{12,5},{6,6},{14,7},{1,8},{9,9},{3,... | collective-permute-start | bytes 1769480 | tf_op jit(solution)/shard_map/ppermute | solution.py:281
  700.4 84.5 %collective-permute-start.38 = (bf16[192,1536]{1,0:T(8,128)(2,1)}, bf16[192,1536]{1,0:T(8,128)(2,1)}, u32[]{:S(2)}, u32[]{:S(2)}) collective-permute-start(bf16[192,1536]{1,0:T(8,128)(2,1)} %get-tuple-element.152), channel_id=1, source_target_pairs={{8,0},{0,1},{10,2},{2,3},{12,4},{4,5},{14,6},{6,7},{9,8},{1,9},{11... | collective-permute-start | bytes 1769480 | tf_op jit(solution)/shard_map/ppermute | solution.py:281
  (101 other events, 1631.2 us)
Sparse Core Ops, SparseCore 0:
  14.0 68.3 all-gather.4
  83.9 87.8 all-gather.8
  173.5 87.8 all-gather.6
  263.4 48.9 all-gather.10
  432.5 47.1 reduce-scatter.19
  540.1 65.2 reduce-scatter.13
  607.7 84.2 reduce-scatter.15
  694.3 85.7 reduce-scatter.17
  784.2 71.6 reduce-scatter.11

commit v3 on v2

--- a/solution.py
+++ b/solution.py
@@ -16,7 +16,8 @@
 TOP = 8
 EXP_DEV = 5
 BLOCK = 256
-CHUNKS = ((0, 1), (2, 3), (4,))
+TILE = 512
+BANDS = 4
 MASKED = -1e30
 epsilon = 1e-06
 
@@ -204,6 +205,210 @@
     return jnp.concatenate([a * cosine - b * sine, b * cosine + a * sine], axis=1)
 
 
+def side_tiles(tiles):
+    return [(0, tiles // 2), (tiles // 2, tiles // 4), (3 * tiles // 4, tiles // 4)]
+
+
+def expert_kernel(start, n, half, tiles, band, has_in, parts, *refs):
+    refs = list(refs)
+    x_refs = refs[:3]
+    g_refs = refs[3:6]
+    wt_refs = refs[6:8]
+    w_ref = refs[8]
+    refs = refs[9:]
+    gin_in = refs.pop(0) if has_in else None
+    gin_refs, refs = refs[:parts], refs[parts:]
+    s_ref, gg_ref, dw_ref, xs, gs, ss, bs, sems = refs
+    step = pl.program_id(0)
+    later = step - tiles
+    m = 2 * n * half
+    arrivals = []
+    for side, (first, size) in enumerate(side_tiles(tiles)):
+        for i in range(size):
+            to = slice((first + i) * TILE, (first + i + 1) * TILE)
+            arrivals.append(
+                [
+                    pltpu.make_async_copy(
+                        sources[side].at[slice(i * TILE, (i + 1) * TILE), :],
+                        target.at[to, :],
+                        sems.at[k, first + i],
+                    )
+                    for k, (sources, target) in enumerate(((x_refs, xs), (g_refs, gs)))
+                ]
+            )
+
+    @pl.when(step == 0)
+    def _():
+        for pair in arrivals:
+            for copy in pair:
+                copy.start()
+
+    for i, pair in enumerate(arrivals):
+
+        @pl.when(step == i)
+        def _():
+            for copy in pair:
+                copy.wait()
+
+    @pl.when(step < tiles)
+    def _():
+        at = pl.ds(pl.multiple_of(step * TILE, TILE), TILE)
+        x = xs[at, :]
+        g = gs[at, :]
+        weights = jnp.where(step < tiles // 2, wt_refs[0][...], wt_refs[1][...]).T
+        sums = []
+        for i in range(n):
+            c = [slice((k * n + i) * half, (k * n + i + 1) * half) for k in range(3)]
+            gate = dot(x, w_ref[:, c[0]], 1, 0)
+            up = dot(x, w_ref[:, c[1]], 1, 0)
+            through = dot(g, w_ref[:, c[2]], 1, 0)
+            weight = weights[:, start + i : start + i + 1]
+            sig = jax.nn.sigmoid(gate)
+            soft = gate * sig
+            act = soft * up
+            sums.append(jnp.sum(act * through, axis=1, keepdims=True))
+            scaled = (weight * act).astype(jnp.bfloat16)
+            ss[at, c[0]] = scaled
+            s_ref[:, c[0]] = scaled
+            grad = weight * through
+            bs[at, c[0]] = (grad * up * sig * (1.0 + gate * (1.0 - sig))).astype(jnp.bfloat16)
+            bs[at, c[1]] = (grad * soft).astype(jnp.bfloat16)
+        gg_ref[...] = jnp.concatenate(sums, axis=1).T
+
+    @pl.when(later >= 0)
+    def _():
+        tile = tiles - 1 - later
+        at = pl.ds(pl.multiple_of(tile * TILE, TILE), TILE)
+        gin = dot(bs[at, :], w_ref[:, :m], 1, 1)
+        if has_in:
+            gin = gin + gin_in[...]
+        if parts == 1:
+            gin_refs[0][...] = gin
+        else:
+            for part in range(parts):
+
+                @pl.when(tile * parts // tiles == part)
+                def _():
+                    gin_refs[part][...] = gin.astype(jnp.bfloat16)
+
+    @pl.when((later >= 0) & (later < BANDS))
+    def _():
+        at = pl.ds(pl.multiple_of(later * band, band), band)
+        dw_ref[:, :m] = dot(xs[:, at], bs[...], 0, 0).astype(jnp.bfloat16)
+        dw_ref[:, m:] = dot(gs[:, at], ss[...], 0, 0).astype(jnp.bfloat16)
+
+
+def expert_chunk(xs, gs, wts, w, js, carried, last):
+    length, width = xs[0].shape
+    count = 2 * length
+    n = len(js)
+    half = w.shape[1] // (3 * n)
+    tiles = count // TILE
+    band = width // BANDS
+    parts = 4 if last else 1
+    sub = tiles // parts
+
+    def early(size):
+        return pl.BlockSpec((TILE, size), lambda i: (jnp.minimum(i, tiles - 1), 0))
+
+    weight_sides = [
+        pl.BlockSpec((EXP_DEV, TILE), lambda i, f=first: (0, jnp.clip(i - f, 0, tiles // 2 - 1)))
+        for first in (0, tiles // 2)
+    ]
+
+    def late(part):
+        return pl.BlockSpec(
+            (TILE, width),
+            lambda i: (jnp.clip(tiles - 1 - jnp.maximum(i - tiles, 0) - part * sub, 0, tiles // parts - 1), 0),
+        )
+
+    args = [*xs, *gs, *wts, w]
+    specs = [
+        *[pl.BlockSpec(memory_space=pl.ANY)] * 6,
+        *weight_sides,
+        pl.BlockSpec(w.shape, lambda i: (0, 0), pipeline_mode=pl.Buffered(1)),
+    ]
+    if carried is not None:
+        args.append(carried)
+        specs.append(
+            pl.BlockSpec((TILE, width), lambda i: (tiles - 1 - jnp.maximum(i - tiles, 0), 0))
+        )
+    out = pl.pallas_call(
+        functools.partial(expert_kernel, js[0], n, half, tiles, band, carried is not None, parts),
+        grid=(2 * tiles,),
+        in_specs=specs,
+        out_specs=[
+            *[late(part) for part in range(parts)],
+            early(n * half),
+            pl.BlockSpec((n, TILE), lambda i: (0, jnp.minimum(i, tiles - 1))),
+            pl.BlockSpec((band, w.shape[1]), lambda i: (jnp.clip(i - tiles, 0, BANDS - 1), 0)),
+        ],
+        out_shape=[
+            *[
+                jax.ShapeDtypeStruct((count // parts, width), jnp.bfloat16 if last else jnp.float32)
+                for _ in range(parts)
+            ],
+            jax.ShapeDtypeStruct((count, n * half), jnp.bfloat16),
+            jax.ShapeDtypeStruct((n, count), jnp.float32),
+            jax.ShapeDtypeStruct(w.shape, jnp.bfloat16),
+        ],
+        scratch_shapes=[
+            pltpu.VMEM((count, width), jnp.bfloat16),
+            pltpu.VMEM((count, width), jnp.bfloat16),
+            pltpu.VMEM((count, n * half), jnp.bfloat16),
+            pltpu.VMEM((count, 2 * n * half), jnp.bfloat16),
+            pltpu.SemaphoreType.DMA((2, tiles)),
+        ],
+        compiler_params=pltpu.CompilerParams(vmem_limit_bytes=60 * 1024 * 1024),
+        cost_estimate=pl.CostEstimate(
+            flops=10 * count * n * half * width,
+            bytes_accessed=8 * count * width + 4 * width * n * half * 3,
+            transcendentals=count * n * half,
+        ),
+        name="experts",
+    )(*args)
+    return (out[:parts] if last else out[0]), *out[parts:]
+
+
+def mix_kernel(n, parts, *refs):
+    refs = refs[: 2 * n] + refs[2 * n + 1 :]
+    total = dot(refs[0][...], refs[n][...], 1, 1)
+    for i in range(1, n):
+        total = total + dot(refs[i][...], refs[n + i][...], 1, 1)
+    step, steps = pl.program_id(0), pl.num_programs(0)
+    for part in range(parts):
+
+        @pl.when((steps - 1 - step) * parts // steps == part)
+        def _():
+            refs[2 * n + part][...] = total.astype(jnp.bfloat16)
+
+
+def mix_experts(scaled, weights, behind):
+    count, width = scaled[0].shape[0], weights[0].shape[0]
+    n, parts, steps = len(scaled), 4, count // TILE
+    sub = steps // parts
+
+    def late(part):
+        return pl.BlockSpec((TILE, width), lambda i: (jnp.clip(steps - 1 - i - part * sub, 0, sub - 1), 0))
+
+    return pl.pallas_call(
+        functools.partial(mix_kernel, n, parts),
+        grid=(steps,),
+        in_specs=[pl.BlockSpec((TILE, s.shape[1]), lambda i: (steps - 1 - i, 0)) for s in scaled]
+        + [pl.BlockSpec((width, s.shape[1]), lambda i: (0, 2)) for s in scaled]
+        + [pl.BlockSpec(memory_space=pl.ANY)],
+        out_specs=[late(part) for part in range(parts)],
+        out_shape=[jax.ShapeDtypeStruct((count // parts, width), jnp.bfloat16) for _ in range(parts)],
+        compiler_params=pltpu.CompilerParams(vmem_limit_bytes=60 * 1024 * 1024),
+        cost_estimate=pl.CostEstimate(
+            flops=2 * count * width * sum(s.shape[1] for s in scaled),
+            bytes_accessed=4 * count * width,
+            transcendentals=0,
+        ),
+        name="mix_experts",
+    )(*scaled, *weights, behind)
+
+
 def swap_member(v, bit):
     n = lax.axis_size("expert")
     return lax.ppermute(v, "expert", [(i, i ^ bit) for i in range(n)])
@@ -214,9 +419,20 @@
     return lax.ppermute(v, "shard", [(i, i ^ 1) for i in range(n)])
 
 
+def after(v, behind):
+    return pl.pallas_call(
+        lambda *refs: None,
+        in_specs=[pl.BlockSpec(memory_space=pl.ANY)] * 2,
+        out_specs=pl.BlockSpec(memory_space=pl.ANY),
+        out_shape=jax.ShapeDtypeStruct(v.shape, v.dtype),
+        input_output_aliases={0: 0},
+        name="after",
+    )(v, behind)
+
+
 def swap_sequence(v):
     got = swap_shard(v[: v.shape[0] // 2])
-    return jnp.concatenate([got, swap_member(got, 1)], axis=0)
+    return [got, swap_member(got, 1)]
 
 
 def chip_bits():
@@ -249,18 +465,24 @@
     return keep.astype(jnp.float32) + swap(sent).astype(jnp.float32)
 
 
-def scatter_members(own, other, axis=0):
-    kind = own.dtype
-    parts = []
-    for v in (own, other):
+def scatter_chip(v, axis):
+    for bit in reversed(chip_bits()):
         keep, sent = halves(v, axis)
-        parts.append(add_swapped(keep, sent, lambda u: swap_member(u, 1)).astype(kind))
-    own, other = parts
-    total = add_swapped(own, other, swap_shard)
-    for bit in reversed(chip_bits()):
-        keep, sent = halves(total.astype(kind), axis)
-        total = add_swapped(keep, sent, lambda u: swap_member(u, bit))
-    return total
+        v = add_swapped(keep, sent, lambda u: swap_member(u, bit)).astype(v.dtype)
+    return v
+
+
+def scatter_members(parts, axis=0):
+    kind = parts[0].dtype
+    other = add_swapped(parts[2], parts[3], lambda u: swap_member(u, 1)).astype(kind)
+    own = add_swapped(parts[0], parts[1], lambda u: swap_member(u, 1)).astype(kind)
+    if axis == 1:
+        return scatter_chip(add_swapped(own, other, swap_shard), axis)
+    cut = own.shape[1] // 2
+    one = scatter_chip(add_swapped(own[:, :cut], other[:, :cut], swap_shard).astype(kind), 0)
+    two, two_other = scatter_chip(own[:, cut:], 0), scatter_chip(other[:, cut:], 0)
+    two = add_swapped(two, two_other, swap_shard)
+    return jnp.concatenate([one.astype(jnp.float32), two], axis=1)
 
 
 def turn(first, back=False):
@@ -284,6 +506,59 @@
 def shard_lines():
     n = lax.axis_size("shard")
     return [[s for s in range(n) if s & 1 == low] for low in range(2)]
+
+
+def ring():
+    n = lax.axis_size("shard")
+    wide = n // 4
+    walk = [(z, 0) for z in range(4)]
+    for i, z in enumerate(reversed(range(4))):
+        ys = range(1, wide)
+        walk += [(z, y) for y in (ys if i % 2 == 0 else reversed(ys))]
+    return [z * wide + y for z, y in walk]
+
+
+def ring_step(v, by):
+    walk = ring()
+    n = len(walk)
+    return lax.ppermute(v, "shard", [(walk[i], walk[(i + by) % n]) for i in range(n)])
+
+
+def place_kernel(n, owner_ref, *refs):
+    size = refs[0].shape[0]
+    for i in range(n):
+        refs[n][pl.ds(pl.multiple_of(owner_ref[i] * size, 16), size), :] = refs[i][...]
+
+
+def ring_gather(v):
+    n = lax.axis_size("shard")
+    walk = ring()
+    place = [walk.index(i) for i in range(n)]
+    here = jnp.asarray(place, jnp.int32)[lax.axis_index("shard")]
+    pieces, offsets = [v], [0]
+    forth = back = v
+    for k in range(1, n // 2 + 1):
+        forth = ring_step(forth, 1)
+        pieces.append(forth)
+        offsets.append(-k)
+        if k < n // 2:
+            back = ring_step(back, -1)
+            pieces.append(back)
+            offsets.append(k)
+    owners = jnp.asarray(walk, jnp.int32)[(here + jnp.asarray(offsets, jnp.int32)) % n]
+    rows, size = v.shape
+    return pl.pallas_call(
+        functools.partial(place_kernel, n),
+        grid_spec=pltpu.PrefetchScalarGridSpec(
+            num_scalar_prefetch=1,
+            grid=(1,),
+            in_specs=[pl.BlockSpec((rows, size), lambda i, o: (0, 0))] * n,
+            out_specs=pl.BlockSpec((rows * n, size), lambda i, o: (0, 0)),
+        ),
+        out_shape=jax.ShapeDtypeStruct((rows * n, size), v.dtype),
+        compiler_params=pltpu.CompilerParams(vmem_limit_bytes=48 * 1024 * 1024),
+        name="place",
+    )(owners, *pieces)
 
 
 def gather_shard(v):
@@ -349,6 +624,8 @@
     heads, kv_heads = q_cols // HEAD_SIZE, k_cols // HEAD_SIZE
     out_rows = width // (members * shards)
     half = FF // 2
+    step = 2 if length <= 1024 else 1
+    chunks = [tuple(range(i, min(i + step, EXP_DEV))) for i in range(0, EXP_DEV, step)]
     me_ref = me[None].astype(jnp.int32)
 
     def cols(w, n):
@@ -361,29 +638,28 @@
             cols(w_query, q_cols),
             cols(key_weight, k_cols),
             cols(value_weight, k_cols),
-            cols(w_out, q_cols),
             jnp.pad(small, ((0, 0), (0, 128 - small.shape[1]))),
         ],
         axis=1,
     )
     first = gather_shard(first)
     full_qkv = first[:, :total_cols]
-    out_slice = first[:, total_cols : total_cols + q_cols]
-    full_small = first[:, total_cols + q_cols :]
+    full_small = first[:, total_cols:]
     full_router = full_small[:, :experts]
     gain_one = full_small[:, experts].astype(f32)
     gain_two = full_small[:, experts + 1].astype(f32)
 
     all_tokens = gather_members(tokens[0])
-    meta = gather_members(jnp.concatenate([segment_ids[0][:, None], routes[0]], axis=1))
-    seg = meta[:, 0]
-    my_routes = meta[:, 1:]
-    route_ids = jnp.concatenate([my_routes, swap_shard(my_routes)], axis=0)
-    my_grad = gather_members(cotangent[0])
-    all_grad = jnp.concatenate([my_grad, swap_sequence(my_grad)], axis=0)
+    meta = jnp.concatenate([segment_ids, routes[0].T], axis=0)
+    meta = gather_members(meta, axis=1)
+    seg = meta[0]
+    my_routes = meta[1:]
+    my_grad = gather_members(after(cotangent[0], all_tokens))
+    all_grad = [my_grad, *swap_sequence(my_grad)]
+    out_slice = ring_gather(after(cols(w_out, q_cols), all_tokens))
 
     weights = []
-    for js in CHUNKS:
+    for js in chunks:
         sides = [
             jnp.concatenate(
                 [w_gate_up[:, j, h * half : (h + 1) * half] for j in js]
@@ -422,63 +698,45 @@
     hidden = inputs + dot(attended_all, full_out, 0, 0)
     normed_two = hidden * inverse_rms(hidden)
     my_xn_two = (normed_two * gain_two).astype(bf16)
-    xn_two = jnp.concatenate([my_xn_two, swap_sequence(my_xn_two)], axis=0)
-
-    logits = jnp.dot(xn_two, full_router, preferred_element_type=f32)
+    xn_two = [my_xn_two, *swap_sequence(my_xn_two)]
+
+    logits = dot(full_router, my_xn_two, 0, 1)
     named = jnp.any(
-        route_ids[:, :, None] == jnp.arange(experts, dtype=jnp.int32)[None, None, :], axis=1
+        my_routes[:, None, :] == jnp.arange(experts, dtype=jnp.int32)[None, :, None], axis=0
     )
-    peak = jnp.max(jnp.where(named, logits, -jnp.inf), axis=1, keepdims=True)
+    peak = jnp.max(jnp.where(named, logits, -jnp.inf), axis=0, keepdims=True)
     exps = jnp.where(named, jnp.exp(jnp.minimum(logits - peak, 0.0)), 0.0)
-    gates = exps / jnp.sum(exps, axis=1, keepdims=True)
+    gates = exps / jnp.sum(exps, axis=0, keepdims=True)
     group = (me & ~1) | low
-    my_gates = lax.dynamic_slice_in_dim(gates, group * EXP_DEV, EXP_DEV, axis=1)
+    my_gates = [
+        lax.dynamic_slice_in_dim(v, group * EXP_DEV, EXP_DEV, axis=0)
+        for v in (gates, swap_shard(gates))
+    ]
 
     count = 2 * length
-    mix = jnp.zeros((count, width), f32)
-    grad_in = jnp.zeros((count, width), f32)
-    gate_grads, expert_grads = [], []
-    for js, w in zip(CHUNKS, weights):
-        n = len(js) * half
-        w_in, w_back = w[:, : 2 * n], w[:, 2 * n :]
-        gate_up = dot(xn_two, w_in, 1, 0)
-        through = dot(all_grad, w_back, 1, 0)
-        gate, up = gate_up[:, :n], gate_up[:, n:]
-        weight = jnp.concatenate(
-            [jnp.broadcast_to(my_gates[:, j : j + 1], (count, half)) for j in js], axis=1
+    grad_in = None
+    gate_grads, expert_grads, scaled = [], [], []
+    for js, w in zip(chunks, weights):
+        grad_in, s, gg, grads = expert_chunk(
+            xn_two, all_grad, my_gates, w, js, grad_in, js is chunks[-1]
         )
-        sig = jax.nn.sigmoid(gate)
-        act = gate * sig * up
-        product = act * through
-        for i in range(len(js)):
-            gate_grads.append(jnp.sum(product[:, i * half : (i + 1) * half], axis=1))
-        scaled = (weight * act).astype(bf16)
-        grad_act = weight * through
-        back = jnp.concatenate(
-            [grad_act * up * sig * (1.0 + gate * (1.0 - sig)), grad_act * gate * sig], axis=1
-        ).astype(bf16)
-        mix = mix + dot(scaled, w_back, 1, 1)
-        grad_in = grad_in + dot(back, w_in, 1, 1)
-        grads = jnp.concatenate([dot(xn_two, back, 0, 0), dot(all_grad, scaled, 0, 0)], axis=1)
+        scaled.append(s)
+        gate_grads.append(gg)
         expert_grads.append(
             lax.psum_scatter(
-                grads.astype(bf16),
-                "shard",
-                scatter_dimension=0,
-                tiled=True,
-                axis_index_groups=shard_lines(),
+                grads, "shard", scatter_dimension=0, tiled=True, axis_index_groups=shard_lines()
             )
         )
 
-    grad_xn_two = scatter_members(grad_in[:length].astype(bf16), grad_in[length:].astype(bf16))
-    gate_grads = lax.dynamic_update_slice_in_dim(
-        jnp.zeros((experts, count), f32), jnp.stack(gate_grads, axis=0), group * EXP_DEV, axis=0
-    )
-    grad_gates = scatter_members(gate_grads[:, :length], gate_grads[:, length:], axis=1).T
-    own_gates = gates[:rows]
-    grad_chosen = own_gates * (grad_gates - jnp.sum(own_gates * grad_gates, axis=1, keepdims=True))
+    grad_xn_two = scatter_members(grad_in)
+    gate_grads = jnp.tile(jnp.concatenate(gate_grads, axis=0), (members, 1))
+    mine = jnp.arange(experts, dtype=jnp.int32)[:, None] // EXP_DEV == group
+    gate_grads = jnp.where(mine, gate_grads, 0.0)
+    grad_gates = scatter_members(jnp.split(gate_grads, 4, axis=1), axis=1)
+    own_gates = gates[:, :rows]
+    grad_chosen = own_gates * (grad_gates - jnp.sum(own_gates * grad_gates, axis=0, keepdims=True))
     grad_logits = grad_chosen.astype(bf16)
-    grad_xn_two = grad_xn_two + dot(grad_logits, full_router, 1, 1)
+    grad_xn_two = grad_xn_two + dot(grad_logits, full_router, 0, 1)
     my_hidden = hidden[:rows]
 
     my_scale = inverse_rms(my_hidden)
@@ -492,8 +750,7 @@
     grad_attended = dot(full_out[:q_cols], grad_attn, 1, 1).astype(bf16)
     grad_attended = grad_attended.reshape(heads, HEAD_SIZE, length)
     grad_out = jnp.dot(attended_rows, grad_attn, preferred_element_type=f32)
-    out_grads = scatter_shard(grad_out.astype(bf16)).astype(f32)
-    grad_router = dot(xn_two[:rows], grad_logits, 0, 0)
+    grad_router = dot(my_xn_two[:rows], grad_logits, 0, 1)
 
     dq, dk, dv = attention_backward(me_ref, queries, keys, values, attended, grad_attended, lse, seg)
     dq = rotate(dq, cosine, -sine) * HEAD_SIZE**-0.5
@@ -516,15 +773,24 @@
     rest = jnp.pad(rest, ((0, 0), (0, 128 - rest.shape[1])))
     grad_first = jnp.concatenate([grad_first, rest], axis=1).astype(bf16)
     grad_first = jnp.transpose(grad_first.reshape(members, shards, out_rows, -1), (1, 0, 2, 3))
+    grad_out = jnp.transpose(
+        grad_out.astype(bf16).reshape(shards, out_rows, members, q_cols), (0, 2, 1, 3)
+    )
+    grad_first = jnp.concatenate([grad_first, grad_out], axis=3)
     grad_first = scatter_shard(grad_first.reshape(width, -1)).reshape(members, out_rows, -1)
+    out_grads = jnp.transpose(grad_first[:, :, total_cols + 128 :], (1, 0, 2)).astype(f32)
+    grad_first = grad_first[:, :, : total_cols + 128]
     grad_first = lax.all_to_all(grad_first, "expert", split_axis=0, concat_axis=0, tiled=True)
     rest = jnp.sum(grad_first[:, :, total_cols:].astype(f32), axis=0)
     grad_first = jnp.transpose(grad_first, (1, 0, 2)).astype(f32)
 
-    mixed = my_hidden + scatter_members(mix[:length].astype(bf16), mix[length:].astype(bf16))
+    mixed = my_hidden + scatter_members(mix_experts(scaled, weights, grad_attn))
 
     gate_up_out, down_out = [], []
-    for js, v in zip(CHUNKS, expert_grads):
+    one = None
+    for js, v in zip(chunks, expert_grads):
+        if one is not None:
+            v, one = lax.optimization_barrier((v, one))
         size = v.shape[0] // 2
         one = permute_all(jnp.where(core == 0, v[:size], v[size:]), turn(True, True))
         two = permute_all(jnp.where(core == 0, v[size:], v[:size]), turn(False, True))
@@ -544,7 +810,7 @@
         grad_first[:, :, :q_cols].reshape(out_rows, -1),
         grad_first[:, :, q_cols : q_cols + k_cols].reshape(out_rows, -1),
         grad_first[:, :, q_cols + k_cols : total_cols].reshape(out_rows, -1),
-        out_grads,
+        out_grads.reshape(out_rows, -1),
         rest[:, experts + 1],
         rest[:, :experts],
         jnp.stack(gate_up_out, axis=1).astype(f32),

time: 886 us -> 676 us (0.76)
  matrix products: 224 us -> 31.6 us
  waiting for transfers between devices: 398 us -> 247 us
  Pallas kernels: 36.7 us -> 154 us
  starting transfers between devices: 55.8 us -> 101 us
  local copies, waits for them, and re-layouts: 73.7 us -> 45.7 us
    dot_general x25 -> x8, matrix products: 215 us -> 27.5 us  [dot(): lax.dot_general(a, b, (((ca,), (cb,)), ((), ())), preferred_element_type=...]
    pallas_call x0 -> x7, Pallas kernels: none -> 117 us  [the longest x3 101 us: expert_chunk(): pl.pallas_call(functools.partial(expert_kernel, js[0], n, half, tiles, ba...]
    reduce_scatter x3, waiting for transfers between devices: 99.5 us -> 0.02 us  [body(): lax.psum_scatter(grads, 'shard', scatter_dimension=0, tiled=True, axis_in...]
    ppermute x6 -> x8, waiting for transfers between devices: 92.7 us -> 23 us  [swap_shard(): return lax.ppermute(v, 'shard', [(i, i ^ 1) for i in range(n)])]
    reduce_scatter x2 -> x1, waiting for transfers between devices: 52.8 us -> 14.8 us  [scatter_shard(): return lax.psum_scatter(v, 'shard', scatter_dimension=0, tiled=True)]
    ppermute x12, waiting for transfers between devices: 44.7 us -> 80.8 us  [permute_all(): return lax.ppermute(v, ('expert', 'shard'), pairs)]
    unnamed x182 -> x140, local copies, waits for them, and re-layouts: 43 us -> 14.9 us
    ppermute x0 -> x7, waiting for transfers between devices: none -> 24.2 us  [ring_step(): lax.ppermute(v, 'shard', [(walk[i], walk[(i + by) % n]) for i in range(n)])]
  transfers between devices with their start and end apart: 53 -> 65, of which waited for: 21 -> 30; matrix products, arithmetic and copies ran while one was open for 38% -> 19% of each run, Pallas kernels for 4% -> 23%
where the time goes in v3:
time: 676 us; the launch traced here: 667 us
  waiting for transfers between devices  247 us (37%)
  Pallas kernels  154 us (23%)
  starting transfers between devices  101 us (15%)
  other arithmetic  71.2 us (11%)
  local copies, waits for them, and re-layouts  45.7 us (7%)
  matrix products  31.6 us (5%)
  between operations  16.1 us (2%)
    pallas_call x3, Pallas kernels, expert_chunk(): pl.pallas_call(functools.partial(expert_kernel, js[0], n, half, tiles, ba...  101 us
    ppermute x29, waiting for transfers between devices, swap_member(): return lax.ppermute(v, 'expert', [(i, i ^ bit) for i in range(n)])  99.8 us
    ppermute x12, waiting for transfers between devices, permute_all(): return lax.ppermute(v, ('expert', 'shard'), pairs)  80.8 us
    ppermute x12, starting transfers between devices, permute_all(): return lax.ppermute(v, ('expert', 'shard'), pairs)  52.5 us
    dot_general x8, matrix products, dot(): lax.dot_general(a, b, (((ca,), (cb,)), ((), ())), preferred_element_type=...  27.5 us
    ppermute x7, waiting for transfers between devices, ring_step(): lax.ppermute(v, 'shard', [(walk[i], walk[(i + by) % n]) for i in range(n)])  24.2 us
    ppermute x8, waiting for transfers between devices, swap_shard(): return lax.ppermute(v, 'shard', [(i, i ^ 1) for i in range(n)])  23 us
    ppermute x29, starting transfers between devices, swap_member(): return lax.ppermute(v, 'expert', [(i, i ^ bit) for i in range(n)])  20.9 us
  transfers between devices with their start and end apart: 65, of which 30 were waited for; matrix products, arithmetic and copies ran while one was open for 19% of the time, Pallas kernels for 23%

profile of v3, /device:TPU:0, one launch (start us, length us, event | category | flops | bytes accessed | tf_op | source)
XLA Modules:
  0.0 667.0 jit_solution(13565887258717054047)
XLA Ops:
  20.7 17.2 %collective-permute-done.23 = bf16[192,1536]{1,0:T(8,128)(2,1)S(1)} collective-permute-done((bf16[192,1536]{1,0:T(8,128)(2,1)S(1)}, bf16[192,1536]{1,0:T(8,128)(2,1)S(1)}, u32[]{:S(2)}, u32[]{:S(2)}) %collective-permute-start.23) | collective-permute-done | bytes 589856 | tf_op jit(solution)/shard_map/ppermute | solution.py:503
  41.0 17.0 %collective-permute-done = bf16[256,1536]{1,0:T(8,128)(2,1)S(1)} collective-permute-done((bf16[256,1536]{1,0:T(8,128)(2,1)S(1)}, bf16[256,1536]{1,0:T(8,128)(2,1)S(1)}, u32[]{:S(2)}, u32[]{:S(2)}) %collective-permute-start) | collective-permute-done | bytes 786464 | tf_op jit(solution)/shard_map/ppermute | solution.py:414
  61.9 5.9 collective-permute-start.24
  76.5 6.7 %collective-permute-done.6.refs_1_ = bf16[192,384]{1,0:T(8,128)(2,1)S(1)} collective-permute-done((bf16[192,384]{1,0:T(8,128)(2,1)}, bf16[192,384]{1,0:T(8,128)(2,1)S(1)}, u32[]{:S(2)}, u32[]{:S(2)}) %collective-permute-start.6) | collective-permute-done | bytes 147488 | tf_op jit(solution)/shard_map/ppermute | solution.py:524
  90.1 6.7 %collective-permute-start.10 = (bf16[192,384]{1,0:T(8,128)(2,1)S(1)}, bf16[192,384]{1,0:T(8,128)(2,1)S(1)}, u32[]{:S(2)}, u32[]{:S(2)}) collective-permute-start(bf16[192,384]{1,0:T(8,128)(2,1)S(1)} %collective-permute-done.8.refs_3_), channel_id=1, source_target_pairs={{0,2},{2,4},{4,6},{6,7},{7,5},{5,3},{3,1},{1,0},{8,10},{10,12},{12... | collective-permute-start | bytes 442376 | tf_op jit(solution)/shard_map/ppermute | solution.py:524
  103.7 7.1 %collective-permute-start.12 = (bf16[192,384]{1,0:T(8,128)(2,1)S(1)}, bf16[192,384]{1,0:T(8,128)(2,1)S(1)}, u32[]{:S(2)}, u32[]{:S(2)}) collective-permute-start(bf16[192,384]{1,0:T(8,128)(2,1)S(1)} %collective-permute-done.10.refs_5_), channel_id=1, source_target_pairs={{0,2},{2,4},{4,6},{6,7},{7,5},{5,3},{3,1},{1,0},{8,10},{10,12},{12... | collective-permute-start | bytes 442376 | tf_op jit(solution)/shard_map/ppermute | solution.py:524
  110.8 6.2 collective-permute-done.11.refs_6_
  120.4 4.9 fusion.22
  127.1 17.6 %attention_forward.1 = (bf16[6,64,1024]{2,1,0:T(8,128)(2,1)S(1)}, f32[6,1,1024]{2,1,0:T(1,128)S(1)}) custom-call(s32[1]{0:T(128)} %bitcast.1.me_ref, bf16[6,64,1024]{2,1,0:T(8,128)(2,1)S(1)} %fusion.35.q_ref, bf16[2,64,1024]{2,1,0:T(8,128)(2,1)S(1)} %pad_maximum_fusion.14.k_ref, bf16[2,64,1024]{2,1,0:T(8,128)(2,1)S(1)} %bitcast.179, ...), custom_call_target="tpu_custom_call" | custom-call | flops 1610612736 | bytes 2359296 | tf_op jit(solution)/shard_map/attention_forward/pallas_call | solution.py:84
  152.4 8.9 %collective-permute-done.4 = bf16[384,1024]{1,0:T(8,128)(2,1)} collective-permute-done((bf16[384,1024]{1,0:T(8,128)(2,1)S(1)}, bf16[384,1024]{1,0:T(8,128)(2,1)}, u32[]{:S(2)}, u32[]{:S(2)}) %collective-permute-start.4) | collective-permute-done | bytes 786464 | tf_op jit(solution)/shard_map/ppermute | solution.py:414
  167.2 18.5 %collective-permute-done.17 = bf16[256,1536]{1,0:T(8,128)(2,1)S(1)} collective-permute-done((bf16[256,1536]{1,0:T(8,128)(2,1)}, bf16[256,1536]{1,0:T(8,128)(2,1)S(1)}, u32[]{:S(2)}, u32[]{:S(2)}) %collective-permute-start.17) | collective-permute-done | bytes 786464 | tf_op jit(solution)/shard_map/ppermute | solution.py:414
  197.9 5.9 multiply_reduce_fusion
  213.4 51.4 %collective-permute-done.27 = bf16[192,768]{1,0:T(8,128)(2,1)S(1)} collective-permute-done((bf16[192,768]{1,0:T(8,128)(2,1)S(1)}, bf16[192,768]{1,0:T(8,128)(2,1)S(1)}, u32[]{:S(2)}, u32[]{:S(2)}) %collective-permute-start.27) | collective-permute-done | bytes 294944 | tf_op jit(solution)/shard_map/ppermute | solution.py:503
  278.0 37.5 %experts.3 = (f32[2048,1536]{1,0:T(8,128)}, bf16[2048,512]{1,0:T(8,128)(2,1)}, f32[2,2048]{1,0:T(2,128)}, bf16[1536,1536]{1,0:T(8,128)(2,1)}) custom-call(bf16[1024,1536]{1,0:T(8,128)(2,1)} %copy-done.14, bf16[512,1536]{1,0:T(8,128)(2,1)} %collective-permute-done.15.refs_1_, bf16[512,1536]{1,0:T(8,128)(2,1)} %collective-permute-done.16.refs_2_, ...), custom_call_target="tpu_custom_call" | custom-call | flops 16106127360 | bytes 34603008 | tf_op jit(solution)/shard_map/experts/pallas_call | solution.py:336
  316.1 38.4 %experts.4 = (f32[2048,1536]{1,0:T(8,128)}, bf16[2048,512]{1,0:T(8,128)(2,1)}, f32[2,2048]{1,0:T(2,128)}, bf16[1536,1536]{1,0:T(8,128)(2,1)}) custom-call(bf16[1024,1536]{1,0:T(8,128)(2,1)} %copy-done.14, bf16[512,1536]{1,0:T(8,128)(2,1)} %collective-permute-done.15.refs_1_, bf16[512,1536]{1,0:T(8,128)(2,1)} %collective-permute-done.16.refs_2_, ...), custom_call_target="tpu_custom_call" | custom-call | flops 16106127360 | bytes 34603008 | tf_op jit(solution)/shard_map/experts/pallas_call | solution.py:336
  354.8 25.5 %experts.5 = (bf16[512,1536]{1,0:T(8,128)(2,1)}, bf16[512,1536]{1,0:T(8,128)(2,1)}, bf16[512,1536]{1,0:T(8,128)(2,1)}, bf16[512,1536]{1,0:T(8,128)(2,1)}, bf16[2...) custom-call(bf16[1024,1536]{1,0:T(8,128)(2,1)} %copy-done.14, ...), custom_call_target="tpu_custom_call" | custom-call | flops 8053063680 | bytes 29884416 | tf_op jit(solution)/shard_map/experts/pallas_call | solution.py:336
  396.9 9.5 %collective-permute-done.33 = bf16[256,768]{1,0:T(8,128)(2,1)S(1)} collective-permute-done((bf16[256,768]{1,0:T(8,128)(2,1)S(1)}, bf16[256,768]{1,0:T(8,128)(2,1)S(1)}, u32[]{:S(2)}, u32[]{:S(2)}) %collective-permute-start.33) | collective-permute-done | bytes 393248 | tf_op jit(solution)/shard_map/ppermute | solution.py:414
  408.4 6.2 collective-permute-done.30
  427.5 13.7 %collective-permute-done.39 = bf16[256,1536]{1,0:T(8,128)(2,1)S(1)} collective-permute-done((bf16[256,1536]{1,0:T(8,128)(2,1)S(1)}, bf16[256,1536]{1,0:T(8,128)(2,1)S(1)}, u32[]{:S(2)}, u32[]{:S(2)}) %collective-permute-start.39) | collective-permute-done | bytes 786464 | tf_op jit(solution)/shard_map/ppermute | solution.py:414
  450.0 15.8 %attention_backward.1 = (f32[6,64,1024]{2,1,0:T(8,128)S(1)}, f32[2,64,1024]{2,1,0:T(8,128)S(1)}, f32[2,64,1024]{2,1,0:T(8,128)S(1)}) custom-call(s32[1]{0:T(128)} %bitcast.1.me_ref, bf16[6,64,1024]{2,1,0:T(8,128)(2,1)S(1)} %fusion.35.q_ref, bf16[2,64,1024]{2,1,0:T(8,128)(2,1)S(1)} %copy-done.7, bf16[2,64,1024]{2,1,0:T(8,128)(2,1)S(1)} %bitcast.180, ...), custom_call_target="tpu_custom_call" | custom-call | flops 4026531840 | bytes 6291456 | tf_op jit(solution)/shard_map/attention_backward/pallas_call | solution.py:159
  469.2 5.3 fusion.3
  477.8 15.1 %mix_experts.1 = (bf16[512,1536]{1,0:T(8,128)(2,1)}, bf16[512,1536]{1,0:T(8,128)(2,1)}, bf16[512,1536]{1,0:T(8,128)(2,1)}, bf16[512,1536]{1,0:T(8,128)(2,1)}) custom-call(bf16[2048,512]{1,0:T(8,128)(2,1)} %get-tuple-element.38.refs_0_, bf16[2048,512]{1,0:T(8,128)(2,1)} %get-tuple-element.40.refs_1_, bf16[2048,256]{1,0:T(8,128)(2,1)} %get-tuple-element.42.refs_2_, ...), custom_call_target="tpu_custom_call" | custom-call | flops 8053063680 | bytes 12582912 | tf_op jit(solution)/shard_map/mix_experts/pallas_call | solution.py:394
  530.1 6.2 collective-permute-done.43
  538.2 6.7 %collective-permute-done.49 = bf16[256,1536]{1,0:T(8,128)(2,1)S(1)} collective-permute-done((bf16[256,1536]{1,0:T(8,128)(2,1)S(1)}, bf16[256,1536]{1,0:T(8,128)(2,1)S(1)}, u32[]{:S(2)}, u32[]{:S(2)}) %collective-permute-start.49) | collective-permute-done | bytes 786464 | tf_op jit(solution)/shard_map/ppermute | solution.py:414
  546.0 7.3 %collective-permute-done.45 = bf16[256,768]{1,0:T(8,128)(2,1)S(1)} collective-permute-done((bf16[256,768]{1,0:T(8,128)(2,1)S(1)}, bf16[256,768]{1,0:T(8,128)(2,1)S(1)}, u32[]{:S(2)}, u32[]{:S(2)}) %collective-permute-start.45) | collective-permute-done | bytes 393248 | tf_op jit(solution)/shard_map/ppermute | solution.py:414
  554.3 6.5 collective-permute-done.44
  574.3 5.9 collective-permute-start.52
  580.2 5.5 collective-permute-done.51
  587.0 6.4 collective-permute-start.53
  595.4 22.2 %collective-permute-start.55 = (bf16[192,768]{1,0:T(8,128)(2,1)S(1)}, bf16[192,768]{1,0:T(8,128)(2,1)S(1)}, u32[]{:S(2)}, u32[]{:S(2)}) collective-permute-start(bf16[192,768]{1,0:T(8,128)(2,1)S(1)} %get-tuple-element.194), channel_id=1, source_target_pairs={{8,0},{0,1},{10,2},{2,3},{12,4},{4,5},{14,6},{6,7},{9,8},{1,9},{11... | collective-permute-start | bytes 884744 | tf_op jit(solution)/shard_map/ppermute | solution.py:503
  619.2 6.7 %collective-permute-done.55 = bf16[192,768]{1,0:T(8,128)(2,1)S(1)} collective-permute-done((bf16[192,768]{1,0:T(8,128)(2,1)S(1)}, bf16[192,768]{1,0:T(8,128)(2,1)S(1)}, u32[]{:S(2)}, u32[]{:S(2)}) %collective-permute-start.55) | collective-permute-done | bytes 294944 | tf_op jit(solution)/shard_map/ppermute | solution.py:503
  629.9 14.8 %reduce-scatter.5.cloned.1.call-done = bf16[192,1152]{1,0:T(8,128)(2,1)} async-done(((bf16[1536,1152]{1,0:T(8,128)(2,1)}), bf16[192,1152]{1,0:T(8,128)(2,1)}) %reduce-scatter.5.cloned.1.call-update) | async-done | bytes 442384 | tf_op jit(solution)/shard_map/reduce_scatter | solution.py:569
  (413 shorter events, 221.6 us)
Async XLA Ops:
  7.2 111.5 %all-gather.5.cloned.1.call-start = ((), (), s32[]{:S(2)}) async-start(), calls=%async_computation.5 | async-start | bytes 2654208 | tf_op jit(solution)/shard_map/all_gather | solution.py:565
  13.5 264.5 %all-gather.7.cloned.1.call-start = ((), (), s32[]{:S(2)}) async-start(), calls=%async_computation.6 | async-start | bytes 5898240 | tf_op jit(solution)/shard_map/all_gather | solution.py:678
  16.4 21.5 %collective-permute-start.23 = (bf16[192,1536]{1,0:T(8,128)(2,1)S(1)}, bf16[192,1536]{1,0:T(8,128)(2,1)S(1)}, u32[]{:S(2)}, u32[]{:S(2)}) collective-permute-start(bf16[192,1536]{1,0:T(8,128)(2,1)S(1)} %get-tuple-element.150), channel_id=1, source_target_pairs={{0,8},{1,0},{2,10},{3,2},{4,12},{5,4},{6,14},{7,6},{8,9},{9,1},{10... | collective-permute-start | bytes 1769480 | tf_op jit(solution)/shard_map/ppermute | solution.py:503
  39.2 276.9 %all-gather.9.cloned.1.call-start = ((), (), s32[]{:S(2)}) async-start(), calls=%async_computation.7 | async-start | bytes 5898240 | tf_op jit(solution)/shard_map/all_gather | solution.py:678
  59.3 24.6 %collective-permute-start.2 = (s32[9,256]{1,0:T(8,128)S(1)}, s32[9,256]{1,0:T(8,128)S(1)}, u32[]{:S(2)}, u32[]{:S(2)}) collective-permute-start(s32[9,256]{1,0:T(8,128)S(1)} %pad_add_fusion.4), channel_id=1, source_target_pairs={{0,16},{8,24},{16,0},{24,8},{1,17},{9,25},{17,1},{25,9},{2,18},{10... | collective-permute-start | bytes 27656 | tf_op jit(solution)/shard_map/ppermute | solution.py:414
  61.9 84.8 %collective-permute-start.24 = (bf16[192,1536]{1,0:T(8,128)(2,1)}, bf16[192,1536]{1,0:T(8,128)(2,1)}, u32[]{:S(2)}, u32[]{:S(2)}) collective-permute-start(bf16[192,1536]{1,0:T(8,128)(2,1)} %get-tuple-element.145), channel_id=1, source_target_pairs={{0,0},{1,8},{2,2},{3,10},{4,4},{5,12},{6,6},{7,14},{8,1},{9,9},{10... | collective-permute-start | bytes 1769480 | tf_op jit(solution)/shard_map/ppermute | solution.py:503
  67.9 78.9 %collective-permute-start.25 = (bf16[192,1536]{1,0:T(8,128)(2,1)}, bf16[192,1536]{1,0:T(8,128)(2,1)}, u32[]{:S(2)}, u32[]{:S(2)}) collective-permute-start(bf16[192,1536]{1,0:T(8,128)(2,1)} %get-tuple-element.146), channel_id=1, source_target_pairs={{0,8},{1,0},{2,10},{3,2},{4,12},{5,4},{6,14},{7,6},{8,9},{9,1},{10... | collective-permute-start | bytes 1769480 | tf_op jit(solution)/shard_map/ppermute | solution.py:503
  118.6 30.9 %collective-permute-start.13 = (bf16[1,1536,384]{2,1,0:T(8,128)(2,1)S(1)}, bf16[1,1536,384]{2,1,0:T(8,128)(2,1)}, u32[]{:S(2)}, u32[]{:S(2)}) collective-permute-start(bf16[1,1536,384]{2,1,0:T(8,128)(2,1)S(1)} %bitcast.172), channel_id=1, source_target_pairs={{0,16},{8,24},{16,0},{24,8},{1,17},{9,25},{17,1},{25,9},{2,18},{10... | collective-permute-start | bytes 3538952 | tf_op jit(solution)/shard_map/ppermute | solution.py:414
  149.2 205.6 %all-gather.11.cloned.1.call-start = ((), (), s32[]{:S(2)}) async-start(), calls=%async_computation.8 | async-start | bytes 2949120 | tf_op jit(solution)/shard_map/all_gather | solution.py:678
  152.4 37.9 %collective-permute-start.14 = (bf16[2,1536,384]{2,1,0:T(8,128)(2,1)}, bf16[2,1536,384]{2,1,0:T(8,128)(2,1)}, u32[]{:S(2)}, u32[]{:S(2)}) collective-permute-start(bf16[2,1536,384]{2,1,0:T(8,128)(2,1)} %pad_maximum_fusion.5), channel_id=1, source_target_pairs={{0,8},{8,0},{16,24},{24,16},{1,9},{9,1},{17,25},{25,17},{2,10},{10... | collective-permute-start | bytes 7077896 | tf_op jit(solution)/shard_map/ppermute | solution.py:414
  164.7 24.2 %collective-permute-start.5 = (bf16[768,1024]{1,0:T(8,128)(2,1)}, bf16[768,1024]{1,0:T(8,128)(2,1)}, u32[]{:S(2)}, u32[]{:S(2)}) collective-permute-start(bf16[768,1024]{1,0:T(8,128)(2,1)} %maximum_maximum_fusion), channel_id=1, source_target_pairs={{0,8},{8,0},{16,24},{24,16},{1,9},{9,1},{17,25},{25,17},{2,10},{10... | collective-permute-start | bytes 4718600 | tf_op jit(solution)/shard_map/ppermute | solution.py:414
  165.5 20.2 %collective-permute-start.17 = (bf16[256,1536]{1,0:T(8,128)(2,1)}, bf16[256,1536]{1,0:T(8,128)(2,1)S(1)}, u32[]{:S(2)}, u32[]{:S(2)}) collective-permute-start(bf16[256,1536]{1,0:T(8,128)(2,1)} %after.3), channel_id=1, source_target_pairs={{0,16},{8,24},{16,0},{24,8},{1,17},{9,25},{17,1},{25,9},{2,18},{10... | collective-permute-start | bytes 2359304 | tf_op jit(solution)/shard_map/ppermute | solution.py:414
  188.4 77.6 %collective-permute-start.19 = (bf16[512,1536]{1,0:T(8,128)(2,1)}, bf16[512,1536]{1,0:T(8,128)(2,1)}, u32[]{:S(2)}, u32[]{:S(2)}) collective-permute-start(bf16[512,1536]{1,0:T(8,128)(2,1)} %pad_maximum_fusion.7), channel_id=1, source_target_pairs={{0,1},{1,0},{2,3},{3,2},{4,5},{5,4},{6,7},{7,6},{8,9},{9,8},{10,11... | collective-permute-start | bytes 4718600 | tf_op jit(solution)/shard_map/ppermute | solution.py:419
  207.7 58.4 %collective-permute-start.15 = (bf16[512,1536]{1,0:T(8,128)(2,1)}, bf16[512,1536]{1,0:T(8,128)(2,1)}, u32[]{:S(2)}, u32[]{:S(2)}) collective-permute-start(bf16[512,1536]{1,0:T(8,128)(2,1)} %slice.474), channel_id=1, source_target_pairs={{0,1},{1,0},{2,3},{3,2},{4,5},{5,4},{6,7},{7,6},{8,9},{9,8},{10,11... | collective-permute-start | bytes 4718600 | tf_op jit(solution)/shard_map/ppermute | solution.py:419
  210.5 56.4 %collective-permute-start.18 = (bf16[512,1536]{1,0:T(8,128)(2,1)}, bf16[512,1536]{1,0:T(8,128)(2,1)}, u32[]{:S(2)}, u32[]{:S(2)}) collective-permute-start(bf16[512,1536]{1,0:T(8,128)(2,1)} %pad_maximum_fusion.7), channel_id=1, source_target_pairs={{0,8},{8,0},{16,24},{24,16},{1,9},{9,1},{17,25},{25,17},{2,10},{10... | collective-permute-start | bytes 4718600 | tf_op jit(solution)/shard_map/ppermute | solution.py:414
  211.5 53.2 %collective-permute-start.27 = (bf16[192,768]{1,0:T(8,128)(2,1)S(1)}, bf16[192,768]{1,0:T(8,128)(2,1)S(1)}, u32[]{:S(2)}, u32[]{:S(2)}) collective-permute-start(bf16[192,768]{1,0:T(8,128)(2,1)S(1)} %get-tuple-element.200), channel_id=1, source_target_pairs={{0,8},{1,0},{2,10},{3,2},{4,12},{5,4},{6,14},{7,6},{8,9},{9,1},{10... | collective-permute-start | bytes 884744 | tf_op jit(solution)/shard_map/ppermute | solution.py:503
  265.7 296.1 %reduce-scatter.7.cloned.1.call-start = ((), (), s32[]{:S(2)}) async-start(), calls=%async_computation.10 | async-start | bytes 5898240 | tf_op jit(solution)/shard_map/reduce_scatter | solution.py:726
  315.6 256.4 %reduce-scatter.9.cloned.1.call-start = ((), (), s32[]{:S(2)}) async-start(), calls=%async_computation.11 | async-start | bytes 5898240 | tf_op jit(solution)/shard_map/reduce_scatter | solution.py:726
  354.6 239.0 %reduce-scatter.11.cloned.1.call-start = ((), (), s32[]{:S(2)}) async-start(), calls=%async_computation.12 | async-start | bytes 2949120 | tf_op jit(solution)/shard_map/reduce_scatter | solution.py:726
  394.1 20.5 %collective-permute-start.30 = (bf16[512,768]{1,0:T(8,128)(2,1)S(1)}, bf16[512,768]{1,0:T(8,128)(2,1)S(1)}, u32[]{:S(2)}, u32[]{:S(2)}) collective-permute-start(bf16[512,768]{1,0:T(8,128)(2,1)S(1)} %slice.477), channel_id=1, source_target_pairs={{0,1},{1,0},{2,3},{3,2},{4,5},{5,4},{6,7},{7,6},{8,9},{9,8},{10,11... | collective-permute-start | bytes 2359304 | tf_op jit(solution)/shard_map/ppermute | solution.py:419
  396.5 20.1 %collective-permute-start.32 = (bf16[256,768]{1,0:T(8,128)(2,1)S(1)}, bf16[256,768]{1,0:T(8,128)(2,1)S(1)}, u32[]{:S(2)}, u32[]{:S(2)}) collective-permute-start(bf16[256,768]{1,0:T(8,128)(2,1)S(1)} %split.91), channel_id=1, source_target_pairs={{0,16},{8,24},{16,0},{24,8},{1,17},{9,25},{17,1},{25,9},{2,18},{10... | collective-permute-start | bytes 1179656 | tf_op jit(solution)/shard_map/ppermute | solution.py:414
  442.9 201.8 %reduce-scatter.5.cloned.1.call-start = ((), (), s32[]{:S(2)}) async-start(), calls=%async_computation.9 | async-start | bytes 3981312 | tf_op jit(solution)/shard_map/reduce_scatter | solution.py:569
  492.9 20.3 %collective-permute-start.42 = (bf16[512,1536]{1,0:T(8,128)(2,1)}, bf16[512,1536]{1,0:T(8,128)(2,1)}, u32[]{:S(2)}, u32[]{:S(2)}) collective-permute-start(bf16[512,1536]{1,0:T(8,128)(2,1)} %get-tuple-element.53), channel_id=1, source_target_pairs={{0,8},{8,0},{16,24},{24,16},{1,9},{9,1},{17,25},{25,17},{2,10},{10... | collective-permute-start | bytes 4718600 | tf_op jit(solution)/shard_map/ppermute | solution.py:414
  515.8 20.5 %collective-permute-start.43 = (bf16[512,768]{1,0:T(8,128)(2,1)S(1)}, bf16[512,768]{1,0:T(8,128)(2,1)S(1)}, u32[]{:S(2)}, u32[]{:S(2)}) collective-permute-start(bf16[512,768]{1,0:T(8,128)(2,1)S(1)} %slice.480), channel_id=1, source_target_pairs={{0,1},{1,0},{2,3},{3,2},{4,5},{5,4},{6,7},{7,6},{8,9},{9,8},{10,11... | collective-permute-start | bytes 2359304 | tf_op jit(solution)/shard_map/ppermute | solution.py:419
  519.6 25.3 %collective-permute-start.49 = (bf16[256,1536]{1,0:T(8,128)(2,1)S(1)}, bf16[256,1536]{1,0:T(8,128)(2,1)S(1)}, u32[]{:S(2)}, u32[]{:S(2)}) collective-permute-start(bf16[256,1536]{1,0:T(8,128)(2,1)S(1)} %split.109), channel_id=1, source_target_pairs={{0,16},{8,24},{16,0},{24,8},{1,17},{9,25},{17,1},{25,9},{2,18},{10... | collective-permute-start | bytes 2359304 | tf_op jit(solution)/shard_map/ppermute | solution.py:414
  523.3 30.0 %collective-permute-start.45 = (bf16[256,768]{1,0:T(8,128)(2,1)S(1)}, bf16[256,768]{1,0:T(8,128)(2,1)S(1)}, u32[]{:S(2)}, u32[]{:S(2)}) collective-permute-start(bf16[256,768]{1,0:T(8,128)(2,1)S(1)} %split.103), channel_id=1, source_target_pairs={{0,16},{8,24},{16,0},{24,8},{1,17},{9,25},{17,1},{25,9},{2,18},{10... | collective-permute-start | bytes 1179656 | tf_op jit(solution)/shard_map/ppermute | solution.py:414
  528.1 25.2 %collective-permute-start.47 = (bf16[256,768]{1,0:T(8,128)(2,1)S(1)}, bf16[256,768]{1,0:T(8,128)(2,1)S(1)}, u32[]{:S(2)}, u32[]{:S(2)}) collective-permute-start(bf16[256,768]{1,0:T(8,128)(2,1)S(1)} %add_convert_fusion.8), channel_id=1, source_target_pairs={{0,1},{1,0},{2,3},{3,2},{4,5},{5,4},{6,7},{7,6},{8,9},{9,8},{10,11... | collective-permute-start | bytes 1179656 | tf_op jit(solution)/shard_map/ppermute | solution.py:419
  536.5 24.3 %collective-permute-start.44 = (bf16[256,768]{1,0:T(8,128)(2,1)S(1)}, bf16[256,768]{1,0:T(8,128)(2,1)S(1)}, u32[]{:S(2)}, u32[]{:S(2)}) collective-permute-start(bf16[256,768]{1,0:T(8,128)(2,1)S(1)} %split.101), channel_id=1, source_target_pairs={{0,16},{8,24},{16,0},{24,8},{1,17},{9,25},{17,1},{25,9},{2,18},{10... | collective-permute-start | bytes 1179656 | tf_op jit(solution)/shard_map/ppermute | solution.py:414
  565.8 19.9 %collective-permute-start.51 = (bf16[192,1536]{1,0:T(8,128)(2,1)S(1)}, bf16[192,1536]{1,0:T(8,128)(2,1)}, u32[]{:S(2)}, u32[]{:S(2)}) collective-permute-start(bf16[192,1536]{1,0:T(8,128)(2,1)S(1)} %get-tuple-element.142), channel_id=1, source_target_pairs={{8,0},{0,1},{10,2},{2,3},{12,4},{4,5},{14,6},{6,7},{9,8},{1,9},{11... | collective-permute-start | bytes 1769480 | tf_op jit(solution)/shard_map/ppermute | solution.py:503
  587.0 30.6 %collective-permute-start.53 = (bf16[192,1536]{1,0:T(8,128)(2,1)}, bf16[192,1536]{1,0:T(8,128)(2,1)}, u32[]{:S(2)}, u32[]{:S(2)}) collective-permute-start(bf16[192,1536]{1,0:T(8,128)(2,1)} %get-tuple-element.138), channel_id=1, source_target_pairs={{8,0},{0,1},{10,2},{2,3},{12,4},{4,5},{14,6},{6,7},{9,8},{1,9},{11... | collective-permute-start | bytes 1769480 | tf_op jit(solution)/shard_map/ppermute | solution.py:503
  594.7 24.5 %collective-permute-start.54 = (bf16[192,768]{1,0:T(8,128)(2,1)S(1)}, bf16[192,768]{1,0:T(8,128)(2,1)S(1)}, u32[]{:S(2)}, u32[]{:S(2)}) collective-permute-start(bf16[192,768]{1,0:T(8,128)(2,1)S(1)} %get-tuple-element.193), channel_id=1, source_target_pairs={{0,0},{8,1},{2,2},{10,3},{4,4},{12,5},{6,6},{14,7},{1,8},{9,9},{3,... | collective-permute-start | bytes 884744 | tf_op jit(solution)/shard_map/ppermute | solution.py:503
  595.4 30.5 %collective-permute-start.55 = (bf16[192,768]{1,0:T(8,128)(2,1)S(1)}, bf16[192,768]{1,0:T(8,128)(2,1)S(1)}, u32[]{:S(2)}, u32[]{:S(2)}) collective-permute-start(bf16[192,768]{1,0:T(8,128)(2,1)S(1)} %get-tuple-element.194), channel_id=1, source_target_pairs={{8,0},{0,1},{10,2},{2,3},{12,4},{4,5},{14,6},{6,7},{9,8},{1,9},{11... | collective-permute-start | bytes 884744 | tf_op jit(solution)/shard_map/ppermute | solution.py:503
  (97 other events, 1101.8 us)
Sparse Core Ops, SparseCore 0:
  13.6 55.7 all-gather.4
  71.0 95.6 all-gather.6
  168.2 89.5 all-gather.8
  265.8 58.8 all-gather.10
  326.9 84.0 reduce-scatter.6
  413.1 85.7 reduce-scatter.8
  501.2 48.5 reduce-scatter.10
  553.4 91.2 reduce-scatter.4

commit v4 on v3

--- a/solution.py
+++ b/solution.py
@@ -102,7 +102,7 @@
         ],
         compiler_params=pltpu.CompilerParams(vmem_limit_bytes=48 * 1024 * 1024),
         cost_estimate=pl.CostEstimate(
-            flops=4 * heads * length * length * HEAD_SIZE,
+            flops=50 * heads * length * length * HEAD_SIZE,
             bytes_accessed=6 * heads * length * HEAD_SIZE,
             transcendentals=heads * length * length // 2,
         ),
@@ -186,7 +186,7 @@
         ],
         compiler_params=pltpu.CompilerParams(vmem_limit_bytes=48 * 1024 * 1024),
         cost_estimate=pl.CostEstimate(
-            flops=10 * heads * length * length * HEAD_SIZE,
+            flops=46 * heads * length * length * HEAD_SIZE,
             bytes_accessed=16 * heads * length * HEAD_SIZE,
             transcendentals=heads * length * length // 2,
         ),
@@ -361,7 +361,7 @@
         ],
         compiler_params=pltpu.CompilerParams(vmem_limit_bytes=60 * 1024 * 1024),
         cost_estimate=pl.CostEstimate(
-            flops=10 * count * n * half * width,
+            flops=26 * count * n * half * width,
             bytes_accessed=8 * count * width + 4 * width * n * half * 3,
             transcendentals=count * n * half,
         ),
@@ -401,7 +401,7 @@
         out_shape=[jax.ShapeDtypeStruct((count // parts, width), jnp.bfloat16) for _ in range(parts)],
         compiler_params=pltpu.CompilerParams(vmem_limit_bytes=60 * 1024 * 1024),
         cost_estimate=pl.CostEstimate(
-            flops=2 * count * width * sum(s.shape[1] for s in scaled),
+            flops=4 * count * width * sum(s.shape[1] for s in scaled),
             bytes_accessed=4 * count * width,
             transcendentals=0,
         ),
@@ -426,6 +426,7 @@
         out_specs=pl.BlockSpec(memory_space=pl.ANY),
         out_shape=jax.ShapeDtypeStruct(v.shape, v.dtype),
         input_output_aliases={0: 0},
+        cost_estimate=pl.CostEstimate(flops=0, bytes_accessed=1024, transcendentals=0),
         name="after",
     )(v, behind)
 
@@ -446,10 +447,13 @@
     return v
 
 
-def gather_heads(v):
+def gather_heads(v, *behind):
     members = lax.axis_size("expert")
     width = v.shape[1] // members
     for bit in chip_bits() + [1]:
+        if bit == 1:
+            for other in behind:
+                v = after(v, other)
         got = swap_member(v, bit)
         source = [place_of(2 * (p % (members // 2)) + p // (members // 2), bit, members) for p in range(members)]
         got = jnp.concatenate([got[:, p * width : (p + 1) * width] for p in source], axis=1)
@@ -479,10 +483,12 @@
     if axis == 1:
         return scatter_chip(add_swapped(own, other, swap_shard), axis)
     cut = own.shape[1] // 2
-    one = scatter_chip(add_swapped(own[:, :cut], other[:, :cut], swap_shard).astype(kind), 0)
+    one = add_swapped(own[:, :cut], other[:, :cut], swap_shard).astype(kind)
+    halfway = one
+    one = scatter_chip(one, 0)
     two, two_other = scatter_chip(own[:, cut:], 0), scatter_chip(other[:, cut:], 0)
     two = add_swapped(two, two_other, swap_shard)
-    return jnp.concatenate([one.astype(jnp.float32), two], axis=1)
+    return jnp.concatenate([one.astype(jnp.float32), two], axis=1), halfway
 
 
 def turn(first, back=False):
@@ -508,65 +514,30 @@
     return [[s for s in range(n) if s & 1 == low] for low in range(2)]
 
 
-def ring():
-    n = lax.axis_size("shard")
-    wide = n // 4
-    walk = [(z, 0) for z in range(4)]
-    for i, z in enumerate(reversed(range(4))):
-        ys = range(1, wide)
-        walk += [(z, y) for y in (ys if i % 2 == 0 else reversed(ys))]
-    return [z * wide + y for z, y in walk]
-
-
-def ring_step(v, by):
-    walk = ring()
-    n = len(walk)
-    return lax.ppermute(v, "shard", [(walk[i], walk[(i + by) % n]) for i in range(n)])
-
-
-def place_kernel(n, owner_ref, *refs):
-    size = refs[0].shape[0]
-    for i in range(n):
-        refs[n][pl.ds(pl.multiple_of(owner_ref[i] * size, 16), size), :] = refs[i][...]
-
-
-def ring_gather(v):
-    n = lax.axis_size("shard")
-    walk = ring()
-    place = [walk.index(i) for i in range(n)]
-    here = jnp.asarray(place, jnp.int32)[lax.axis_index("shard")]
-    pieces, offsets = [v], [0]
-    forth = back = v
-    for k in range(1, n // 2 + 1):
-        forth = ring_step(forth, 1)
-        pieces.append(forth)
-        offsets.append(-k)
-        if k < n // 2:
-            back = ring_step(back, -1)
-            pieces.append(back)
-            offsets.append(k)
-    owners = jnp.asarray(walk, jnp.int32)[(here + jnp.asarray(offsets, jnp.int32)) % n]
-    rows, size = v.shape
-    return pl.pallas_call(
-        functools.partial(place_kernel, n),
-        grid_spec=pltpu.PrefetchScalarGridSpec(
-            num_scalar_prefetch=1,
-            grid=(1,),
-            in_specs=[pl.BlockSpec((rows, size), lambda i, o: (0, 0))] * n,
-            out_specs=pl.BlockSpec((rows * n, size), lambda i, o: (0, 0)),
-        ),
-        out_shape=jax.ShapeDtypeStruct((rows * n, size), v.dtype),
-        compiler_params=pltpu.CompilerParams(vmem_limit_bytes=48 * 1024 * 1024),
-        name="place",
-    )(owners, *pieces)
-
-
-def gather_shard(v):
-    return lax.all_gather(v, "shard", axis=0, tiled=True)
-
-
-def scatter_shard(v):
-    return lax.psum_scatter(v, "shard", scatter_dimension=0, tiled=True)
+def gather_line(v):
+    return lax.all_gather(v, "shard", axis=0, tiled=True, axis_index_groups=shard_lines())
+
+
+def scatter_line(v):
+    return lax.psum_scatter(
+        v, "shard", scatter_dimension=0, tiled=True, axis_index_groups=shard_lines()
+    )
+
+
+def merge_lines(v, low):
+    n = lax.axis_size("shard") // 2
+    got = swap_shard(v)
+    v, got = v.reshape(n, -1, v.shape[1]), got.reshape(n, -1, v.shape[1])
+    sides = [jnp.where(low == 0, v, got), jnp.where(low == 0, got, v)]
+    return jnp.stack(sides, axis=1).reshape(-1, v.shape[2])
+
+
+def split_lines(v, low):
+    n = lax.axis_size("shard") // 2
+    v = v.reshape(n, 2, -1, v.shape[1])
+    keep, sent = jnp.where(low == 0, v[:, 0], v[:, 1]), jnp.where(low == 0, v[:, 1], v[:, 0])
+    keep, sent = keep.reshape(-1, v.shape[3]), sent.reshape(-1, v.shape[3])
+    return add_swapped(keep, sent, swap_shard).astype(v.dtype)
 
 
 def out_kernel(members, me_ref, slice_ref, out_ref):
@@ -591,6 +562,9 @@
         ),
         out_shape=jax.ShapeDtypeStruct((rows, size * members), slices.dtype),
         compiler_params=pltpu.CompilerParams(vmem_limit_bytes=48 * 1024 * 1024),
+        cost_estimate=pl.CostEstimate(
+            flops=0, bytes_accessed=4 * rows * size * members, transcendentals=0
+        ),
         name="assemble_out",
     )(me, slices)
 
@@ -624,17 +598,29 @@
     heads, kv_heads = q_cols // HEAD_SIZE, k_cols // HEAD_SIZE
     out_rows = width // (members * shards)
     half = FF // 2
-    step = 2 if length <= 1024 else 1
-    chunks = [tuple(range(i, min(i + step, EXP_DEV))) for i in range(0, EXP_DEV, step)]
+    cuts = [0, 2, EXP_DEV] if length <= 1024 else range(EXP_DEV + 1)
+    chunks = [tuple(range(a, b)) for a, b in zip(cuts[:-1], cuts[1:])]
     me_ref = me[None].astype(jnp.int32)
 
     def cols(w, n):
         return lax.dynamic_slice_in_dim(w, me * n, n, axis=1)
+
+    all_tokens = gather_members(tokens[0])
+    meta = jnp.concatenate([segment_ids, routes[0].T], axis=0)
+    meta = gather_members(meta, axis=1)
+    seg = meta[0]
+    my_routes = meta[1:]
+    my_grad = after(cotangent[0], all_tokens)
+    for bit in chip_bits():
+        my_grad = jnp.concatenate([my_grad, swap_member(my_grad, bit)], axis=0)
+    grad_pair = my_grad
+    my_grad = jnp.concatenate([my_grad, swap_member(my_grad, 1)], axis=0)
 
     small = jnp.concatenate([w_router, gain_attn[:, None], gain_ffn[:, None]], axis=1)
     total_cols = q_cols + 2 * k_cols
     first = jnp.concatenate(
         [
+            cols(w_out, q_cols),
             cols(w_query, q_cols),
             cols(key_weight, k_cols),
             cols(value_weight, k_cols),
@@ -642,23 +628,17 @@
         ],
         axis=1,
     )
-    first = gather_shard(first)
+    first = gather_line(first)
+    out_slice = first[:, :q_cols]
+    first = merge_lines(after(first[:, q_cols:], grad_pair), low)
+    out_slice = merge_lines(after(out_slice, first), low)
     full_qkv = first[:, :total_cols]
     full_small = first[:, total_cols:]
     full_router = full_small[:, :experts]
     gain_one = full_small[:, experts].astype(f32)
     gain_two = full_small[:, experts + 1].astype(f32)
 
-    all_tokens = gather_members(tokens[0])
-    meta = jnp.concatenate([segment_ids, routes[0].T], axis=0)
-    meta = gather_members(meta, axis=1)
-    seg = meta[0]
-    my_routes = meta[1:]
-    my_grad = gather_members(after(cotangent[0], all_tokens))
-    all_grad = [my_grad, *swap_sequence(my_grad)]
-    out_slice = ring_gather(after(cols(w_out, q_cols), all_tokens))
-
-    weights = []
+    weights, blocks = [], []
     for js in chunks:
         sides = [
             jnp.concatenate(
@@ -669,13 +649,17 @@
             )
             for h in range(2)
         ]
-        one = permute_all(jnp.where(low == 0, sides[0], sides[1]), turn(True))
-        two = permute_all(jnp.where(low == 0, sides[1], sides[0]), turn(False))
+        one = jnp.where(low == 0, sides[0], sides[1])
+        two = jnp.where(low == 0, sides[1], sides[0])
+        if blocks:
+            one, two = after(one, out_slice), after(two, out_slice)
+        one, two = permute_all(one, turn(True)), permute_all(two, turn(False))
         block = jnp.concatenate(
             [jnp.where(core == 0, one, two), jnp.where(core == 0, two, one)], axis=0
         )
+        blocks.append(block)
         weights.append(
-            lax.all_gather(block, "shard", axis=0, tiled=True, axis_index_groups=shard_lines())
+            gather_line(block)
         )
 
     inputs = all_tokens.astype(f32)
@@ -692,8 +676,13 @@
     values = qkv[heads + kv_heads :].astype(bf16)
     attended, lse = attention_forward(me_ref, queries, keys, values, seg)
     attended_rows = attended.reshape(q_cols, length)
-    attended_all = gather_heads(attended_rows)
-    full_out = assemble_out(me_ref, gather_members(out_slice[None]))
+    all_grad = [my_grad, *swap_sequence(my_grad)]
+    out_slices = out_slice[None]
+    for bit in chip_bits():
+        out_slices = jnp.concatenate([out_slices, swap_member(out_slices, bit)], axis=0)
+    attended_all = gather_heads(attended_rows, blocks[-1], out_slices)
+    out_slices = jnp.concatenate([out_slices, swap_member(out_slices, 1)], axis=0)
+    full_out = assemble_out(me_ref, out_slices)
 
     hidden = inputs + dot(attended_all, full_out, 0, 0)
     normed_two = hidden * inverse_rms(hidden)
@@ -722,13 +711,13 @@
         )
         scaled.append(s)
         gate_grads.append(gg)
-        expert_grads.append(
-            lax.psum_scatter(
-                grads, "shard", scatter_dimension=0, tiled=True, axis_index_groups=shard_lines()
-            )
-        )
-
-    grad_xn_two = scatter_members(grad_in)
+        expert_grads.append(grads)
+
+    grad_xn_two, halfway = scatter_members(grad_in)
+    for i, grads in enumerate(expert_grads):
+        if i > 0:
+            grads = after(after(grads, expert_grads[i - 1]), halfway)
+        expert_grads[i] = scatter_line(grads)
     gate_grads = jnp.tile(jnp.concatenate(gate_grads, axis=0), (members, 1))
     mine = jnp.arange(experts, dtype=jnp.int32)[:, None] // EXP_DEV == group
     gate_grads = jnp.where(mine, gate_grads, 0.0)
@@ -750,14 +739,18 @@
     grad_attended = dot(full_out[:q_cols], grad_attn, 1, 1).astype(bf16)
     grad_attended = grad_attended.reshape(heads, HEAD_SIZE, length)
     grad_out = jnp.dot(attended_rows, grad_attn, preferred_element_type=f32)
+    grad_out = jnp.transpose(
+        grad_out.astype(bf16).reshape(shards, out_rows, members, q_cols), (0, 2, 1, 3)
+    )
+    grad_out = split_lines(grad_out.reshape(width, q_cols), low)
     grad_router = dot(my_xn_two[:rows], grad_logits, 0, 1)
 
     dq, dk, dv = attention_backward(me_ref, queries, keys, values, attended, grad_attended, lse, seg)
     dq = rotate(dq, cosine, -sine) * HEAD_SIZE**-0.5
     dk = rotate(dk, cosine, -sine)
     grad_qkv = jnp.concatenate([dq, dk, dv], axis=0).astype(bf16).reshape(-1, length)
-    grad_first = dot(xn_one, grad_qkv, 0, 1)
-    grad_xn_one = dot(grad_qkv, full_qkv, 0, 1)
+    grad_first = behind = dot(xn_one, grad_qkv, 0, 1)
+    grad_xn_one = dot(after(grad_qkv, grad_first), full_qkv, 0, 1)
     grad_gain_one = jnp.sum(grad_xn_one * normed_one, axis=0)
     grad_xn_one = grad_xn_one.astype(bf16)
     for bit in [1] + chip_bits()[::-1]:
@@ -773,18 +766,16 @@
     rest = jnp.pad(rest, ((0, 0), (0, 128 - rest.shape[1])))
     grad_first = jnp.concatenate([grad_first, rest], axis=1).astype(bf16)
     grad_first = jnp.transpose(grad_first.reshape(members, shards, out_rows, -1), (1, 0, 2, 3))
-    grad_out = jnp.transpose(
-        grad_out.astype(bf16).reshape(shards, out_rows, members, q_cols), (0, 2, 1, 3)
-    )
-    grad_first = jnp.concatenate([grad_first, grad_out], axis=3)
-    grad_first = scatter_shard(grad_first.reshape(width, -1)).reshape(members, out_rows, -1)
+    grad_first = split_lines(grad_first.reshape(width, -1), low)
+    grad_first = jnp.concatenate([grad_first, grad_out], axis=1)
+    grad_first = scatter_line(after(grad_first, expert_grads[-1])).reshape(members, out_rows, -1)
     out_grads = jnp.transpose(grad_first[:, :, total_cols + 128 :], (1, 0, 2)).astype(f32)
     grad_first = grad_first[:, :, : total_cols + 128]
     grad_first = lax.all_to_all(grad_first, "expert", split_axis=0, concat_axis=0, tiled=True)
     rest = jnp.sum(grad_first[:, :, total_cols:].astype(f32), axis=0)
     grad_first = jnp.transpose(grad_first, (1, 0, 2)).astype(f32)
 
-    mixed = my_hidden + scatter_members(mix_experts(scaled, weights, grad_attn))
+    mixed = my_hidden + scatter_members(mix_experts(scaled, weights, behind))[0]
 
     gate_up_out, down_out = [], []
     one = None

time: 676 us -> 618 us (0.914)
  starting transfers between devices: 101 us -> 51.6 us
  Pallas kernels: 154 us -> 145 us
    ppermute x8 -> x12, waiting for transfers between devices: 23 us -> 99.8 us  [swap_shard(): return lax.ppermute(v, 'shard', [(i, i ^ 1) for i in range(n)])]
    ppermute x12 -> x8, waiting for transfers between devices: 80.8 us -> 13.4 us  [permute_all(): return lax.ppermute(v, ('expert', 'shard'), pairs)]
    ppermute x12 -> x8, starting transfers between devices: 52.5 us -> 13.8 us  [permute_all(): return lax.ppermute(v, ('expert', 'shard'), pairs)]
    ppermute x7 -> x0, waiting for transfers between devices: 24.2 us -> none  [ring_step(): lax.ppermute(v, 'shard', [(walk[i], walk[(i + by) % n]) for i in range(n)])]
    concatenate x9 -> x4, other arithmetic: 19 us -> 1.36 us  [gather_members(): v = jnp.concatenate([v, swap_member(v, bit)], axis=axis)]
    ppermute x7 -> x0, starting transfers between devices: 15.8 us -> none  [ring_step(): lax.ppermute(v, 'shard', [(walk[i], walk[(i + by) % n]) for i in range(n)])]
    concatenate x2 -> x7, other arithmetic: 2.04 us -> 15.8 us  [the longest x1 4.62 us: body(): jnp.concatenate([out_slices, swap_member(out_slices, 1)], axis=0)]
    ppermute x29, waiting for transfers between devices: 99.8 us -> 112 us  [swap_member(): return lax.ppermute(v, 'expert', [(i, i ^ bit) for i in range(n)])]
  transfers between devices with their start and end apart: 65 -> 56, of which waited for: 30 -> 29; matrix products, arithmetic and copies ran while one was open for 19% -> 21% of each run, Pallas kernels for 23% -> 24%
where the time goes in v4:
time: 618 us; the launch traced here: 608 us
  waiting for transfers between devices  247 us (40%)
  Pallas kernels  145 us (23%)
  other arithmetic  66.8 us (11%)
  starting transfers between devices  51.6 us (8%)
  local copies, waits for them, and re-layouts  48.3 us (8%)
  matrix products  33.1 us (5%)
  between operations  16.1 us (3%)
    ppermute x29, waiting for transfers between devices, swap_member(): return lax.ppermute(v, 'expert', [(i, i ^ bit) for i in range(n)])  112 us
    ppermute x12, waiting for transfers between devices, swap_shard(): return lax.ppermute(v, 'shard', [(i, i ^ 1) for i in range(n)])  99.8 us
    pallas_call x2, Pallas kernels, expert_chunk(): pl.pallas_call(functools.partial(expert_kernel, js[0], n, half, tiles, ba...  92 us
    dot_general x8, matrix products, dot(): lax.dot_general(a, b, (((ca,), (cb,)), ((), ())), preferred_element_type=...  29.3 us
    unnamed x153, local copies, waits for them, and re-layouts  24.7 us
    ppermute x29, starting transfers between devices, swap_member(): return lax.ppermute(v, 'expert', [(i, i ^ bit) for i in range(n)])  20.9 us
    pallas_call x1, Pallas kernels, attention_forward(): pl.pallas_call(functools.partial(attention_forward_kernel, blocks), grid_...  17.6 us
    pallas_call x1, Pallas kernels, attention_backward(): pl.pallas_call(functools.partial(attention_backward_kernel, blocks), grid...  16 us
  transfers between devices with their start and end apart: 56, of which 29 were waited for; matrix products, arithmetic and copies ran while one was open for 21% of the time, Pallas kernels for 24%

profile of v4, /device:TPU:0, one launch (start us, length us, event | category | flops | bytes accessed | tf_op | source)
XLA Modules:
  0.0 607.9 jit_solution(13476808432031050744)
XLA Ops:
  19.8 8.2 %collective-permute-done = bf16[256,1536]{1,0:T(8,128)(2,1)S(1)} collective-permute-done((bf16[256,1536]{1,0:T(8,128)(2,1)}, bf16[256,1536]{1,0:T(8,128)(2,1)S(1)}, u32[]{:S(2)}, u32[]{:S(2)}) %collective-permute-start) | collective-permute-done | bytes 786464 | tf_op jit(solution)/shard_map/ppermute | solution.py:414
  41.2 12.6 %collective-permute-done.4 = s32[9,256]{1,0:T(8,128)S(1)} collective-permute-done((s32[9,256]{1,0:T(8,128)S(1)}, s32[9,256]{1,0:T(8,128)S(1)}, u32[]{:S(2)}, u32[]{:S(2)}) %collective-permute-start.4) | collective-permute-done | bytes 9248 | tf_op jit(solution)/shard_map/ppermute | solution.py:414
  69.4 19.9 %collective-permute-done.3 = bf16[768,768]{1,0:T(8,128)(2,1)} collective-permute-done((bf16[768,768]{1,0:T(8,128)(2,1)}, bf16[768,768]{1,0:T(8,128)(2,1)}, u32[]{:S(2)}, u32[]{:S(2)}) %collective-permute-start.3) | collective-permute-done | bytes 1179680 | tf_op jit(solution)/shard_map/ppermute | solution.py:419
  101.4 17.6 %attention_forward.1 = (bf16[6,64,1024]{2,1,0:T(8,128)(2,1)S(1)}, f32[6,1,1024]{2,1,0:T(1,128)S(1)}) custom-call(s32[1]{0:T(128)} %bitcast.1.me_ref, bf16[6,64,1024]{2,1,0:T(8,128)(2,1)S(1)} %fusion.31.q_ref, bf16[2,64,1024]{2,1,0:T(8,128)(2,1)S(1)} %pad_maximum_fusion.17.k_ref, bf16[2,64,1024]{2,1,0:T(8,128)(2,1)S(1)} %bitcast.189, ...), custom_call_target="tpu_custom_call" | custom-call | flops 20132659200 | bytes 2359296 | tf_op jit(solution)/shard_map/attention_forward/pallas_call | solution.py:84
  125.6 14.1 %collective-permute-done.6 = bf16[384,1024]{1,0:T(8,128)(2,1)} collective-permute-done((bf16[384,1024]{1,0:T(8,128)(2,1)S(1)}, bf16[384,1024]{1,0:T(8,128)(2,1)}, u32[]{:S(2)}, u32[]{:S(2)}) %collective-permute-start.6) | collective-permute-done | bytes 786464 | tf_op jit(solution)/shard_map/ppermute | solution.py:414
  142.3 20.3 %collective-permute-done.10 = bf16[1,1536,384]{2,1,0:T(8,128)(2,1)} collective-permute-done((bf16[1,1536,384]{2,1,0:T(8,128)(2,1)}, bf16[1,1536,384]{2,1,0:T(8,128)(2,1)}, u32[]{:S(2)}, u32[]{:S(2)}) %collective-permute-start.10) | collective-permute-done | bytes 1179680 | tf_op jit(solution)/shard_map/ppermute | solution.py:414
  174.7 4.6 pad_maximum_fusion.slice_ref
  179.3 4.0 assemble_out.1
  183.4 5.9 multiply_reduce_fusion
  194.2 12.8 %collective-permute-done.16.refs_4_ = bf16[512,1536]{1,0:T(8,128)(2,1)} collective-permute-done((bf16[512,1536]{1,0:T(8,128)(2,1)}, bf16[512,1536]{1,0:T(8,128)(2,1)}, u32[]{:S(2)}, u32[]{:S(2)}) %collective-permute-start.16) | collective-permute-done | bytes 1572896 | tf_op jit(solution)/shard_map/ppermute | solution.py:419
  207.0 32.7 %collective-permute-done.13.refs_1_ = bf16[512,1536]{1,0:T(8,128)(2,1)} collective-permute-done((bf16[512,1536]{1,0:T(8,128)(2,1)S(1)}, bf16[512,1536]{1,0:T(8,128)(2,1)}, u32[]{:S(2)}, u32[]{:S(2)}) %collective-permute-start.13) | collective-permute-done | bytes 1572896 | tf_op jit(solution)/shard_map/ppermute | solution.py:419
  246.7 4.0 collective-permute-done.18
  251.4 37.3 %experts.2 = (f32[2048,1536]{1,0:T(8,128)}, bf16[2048,512]{1,0:T(8,128)(2,1)}, f32[2,2048]{1,0:T(2,128)}, bf16[1536,1536]{1,0:T(8,128)(2,1)}) custom-call(bf16[1024,1536]{1,0:T(8,128)(2,1)} %copy-done.6, bf16[512,1536]{1,0:T(8,128)(2,1)} %collective-permute-done.13.refs_1_, bf16[512,1536]{1,0:T(8,128)(2,1)} %collective-permute-done.14.refs_2_, ...), custom_call_target="tpu_custom_call" | custom-call | flops 41875931136 | bytes 34603008 | tf_op jit(solution)/shard_map/experts/pallas_call | solution.py:336
  288.8 7.0 %all-gather.8.cloned.1.call-done.refs_8_.refs_3_ = bf16[1536,2304]{1,0:T(8,128)(2,1)} async-done(((bf16[384,2304]{1,0:T(8,128)(2,1)}), bf16[1536,2304]{1,0:T(8,128)(2,1)}) %all-gather.8.cloned.1.call-update) | async-done | bytes 7077904 | tf_op jit(solution)/shard_map/all_gather | solution.py:518
  295.7 54.7 %experts.3 = (bf16[512,1536]{1,0:T(8,128)(2,1)}, bf16[512,1536]{1,0:T(8,128)(2,1)}, bf16[512,1536]{1,0:T(8,128)(2,1)}, bf16[512,1536]{1,0:T(8,128)(2,1)}, bf16[2...) custom-call(bf16[1024,1536]{1,0:T(8,128)(2,1)} %copy-done.6, ...), custom_call_target="tpu_custom_call" | custom-call | flops 62813896704 | bytes 39321600 | tf_op jit(solution)/shard_map/experts/pallas_call | solution.py:336
  368.7 9.5 %collective-permute-done.26 = bf16[256,768]{1,0:T(8,128)(2,1)S(1)} collective-permute-done((bf16[256,768]{1,0:T(8,128)(2,1)S(1)}, bf16[256,768]{1,0:T(8,128)(2,1)S(1)}, u32[]{:S(2)}, u32[]{:S(2)}) %collective-permute-start.26) | collective-permute-done | bytes 393248 | tf_op jit(solution)/shard_map/ppermute | solution.py:414
  379.0 6.2 %collective-permute-done.23 = bf16[512,768]{1,0:T(8,128)(2,1)S(1)} collective-permute-done((bf16[512,768]{1,0:T(8,128)(2,1)S(1)}, bf16[512,768]{1,0:T(8,128)(2,1)S(1)}, u32[]{:S(2)}, u32[]{:S(2)}) %collective-permute-start.23) | collective-permute-done | bytes 786464 | tf_op jit(solution)/shard_map/ppermute | solution.py:419
  387.0 4.6 collective-permute-done.27
  397.9 14.4 %collective-permute-done.32 = bf16[256,1536]{1,0:T(8,128)(2,1)S(1)} collective-permute-done((bf16[256,1536]{1,0:T(8,128)(2,1)S(1)}, bf16[256,1536]{1,0:T(8,128)(2,1)S(1)}, u32[]{:S(2)}, u32[]{:S(2)}) %collective-permute-start.32) | collective-permute-done | bytes 786464 | tf_op jit(solution)/shard_map/ppermute | solution.py:414
  418.4 6.0 collective-permute-start.45
  427.8 16.0 %attention_backward.1 = (f32[6,64,1024]{2,1,0:T(8,128)S(1)}, f32[2,64,1024]{2,1,0:T(8,128)S(1)}, f32[2,64,1024]{2,1,0:T(8,128)S(1)}) custom-call(s32[1]{0:T(128)} %bitcast.1.me_ref, bf16[6,64,1024]{2,1,0:T(8,128)(2,1)S(1)} %copy-done.2, bf16[2,64,1024]{2,1,0:T(8,128)(2,1)S(1)} %copy-done.4, bf16[2,64,1024]{2,1,0:T(8,128)(2,1)S(1)} %bitcast.190, ...), custom_call_target="tpu_custom_call" | custom-call | flops 18522046464 | bytes 6291456 | tf_op jit(solution)/shard_map/attention_backward/pallas_call | solution.py:159
  446.7 5.0 fusion.74
  451.6 7.6 %fusion.3 = (bf16[1536]{0:T(1024)(128)(2,1)S(1)}, bf16[1024,1536]{1,0:T(8,128)(2,1)}) fusion(bf16[1024,1536]{1,0:T(8,128)(2,1)} %get-tuple-element.93.refs_1_, f32[1024]{0:T(1024)S(1)} %copy-done.63, bf16[640,1024]{1,0:T(8,128)(2,1)} %after.18, bf16[1536,768]{1,0:T(8,128)(2,1)} %bitcast.203), kind=kOutput, calls=%fused_computation.6 | convolution fusion | flops 2021128704 | bytes 9575424 | tf_op jit(solution)/shard_map/dot_general | solution.py:26
  472.9 15.2 %mix_experts.1 = (bf16[512,1536]{1,0:T(8,128)(2,1)}, bf16[512,1536]{1,0:T(8,128)(2,1)}, bf16[512,1536]{1,0:T(8,128)(2,1)}, bf16[512,1536]{1,0:T(8,128)(2,1)}) custom-call(bf16[2048,512]{1,0:T(8,128)(2,1)} %get-tuple-element.33.refs_0_, bf16[2048,768]{1,0:T(8,128)(2,1)} %get-tuple-element.35.refs_1_, ...), custom_call_target="tpu_custom_call" | custom-call | flops 16106127360 | bytes 12582912 | tf_op jit(solution)/shard_map/mix_experts/pallas_call | solution.py:394
  492.1 12.3 %collective-permute-done.44 = bf16[768,384]{1,0:T(8,128)(2,1)} collective-permute-done((bf16[768,384]{1,0:T(8,128)(2,1)}, bf16[768,384]{1,0:T(8,128)(2,1)}, u32[]{:S(2)}, u32[]{:S(2)}) %collective-permute-start.44) | collective-permute-done | bytes 589856 | tf_op jit(solution)/shard_map/ppermute | solution.py:419
  515.9 7.5 %collective-permute-done.39 = bf16[256,768]{1,0:T(8,128)(2,1)S(1)} collective-permute-done((bf16[256,768]{1,0:T(8,128)(2,1)S(1)}, bf16[256,768]{1,0:T(8,128)(2,1)S(1)}, u32[]{:S(2)}, u32[]{:S(2)}) %collective-permute-start.39) | collective-permute-done | bytes 393248 | tf_op jit(solution)/shard_map/ppermute | solution.py:414
  524.1 6.2 %collective-permute-done.36 = bf16[512,768]{1,0:T(8,128)(2,1)S(1)} collective-permute-done((bf16[512,768]{1,0:T(8,128)(2,1)S(1)}, bf16[512,768]{1,0:T(8,128)(2,1)S(1)}, u32[]{:S(2)}, u32[]{:S(2)}) %collective-permute-start.36) | collective-permute-done | bytes 786464 | tf_op jit(solution)/shard_map/ppermute | solution.py:419
  532.9 7.3 %collective-permute-done.42 = bf16[256,1536]{1,0:T(8,128)(2,1)S(1)} collective-permute-done((bf16[256,1536]{1,0:T(8,128)(2,1)S(1)}, bf16[256,1536]{1,0:T(8,128)(2,1)S(1)}, u32[]{:S(2)}, u32[]{:S(2)}) %collective-permute-start.42) | collective-permute-done | bytes 786464 | tf_op jit(solution)/shard_map/ppermute | solution.py:414
  541.6 7.0 %collective-permute-done.38 = bf16[256,768]{1,0:T(8,128)(2,1)S(1)} collective-permute-done((bf16[256,768]{1,0:T(8,128)(2,1)S(1)}, bf16[256,768]{1,0:T(8,128)(2,1)S(1)}, u32[]{:S(2)}, u32[]{:S(2)}) %collective-permute-start.38) | collective-permute-done | bytes 393248 | tf_op jit(solution)/shard_map/ppermute | solution.py:414
  559.9 13.4 %collective-permute-done.48 = bf16[192,2304]{1,0:T(8,128)(2,1)S(1)} collective-permute-done((bf16[192,2304]{1,0:T(8,128)(2,1)S(1)}, bf16[192,2304]{1,0:T(8,128)(2,1)S(1)}, u32[]{:S(2)}, u32[]{:S(2)}) %collective-permute-start.48) | collective-permute-done | bytes 884768 | tf_op jit(solution)/shard_map/ppermute | solution.py:509
  579.4 6.2 %reduce-scatter.8.cloned.1.call-done = bf16[192,1152]{1,0:T(8,128)(2,1)} async-done(((bf16[768,1152]{1,0:T(8,128)(2,1)}), bf16[192,1152]{1,0:T(8,128)(2,1)}) %reduce-scatter.8.cloned.1.call-update) | async-done | bytes 442384 | tf_op jit(solution)/shard_map/reduce_scatter | solution.py:522
  592.4 4.7 all-to-all-done
  (408 shorter events, 186.9 us)
Async XLA Ops:
  7.2 50.4 %all-gather.4.cloned.1.call-start = ((), (), s32[]{:S(2)}) async-start(), calls=%async_computation.4 | async-start | bytes 2211840 | tf_op jit(solution)/shard_map/all_gather | solution.py:518
  7.2 20.8 %collective-permute-start = (bf16[256,1536]{1,0:T(8,128)(2,1)}, bf16[256,1536]{1,0:T(8,128)(2,1)S(1)}, u32[]{:S(2)}, u32[]{:S(2)}) collective-permute-start(bf16[256,1536]{1,0:T(8,128)(2,1)} %bitcast.195), channel_id=1, source_target_pairs={{0,16},{8,24},{16,0},{24,8},{1,17},{9,25},{17,1},{25,9},{2,18},{10... | collective-permute-start | bytes 2359304 | tf_op jit(solution)/shard_map/ppermute | solution.py:414
  16.8 234.5 %all-gather.6.cloned.1.call-start = ((), (), s32[]{:S(2)}) async-start(), calls=%async_computation.5 | async-start | bytes 5898240 | tf_op jit(solution)/shard_map/all_gather | solution.py:518
  33.6 26.4 %collective-permute-start.2 = (bf16[256,1536]{1,0:T(8,128)(2,1)}, bf16[256,1536]{1,0:T(8,128)(2,1)S(1)}, u32[]{:S(2)}, u32[]{:S(2)}) collective-permute-start(bf16[256,1536]{1,0:T(8,128)(2,1)} %after.11), channel_id=1, source_target_pairs={{0,16},{8,24},{16,0},{24,8},{1,17},{9,25},{17,1},{25,9},{2,18},{10... | collective-permute-start | bytes 2359304 | tf_op jit(solution)/shard_map/ppermute | solution.py:414
  36.5 27.7 %collective-permute-start.19 = (bf16[192,1536]{1,0:T(8,128)(2,1)}, bf16[192,1536]{1,0:T(8,128)(2,1)S(1)}, u32[]{:S(2)}, u32[]{:S(2)}) collective-permute-start(bf16[192,1536]{1,0:T(8,128)(2,1)} %get-tuple-element.142), channel_id=1, source_target_pairs={{0,0},{1,8},{2,2},{3,10},{4,4},{5,12},{6,6},{7,14},{8,1},{9,9},{10... | collective-permute-start | bytes 1769480 | tf_op jit(solution)/shard_map/ppermute | solution.py:509
  38.2 26.8 %collective-permute-start.20 = (bf16[192,1536]{1,0:T(8,128)(2,1)}, bf16[192,1536]{1,0:T(8,128)(2,1)}, u32[]{:S(2)}, u32[]{:S(2)}) collective-permute-start(bf16[192,1536]{1,0:T(8,128)(2,1)} %get-tuple-element.143), channel_id=1, source_target_pairs={{0,8},{1,0},{2,10},{3,2},{4,12},{5,4},{6,14},{7,6},{8,9},{9,1},{10... | collective-permute-start | bytes 1769480 | tf_op jit(solution)/shard_map/ppermute | solution.py:509
  61.2 28.0 %collective-permute-start.3 = (bf16[768,768]{1,0:T(8,128)(2,1)}, bf16[768,768]{1,0:T(8,128)(2,1)}, u32[]{:S(2)}, u32[]{:S(2)}) collective-permute-start(bf16[768,768]{1,0:T(8,128)(2,1)} %after.12), channel_id=1, source_target_pairs={{0,1},{1,0},{2,3},{3,2},{4,5},{5,4},{6,7},{7,6},{8,9},{9,8},{10,11... | collective-permute-start | bytes 3538952 | tf_op jit(solution)/shard_map/ppermute | solution.py:419
  67.4 228.3 %all-gather.8.cloned.1.call-start = ((), (), s32[]{:S(2)}) async-start(), calls=%async_computation.6 | async-start | bytes 8847360 | tf_op jit(solution)/shard_map/all_gather | solution.py:518
  97.7 22.8 %collective-permute-start.7 = (bf16[768,384]{1,0:T(8,128)(2,1)}, bf16[768,384]{1,0:T(8,128)(2,1)S(1)}, u32[]{:S(2)}, u32[]{:S(2)}) collective-permute-start(bf16[768,384]{1,0:T(8,128)(2,1)} %after.13), channel_id=1, source_target_pairs={{0,1},{1,0},{2,3},{3,2},{4,5},{5,4},{6,7},{7,6},{8,9},{9,8},{10,11... | collective-permute-start | bytes 1769480 | tf_op jit(solution)/shard_map/ppermute | solution.py:419
  119.1 20.6 %collective-permute-start.6 = (bf16[384,1024]{1,0:T(8,128)(2,1)S(1)}, bf16[384,1024]{1,0:T(8,128)(2,1)}, u32[]{:S(2)}, u32[]{:S(2)}) collective-permute-start(bf16[384,1024]{1,0:T(8,128)(2,1)S(1)} %bitcast.186), channel_id=1, source_target_pairs={{0,16},{8,24},{16,0},{24,8},{1,17},{9,25},{17,1},{25,9},{2,18},{10... | collective-permute-start | bytes 2359304 | tf_op jit(solution)/shard_map/ppermute | solution.py:414
  121.9 40.8 %collective-permute-start.10 = (bf16[1,1536,384]{2,1,0:T(8,128)(2,1)}, bf16[1,1536,384]{2,1,0:T(8,128)(2,1)}, u32[]{:S(2)}, u32[]{:S(2)}) collective-permute-start(bf16[1,1536,384]{2,1,0:T(8,128)(2,1)} %bitcast.37), channel_id=1, source_target_pairs={{0,16},{8,24},{16,0},{24,8},{1,17},{9,25},{17,1},{25,9},{2,18},{10... | collective-permute-start | bytes 3538952 | tf_op jit(solution)/shard_map/ppermute | solution.py:414
  123.8 42.1 %collective-permute-start.9 = (bf16[192,2304]{1,0:T(8,128)(2,1)}, bf16[192,2304]{1,0:T(8,128)(2,1)}, u32[]{:S(2)}, u32[]{:S(2)}) collective-permute-start(bf16[192,2304]{1,0:T(8,128)(2,1)} %after.15), channel_id=1, source_target_pairs={{0,8},{1,0},{2,10},{3,2},{4,12},{5,4},{6,14},{7,6},{8,9},{9,1},{10... | collective-permute-start | bytes 2654216 | tf_op jit(solution)/shard_map/ppermute | solution.py:509
  123.8 42.1 %collective-permute-start.8 = (bf16[192,2304]{1,0:T(8,128)(2,1)}, bf16[192,2304]{1,0:T(8,128)(2,1)S(1)}, u32[]{:S(2)}, u32[]{:S(2)}) collective-permute-start(bf16[192,2304]{1,0:T(8,128)(2,1)} %after.14), channel_id=1, source_target_pairs={{0,0},{1,8},{2,2},{3,10},{4,4},{5,12},{6,6},{7,14},{8,1},{9,9},{10... | collective-permute-start | bytes 2654216 | tf_op jit(solution)/shard_map/ppermute | solution.py:509
  169.1 245.3 %reduce-scatter.4.cloned.1.call-start = ((), (), s32[]{:S(2)}) async-start(), calls=%async_computation.7 | async-start | bytes 5898240 | tf_op jit(solution)/shard_map/reduce_scatter | solution.py:522
  169.3 37.6 %collective-permute-start.16 = (bf16[512,1536]{1,0:T(8,128)(2,1)}, bf16[512,1536]{1,0:T(8,128)(2,1)}, u32[]{:S(2)}, u32[]{:S(2)}) collective-permute-start(bf16[512,1536]{1,0:T(8,128)(2,1)} %pad_maximum_fusion.10.refs_1_), channel_id=1, source_target_pairs={{0,1},{1,0},{2,3},{3,2},{4,5},{5,4},{6,7},{7,6},{8,9},{9,8},{10,11... | collective-permute-start | bytes 4718600 | tf_op jit(solution)/shard_map/ppermute | solution.py:419
  193.5 46.2 %collective-permute-start.13 = (bf16[512,1536]{1,0:T(8,128)(2,1)S(1)}, bf16[512,1536]{1,0:T(8,128)(2,1)}, u32[]{:S(2)}, u32[]{:S(2)}) collective-permute-start(bf16[512,1536]{1,0:T(8,128)(2,1)S(1)} %slice.492), channel_id=1, source_target_pairs={{0,1},{1,0},{2,3},{3,2},{4,5},{5,4},{6,7},{7,6},{8,9},{9,8},{10,11... | collective-permute-start | bytes 4718600 | tf_op jit(solution)/shard_map/ppermute | solution.py:419
  194.2 45.8 %collective-permute-start.15 = (bf16[512,1536]{1,0:T(8,128)(2,1)}, bf16[512,1536]{1,0:T(8,128)(2,1)}, u32[]{:S(2)}, u32[]{:S(2)}) collective-permute-start(bf16[512,1536]{1,0:T(8,128)(2,1)} %pad_maximum_fusion.10.refs_1_), channel_id=1, source_target_pairs={{0,8},{8,0},{16,24},{24,16},{1,9},{9,1},{17,25},{25,17},{2,10},{10... | collective-permute-start | bytes 4718600 | tf_op jit(solution)/shard_map/ppermute | solution.py:414
  207.0 44.4 %collective-permute-start.17 = (bf16[512,1536]{1,0:T(8,128)(2,1)}, bf16[512,1536]{1,0:T(8,128)(2,1)}, u32[]{:S(2)}, u32[]{:S(2)}) collective-permute-start(bf16[512,1536]{1,0:T(8,128)(2,1)} %collective-permute-done.16.refs_4_), channel_id=1, source_target_pairs={{0,8},{8,0},{16,24},{24,16},{1,9},{9,1},{17,25},{25,17},{2,10},{10... | collective-permute-start | bytes 4718600 | tf_op jit(solution)/shard_map/ppermute | solution.py:414
  288.7 261.0 %reduce-scatter.6.cloned.1.call-start = ((), (), s32[]{:S(2)}) async-start(), calls=%async_computation.8 | async-start | bytes 8847360 | tf_op jit(solution)/shard_map/reduce_scatter | solution.py:522
  364.7 20.5 %collective-permute-start.23 = (bf16[512,768]{1,0:T(8,128)(2,1)S(1)}, bf16[512,768]{1,0:T(8,128)(2,1)S(1)}, u32[]{:S(2)}, u32[]{:S(2)}) collective-permute-start(bf16[512,768]{1,0:T(8,128)(2,1)S(1)} %slice.496), channel_id=1, source_target_pairs={{0,1},{1,0},{2,3},{3,2},{4,5},{5,4},{6,7},{7,6},{8,9},{9,8},{10,11... | collective-permute-start | bytes 2359304 | tf_op jit(solution)/shard_map/ppermute | solution.py:419
  414.5 171.1 %reduce-scatter.8.cloned.1.call-start = ((), (), s32[]{:S(2)}) async-start(), calls=%async_computation.9 | async-start | bytes 2211840 | tf_op jit(solution)/shard_map/reduce_scatter | solution.py:522
  418.4 71.3 %collective-permute-start.45 = (bf16[192,1536]{1,0:T(8,128)(2,1)}, bf16[192,1536]{1,0:T(8,128)(2,1)}, u32[]{:S(2)}, u32[]{:S(2)}) collective-permute-start(bf16[192,1536]{1,0:T(8,128)(2,1)} %get-tuple-element.136), channel_id=1, source_target_pairs={{0,0},{8,1},{2,2},{10,3},{4,4},{12,5},{6,6},{14,7},{1,8},{9,9},{3,... | collective-permute-start | bytes 1769480 | tf_op jit(solution)/shard_map/ppermute | solution.py:509
  424.4 65.8 %collective-permute-start.46 = (bf16[192,1536]{1,0:T(8,128)(2,1)}, bf16[192,1536]{1,0:T(8,128)(2,1)}, u32[]{:S(2)}, u32[]{:S(2)}) collective-permute-start(bf16[192,1536]{1,0:T(8,128)(2,1)} %get-tuple-element.137), channel_id=1, source_target_pairs={{8,0},{0,1},{10,2},{2,3},{12,4},{4,5},{14,6},{6,7},{9,8},{1,9},{11... | collective-permute-start | bytes 1769480 | tf_op jit(solution)/shard_map/ppermute | solution.py:509
  463.2 42.4 %collective-permute-start.43 = (bf16[768,768]{1,0:T(8,128)(2,1)}, bf16[768,768]{1,0:T(8,128)(2,1)}, u32[]{:S(2)}, u32[]{:S(2)}) collective-permute-start(bf16[768,768]{1,0:T(8,128)(2,1)} %bitcast.60), channel_id=1, source_target_pairs={{0,1},{1,0},{2,3},{3,2},{4,5},{5,4},{6,7},{7,6},{8,9},{9,8},{10,11... | collective-permute-start | bytes 3538952 | tf_op jit(solution)/shard_map/ppermute | solution.py:419
  472.4 32.0 %collective-permute-start.44 = (bf16[768,384]{1,0:T(8,128)(2,1)}, bf16[768,384]{1,0:T(8,128)(2,1)}, u32[]{:S(2)}, u32[]{:S(2)}) collective-permute-start(bf16[768,384]{1,0:T(8,128)(2,1)} %bitcast.65), channel_id=1, source_target_pairs={{0,1},{1,0},{2,3},{3,2},{4,5},{5,4},{6,7},{7,6},{8,9},{9,8},{10,11... | collective-permute-start | bytes 1769480 | tf_op jit(solution)/shard_map/ppermute | solution.py:419
  488.1 25.8 %collective-permute-start.34 = (bf16[512,1536]{1,0:T(8,128)(2,1)}, bf16[512,1536]{1,0:T(8,128)(2,1)S(1)}, u32[]{:S(2)}, u32[]{:S(2)}) collective-permute-start(bf16[512,1536]{1,0:T(8,128)(2,1)} %get-tuple-element.47), channel_id=1, source_target_pairs={{0,8},{8,0},{16,24},{24,16},{1,9},{9,1},{17,25},{25,17},{2,10},{10... | collective-permute-start | bytes 4718600 | tf_op jit(solution)/shard_map/ppermute | solution.py:414
  490.3 22.6 %collective-permute-start.41 = (bf16[512,1536]{1,0:T(8,128)(2,1)S(1)}, bf16[512,1536]{1,0:T(8,128)(2,1)S(1)}, u32[]{:S(2)}, u32[]{:S(2)}) collective-permute-start(bf16[512,1536]{1,0:T(8,128)(2,1)S(1)} %split.107), channel_id=1, source_target_pairs={{0,8},{8,0},{16,24},{24,16},{1,9},{9,1},{17,25},{25,17},{2,10},{10... | collective-permute-start | bytes 4718600 | tf_op jit(solution)/shard_map/ppermute | solution.py:414
  513.3 26.9 %collective-permute-start.42 = (bf16[256,1536]{1,0:T(8,128)(2,1)S(1)}, bf16[256,1536]{1,0:T(8,128)(2,1)S(1)}, u32[]{:S(2)}, u32[]{:S(2)}) collective-permute-start(bf16[256,1536]{1,0:T(8,128)(2,1)S(1)} %split.109), channel_id=1, source_target_pairs={{0,16},{8,24},{16,0},{24,8},{1,17},{9,25},{17,1},{25,9},{2,18},{10... | collective-permute-start | bytes 2359304 | tf_op jit(solution)/shard_map/ppermute | solution.py:414
  515.1 33.6 %collective-permute-start.38 = (bf16[256,768]{1,0:T(8,128)(2,1)S(1)}, bf16[256,768]{1,0:T(8,128)(2,1)S(1)}, u32[]{:S(2)}, u32[]{:S(2)}) collective-permute-start(bf16[256,768]{1,0:T(8,128)(2,1)S(1)} %split.103), channel_id=1, source_target_pairs={{0,16},{8,24},{16,0},{24,8},{1,17},{9,25},{17,1},{25,9},{2,18},{10... | collective-permute-start | bytes 1179656 | tf_op jit(solution)/shard_map/ppermute | solution.py:414
  523.5 25.2 %collective-permute-start.40 = (bf16[256,768]{1,0:T(8,128)(2,1)S(1)}, bf16[256,768]{1,0:T(8,128)(2,1)S(1)}, u32[]{:S(2)}, u32[]{:S(2)}) collective-permute-start(bf16[256,768]{1,0:T(8,128)(2,1)S(1)} %add_convert_fusion.8), channel_id=1, source_target_pairs={{0,1},{1,0},{2,3},{3,2},{4,5},{5,4},{6,7},{7,6},{8,9},{9,8},{10,11... | collective-permute-start | bytes 1179656 | tf_op jit(solution)/shard_map/ppermute | solution.py:419
  531.5 23.6 %collective-permute-start.37 = (bf16[256,768]{1,0:T(8,128)(2,1)}, bf16[256,768]{1,0:T(8,128)(2,1)}, u32[]{:S(2)}, u32[]{:S(2)}) collective-permute-start(bf16[256,768]{1,0:T(8,128)(2,1)} %split.101), channel_id=1, source_target_pairs={{0,16},{8,24},{16,0},{24,8},{1,17},{9,25},{17,1},{25,9},{2,18},{10... | collective-permute-start | bytes 1179656 | tf_op jit(solution)/shard_map/ppermute | solution.py:414
  552.2 21.2 %collective-permute-start.48 = (bf16[192,2304]{1,0:T(8,128)(2,1)S(1)}, bf16[192,2304]{1,0:T(8,128)(2,1)S(1)}, u32[]{:S(2)}, u32[]{:S(2)}) collective-permute-start(bf16[192,2304]{1,0:T(8,128)(2,1)S(1)} %get-tuple-element.127), channel_id=1, source_target_pairs={{8,0},{0,1},{10,2},{2,3},{12,4},{4,5},{14,6},{6,7},{9,8},{1,9},{11... | collective-permute-start | bytes 2654216 | tf_op jit(solution)/shard_map/ppermute | solution.py:509
  (91 other events, 797.1 us)
Sparse Core Ops, SparseCore 0:
  16.9 40.6 all-gather.3
  67.5 87.3 all-gather.5
  169.2 126.4 all-gather.7
  297.9 83.4 reduce-scatter.3
  414.6 121.7 reduce-scatter.5
  549.8 35.6 reduce-scatter.7

commit v5 on v4

--- a/solution.py
+++ b/solution.py
@@ -361,7 +361,7 @@
         ],
         compiler_params=pltpu.CompilerParams(vmem_limit_bytes=60 * 1024 * 1024),
         cost_estimate=pl.CostEstimate(
-            flops=26 * count * n * half * width,
+            flops=16 * count * n * half * width,
             bytes_accessed=8 * count * width + 4 * width * n * half * 3,
             transcendentals=count * n * half,
         ),

time: 618 us -> 641 us (1.037)
  waiting for transfers between devices: 247 us -> 263 us
  local copies, waits for them, and re-layouts: 48.3 us -> 57.1 us
    ppermute x12, waiting for transfers between devices: 99.8 us -> 113 us  [swap_shard(): return lax.ppermute(v, 'shard', [(i, i ^ 1) for i in range(n)])]
    all_gather x3, waiting for transfers between devices: 10.8 us -> 0.04 us  [gather_line(): lax.all_gather(v, 'shard', axis=0, tiled=True, axis_index_groups=shard_li...]
    unnamed x153 -> x151, local copies, waits for them, and re-layouts: 24.7 us -> 35 us
    ppermute x8, waiting for transfers between devices: 13.4 us -> 20.3 us  [permute_all(): return lax.ppermute(v, ('expert', 'shard'), pairs)]
  transfers between devices with their start and end apart: 56 -> 56, of which waited for: 29 -> 27; matrix products, arithmetic and copies ran while one was open for 21% -> 21% of each run, Pallas kernels for 24% -> 23%
where the time goes in v5:
time: 641 us; the launch traced here: 631 us
  waiting for transfers between devices  263 us (41%)
  Pallas kernels  145 us (23%)
  other arithmetic  68.1 us (11%)
  local copies, waits for them, and re-layouts  57.1 us (9%)
  starting transfers between devices  46.5 us (7%)
  matrix products  35.1 us (5%)
  between operations  16 us (2%)
    ppermute x29, waiting for transfers between devices, swap_member(): return lax.ppermute(v, 'expert', [(i, i ^ bit) for i in range(n)])  115 us
    ppermute x12, waiting for transfers between devices, swap_shard(): return lax.ppermute(v, 'shard', [(i, i ^ 1) for i in range(n)])  113 us
    pallas_call x2, Pallas kernels, expert_chunk(): pl.pallas_call(functools.partial(expert_kernel, js[0], n, half, tiles, ba...  92.2 us
    unnamed x151, local copies, waits for them, and re-layouts  35 us
    dot_general x8, matrix products, dot(): lax.dot_general(a, b, (((ca,), (cb,)), ((), ())), preferred_element_type=...  31.3 us
    ppermute x8, waiting for transfers between devices, permute_all(): return lax.ppermute(v, ('expert', 'shard'), pairs)  20.3 us
    pallas_call x1, Pallas kernels, attention_forward(): pl.pallas_call(functools.partial(attention_forward_kernel, blocks), grid_...  17.6 us
    ppermute x8, starting transfers between devices, permute_all(): return lax.ppermute(v, ('expert', 'shard'), pairs)  17.3 us
  transfers between devices with their start and end apart: 56, of which 27 were waited for; matrix products, arithmetic and copies ran while one was open for 21% of the time, Pallas kernels for 23%

profile of v5, /device:TPU:0, one launch (start us, length us, event | category | flops | bytes accessed | tf_op | source)
XLA Modules:
  0.0 630.6 jit_solution(1504220604753810833)
XLA Ops:
  27.5 7.0 %collective-permute-done = bf16[256,1536]{1,0:T(8,128)(2,1)S(1)} collective-permute-done((bf16[256,1536]{1,0:T(8,128)(2,1)}, bf16[256,1536]{1,0:T(8,128)(2,1)S(1)}, u32[]{:S(2)}, u32[]{:S(2)}) %collective-permute-start) | collective-permute-done | bytes 786464 | tf_op jit(solution)/shard_map/ppermute | solution.py:414
  45.4 6.0 collective-permute-start.19
  57.4 6.5 %collective-permute-done.20 = bf16[192,1536]{1,0:T(8,128)(2,1)} collective-permute-done((bf16[192,1536]{1,0:T(8,128)(2,1)}, bf16[192,1536]{1,0:T(8,128)(2,1)}, u32[]{:S(2)}, u32[]{:S(2)}) %collective-permute-start.20) | collective-permute-done | bytes 589856 | tf_op jit(solution)/shard_map/ppermute | solution.py:509
  68.8 8.6 %collective-permute-done.2 = bf16[256,1536]{1,0:T(8,128)(2,1)S(1)} collective-permute-done((bf16[256,1536]{1,0:T(8,128)(2,1)}, bf16[256,1536]{1,0:T(8,128)(2,1)S(1)}, u32[]{:S(2)}, u32[]{:S(2)}) %collective-permute-start.2) | collective-permute-done | bytes 786464 | tf_op jit(solution)/shard_map/ppermute | solution.py:414
  86.4 20.7 %collective-permute-done.3 = bf16[768,768]{1,0:T(8,128)(2,1)S(1)} collective-permute-done((bf16[768,768]{1,0:T(8,128)(2,1)}, bf16[768,768]{1,0:T(8,128)(2,1)S(1)}, u32[]{:S(2)}, u32[]{:S(2)}) %collective-permute-start.3) | collective-permute-done | bytes 1179680 | tf_op jit(solution)/shard_map/ppermute | solution.py:419
  111.2 4.3 fusion.15
  116.4 7.5 %collective-permute-done.7 = bf16[768,384]{1,0:T(8,128)(2,1)S(1)} collective-permute-done((bf16[768,384]{1,0:T(8,128)(2,1)}, bf16[768,384]{1,0:T(8,128)(2,1)S(1)}, u32[]{:S(2)}, u32[]{:S(2)}) %collective-permute-start.7) | collective-permute-done | bytes 589856 | tf_op jit(solution)/shard_map/ppermute | solution.py:419
  127.1 17.6 %attention_forward.1 = (bf16[6,64,1024]{2,1,0:T(8,128)(2,1)S(1)}, f32[6,1,1024]{2,1,0:T(1,128)S(1)}) custom-call(s32[1]{0:T(128)} %bitcast.1.me_ref, bf16[6,64,1024]{2,1,0:T(8,128)(2,1)S(1)} %fusion.31.q_ref, bf16[2,64,1024]{2,1,0:T(8,128)(2,1)S(1)} %pad_maximum_fusion.17.k_ref, bf16[2,64,1024]{2,1,0:T(8,128)(2,1)S(1)} %bitcast.189, ...), custom_call_target="tpu_custom_call" | custom-call | flops 20132659200 | bytes 2359296 | tf_op jit(solution)/shard_map/attention_forward/pallas_call | solution.py:84
  148.5 40.7 %collective-permute-done.10 = bf16[1,1536,384]{2,1,0:T(8,128)(2,1)} collective-permute-done((bf16[1,1536,384]{2,1,0:T(8,128)(2,1)}, bf16[1,1536,384]{2,1,0:T(8,128)(2,1)}, u32[]{:S(2)}, u32[]{:S(2)}) %collective-permute-start.10) | collective-permute-done | bytes 1179680 | tf_op jit(solution)/shard_map/ppermute | solution.py:414
  208.7 5.9 multiply_reduce_fusion
  219.3 14.8 %collective-permute-done.16.refs_4_ = bf16[512,1536]{1,0:T(8,128)(2,1)} collective-permute-done((bf16[512,1536]{1,0:T(8,128)(2,1)}, bf16[512,1536]{1,0:T(8,128)(2,1)}, u32[]{:S(2)}, u32[]{:S(2)}) %collective-permute-start.16) | collective-permute-done | bytes 1572896 | tf_op jit(solution)/shard_map/ppermute | solution.py:419
  234.1 33.3 %collective-permute-done.13.refs_1_ = bf16[512,1536]{1,0:T(8,128)(2,1)} collective-permute-done((bf16[512,1536]{1,0:T(8,128)(2,1)S(1)}, bf16[512,1536]{1,0:T(8,128)(2,1)}, u32[]{:S(2)}, u32[]{:S(2)}) %collective-permute-start.13) | collective-permute-done | bytes 1572896 | tf_op jit(solution)/shard_map/ppermute | solution.py:419
  274.8 4.3 collective-permute-done.18
  279.7 37.3 %experts.2 = (f32[2048,1536]{1,0:T(8,128)}, bf16[2048,512]{1,0:T(8,128)(2,1)}, f32[2,2048]{1,0:T(2,128)}, bf16[1536,1536]{1,0:T(8,128)(2,1)}) custom-call(bf16[1024,1536]{1,0:T(8,128)(2,1)} %copy-done.2, bf16[512,1536]{1,0:T(8,128)(2,1)} %collective-permute-done.13.refs_1_, bf16[512,1536]{1,0:T(8,128)(2,1)} %collective-permute-done.14.refs_2_, ...), custom_call_target="tpu_custom_call" | custom-call | flops 25769803776 | bytes 34603008 | tf_op jit(solution)/shard_map/experts/pallas_call | solution.py:336
  317.1 54.9 %experts.3 = (bf16[512,1536]{1,0:T(8,128)(2,1)}, bf16[512,1536]{1,0:T(8,128)(2,1)}, bf16[512,1536]{1,0:T(8,128)(2,1)}, bf16[512,1536]{1,0:T(8,128)(2,1)}, bf16[2...) custom-call(bf16[1024,1536]{1,0:T(8,128)(2,1)} %copy-done.2, ...), custom_call_target="tpu_custom_call" | custom-call | flops 38654705664 | bytes 39321600 | tf_op jit(solution)/shard_map/experts/pallas_call | solution.py:336
  388.5 9.5 %collective-permute-done.26 = bf16[256,768]{1,0:T(8,128)(2,1)S(1)} collective-permute-done((bf16[256,768]{1,0:T(8,128)(2,1)S(1)}, bf16[256,768]{1,0:T(8,128)(2,1)S(1)}, u32[]{:S(2)}, u32[]{:S(2)}) %collective-permute-start.26) | collective-permute-done | bytes 393248 | tf_op jit(solution)/shard_map/ppermute | solution.py:414
  400.2 6.2 collective-permute-done.23
  407.1 5.4 collective-permute-done.27
  418.0 15.0 %collective-permute-done.32 = bf16[256,1536]{1,0:T(8,128)(2,1)S(1)} collective-permute-done((bf16[256,1536]{1,0:T(8,128)(2,1)S(1)}, bf16[256,1536]{1,0:T(8,128)(2,1)S(1)}, u32[]{:S(2)}, u32[]{:S(2)}) %collective-permute-start.32) | collective-permute-done | bytes 786464 | tf_op jit(solution)/shard_map/ppermute | solution.py:414
  438.4 6.0 collective-permute-start.45
  447.7 15.9 %attention_backward.1 = (f32[6,64,1024]{2,1,0:T(8,128)S(1)}, f32[2,64,1024]{2,1,0:T(8,128)S(1)}, f32[2,64,1024]{2,1,0:T(8,128)S(1)}) custom-call(s32[1]{0:T(128)} %bitcast.1.me_ref, bf16[6,64,1024]{2,1,0:T(8,128)(2,1)S(1)} %fusion.31.q_ref, bf16[2,64,1024]{2,1,0:T(8,128)(2,1)S(1)} %pad_maximum_fusion.17.k_ref, bf16[2,64,1024]{2,1,0:T(8,128)(2,1)S(1)} %bitcast.190, ...), custom_call_target="tpu_custom_call" | custom-call | flops 18522046464 | bytes 6291456 | tf_op jit(solution)/shard_map/attention_backward/pallas_call | solution.py:159
  466.4 5.0 fusion.74
  471.5 7.7 %fusion.3 = (bf16[1536]{0:T(1024)(128)(2,1)S(1)}, bf16[1024,1536]{1,0:T(8,128)(2,1)}) fusion(bf16[1024,1536]{1,0:T(8,128)(2,1)} %get-tuple-element.93.refs_1_, f32[1024]{0:T(1024)S(1)} %copy-done.61, bf16[640,1024]{1,0:T(8,128)(2,1)} %after.18, bf16[1536,768]{1,0:T(8,128)(2,1)} %bitcast.201), kind=kOutput, calls=%fused_computation.6 | convolution fusion | flops 2021128704 | bytes 9575424 | tf_op jit(solution)/shard_map/dot_general | solution.py:26
  492.1 15.2 %mix_experts.1 = (bf16[512,1536]{1,0:T(8,128)(2,1)}, bf16[512,1536]{1,0:T(8,128)(2,1)}, bf16[512,1536]{1,0:T(8,128)(2,1)}, bf16[512,1536]{1,0:T(8,128)(2,1)}) custom-call(bf16[2048,512]{1,0:T(8,128)(2,1)} %get-tuple-element.33.refs_0_, bf16[2048,768]{1,0:T(8,128)(2,1)} %get-tuple-element.35.refs_1_, ...), custom_call_target="tpu_custom_call" | custom-call | flops 16106127360 | bytes 12582912 | tf_op jit(solution)/shard_map/mix_experts/pallas_call | solution.py:394
  511.4 12.6 %collective-permute-done.44 = bf16[768,384]{1,0:T(8,128)(2,1)} collective-permute-done((bf16[768,384]{1,0:T(8,128)(2,1)}, bf16[768,384]{1,0:T(8,128)(2,1)}, u32[]{:S(2)}, u32[]{:S(2)}) %collective-permute-start.44) | collective-permute-done | bytes 589856 | tf_op jit(solution)/shard_map/ppermute | solution.py:419
  534.2 7.7 %collective-permute-done.39 = bf16[256,768]{1,0:T(8,128)(2,1)S(1)} collective-permute-done((bf16[256,768]{1,0:T(8,128)(2,1)S(1)}, bf16[256,768]{1,0:T(8,128)(2,1)S(1)}, u32[]{:S(2)}, u32[]{:S(2)}) %collective-permute-start.39) | collective-permute-done | bytes 393248 | tf_op jit(solution)/shard_map/ppermute | solution.py:414
  543.7 6.2 collective-permute-done.36
  551.4 7.5 %collective-permute-done.42 = bf16[256,1536]{1,0:T(8,128)(2,1)S(1)} collective-permute-done((bf16[256,1536]{1,0:T(8,128)(2,1)S(1)}, bf16[256,1536]{1,0:T(8,128)(2,1)S(1)}, u32[]{:S(2)}, u32[]{:S(2)}) %collective-permute-start.42) | collective-permute-done | bytes 786464 | tf_op jit(solution)/shard_map/ppermute | solution.py:414
  559.3 7.9 %collective-permute-done.38 = bf16[256,768]{1,0:T(8,128)(2,1)S(1)} collective-permute-done((bf16[256,768]{1,0:T(8,128)(2,1)S(1)}, bf16[256,768]{1,0:T(8,128)(2,1)S(1)}, u32[]{:S(2)}, u32[]{:S(2)}) %collective-permute-start.38) | collective-permute-done | bytes 393248 | tf_op jit(solution)/shard_map/ppermute | solution.py:414
  579.1 13.9 %collective-permute-done.48 = bf16[192,2304]{1,0:T(8,128)(2,1)S(1)} collective-permute-done((bf16[192,2304]{1,0:T(8,128)(2,1)S(1)}, bf16[192,2304]{1,0:T(8,128)(2,1)S(1)}, u32[]{:S(2)}, u32[]{:S(2)}) %collective-permute-start.48) | collective-permute-done | bytes 884768 | tf_op jit(solution)/shard_map/ppermute | solution.py:509
  599.0 9.3 %reduce-scatter.8.cloned.1.call-done = bf16[192,1152]{1,0:T(8,128)(2,1)} async-done(((bf16[768,1152]{1,0:T(8,128)(2,1)}), bf16[192,1152]{1,0:T(8,128)(2,1)}) %reduce-scatter.8.cloned.1.call-update) | async-done | bytes 442384 | tf_op jit(solution)/shard_map/reduce_scatter | solution.py:522
  615.2 4.7 all-to-all-done
  (406 shorter events, 189.7 us)
Async XLA Ops:
  7.2 59.2 %all-gather.4.cloned.1.call-start = ((), (), s32[]{:S(2)}) async-start(), calls=%async_computation.4 | async-start | bytes 2211840 | tf_op jit(solution)/shard_map/all_gather | solution.py:518
  13.7 266.0 %all-gather.6.cloned.1.call-start = ((), (), s32[]{:S(2)}) async-start(), calls=%async_computation.5 | async-start | bytes 5898240 | tf_op jit(solution)/shard_map/all_gather | solution.py:518
  13.8 20.8 %collective-permute-start = (bf16[256,1536]{1,0:T(8,128)(2,1)}, bf16[256,1536]{1,0:T(8,128)(2,1)S(1)}, u32[]{:S(2)}, u32[]{:S(2)}) collective-permute-start(bf16[256,1536]{1,0:T(8,128)(2,1)} %bitcast.195), channel_id=1, source_target_pairs={{0,16},{8,24},{16,0},{24,8},{1,17},{9,25},{17,1},{25,9},{2,18},{10... | collective-permute-start | bytes 2359304 | tf_op jit(solution)/shard_map/ppermute | solution.py:414
  51.4 31.5 %collective-permute-start.4 = (s32[9,256]{1,0:T(8,128)S(1)}, s32[9,256]{1,0:T(8,128)S(1)}, u32[]{:S(2)}, u32[]{:S(2)}) collective-permute-start(s32[9,256]{1,0:T(8,128)S(1)} %pad_add_fusion.4), channel_id=1, source_target_pairs={{0,16},{8,24},{16,0},{24,8},{1,17},{9,25},{17,1},{25,9},{2,18},{10... | collective-permute-start | bytes 27656 | tf_op jit(solution)/shard_map/ppermute | solution.py:414
  57.1 20.2 %collective-permute-start.2 = (bf16[256,1536]{1,0:T(8,128)(2,1)}, bf16[256,1536]{1,0:T(8,128)(2,1)S(1)}, u32[]{:S(2)}, u32[]{:S(2)}) collective-permute-start(bf16[256,1536]{1,0:T(8,128)(2,1)} %after.11), channel_id=1, source_target_pairs={{0,16},{8,24},{16,0},{24,8},{1,17},{9,25},{17,1},{25,9},{2,18},{10... | collective-permute-start | bytes 2359304 | tf_op jit(solution)/shard_map/ppermute | solution.py:414
  66.3 250.8 %all-gather.8.cloned.1.call-start = ((), (), s32[]{:S(2)}) async-start(), calls=%async_computation.6 | async-start | bytes 8847360 | tf_op jit(solution)/shard_map/all_gather | solution.py:518
  78.7 28.3 %collective-permute-start.3 = (bf16[768,768]{1,0:T(8,128)(2,1)}, bf16[768,768]{1,0:T(8,128)(2,1)S(1)}, u32[]{:S(2)}, u32[]{:S(2)}) collective-permute-start(bf16[768,768]{1,0:T(8,128)(2,1)} %after.12), channel_id=1, source_target_pairs={{0,1},{1,0},{2,3},{3,2},{4,5},{5,4},{6,7},{7,6},{8,9},{9,8},{10,11... | collective-permute-start | bytes 3538952 | tf_op jit(solution)/shard_map/ppermute | solution.py:419
  125.2 21.5 %collective-permute-start.9 = (bf16[192,2304]{1,0:T(8,128)(2,1)}, bf16[192,2304]{1,0:T(8,128)(2,1)S(1)}, u32[]{:S(2)}, u32[]{:S(2)}) collective-permute-start(bf16[192,2304]{1,0:T(8,128)(2,1)} %after.15), channel_id=1, source_target_pairs={{0,8},{1,0},{2,10},{3,2},{4,12},{5,4},{6,14},{7,6},{8,9},{9,1},{10... | collective-permute-start | bytes 2654216 | tf_op jit(solution)/shard_map/ppermute | solution.py:509
  125.2 21.5 %collective-permute-start.8 = (bf16[192,2304]{1,0:T(8,128)(2,1)}, bf16[192,2304]{1,0:T(8,128)(2,1)S(1)}, u32[]{:S(2)}, u32[]{:S(2)}) collective-permute-start(bf16[192,2304]{1,0:T(8,128)(2,1)} %after.14), channel_id=1, source_target_pairs={{0,0},{1,8},{2,2},{3,10},{4,4},{5,12},{6,6},{7,14},{8,1},{9,9},{10... | collective-permute-start | bytes 2654216 | tf_op jit(solution)/shard_map/ppermute | solution.py:509
  144.6 49.3 %collective-permute-start.6 = (bf16[384,1024]{1,0:T(8,128)(2,1)S(1)}, bf16[384,1024]{1,0:T(8,128)(2,1)}, u32[]{:S(2)}, u32[]{:S(2)}) collective-permute-start(bf16[384,1024]{1,0:T(8,128)(2,1)S(1)} %bitcast.186), channel_id=1, source_target_pairs={{0,16},{8,24},{16,0},{24,8},{1,17},{9,25},{17,1},{25,9},{2,18},{10... | collective-permute-start | bytes 2359304 | tf_op jit(solution)/shard_map/ppermute | solution.py:414
  145.3 43.9 %collective-permute-start.10 = (bf16[1,1536,384]{2,1,0:T(8,128)(2,1)}, bf16[1,1536,384]{2,1,0:T(8,128)(2,1)}, u32[]{:S(2)}, u32[]{:S(2)}) collective-permute-start(bf16[1,1536,384]{2,1,0:T(8,128)(2,1)} %bitcast.37), channel_id=1, source_target_pairs={{0,16},{8,24},{16,0},{24,8},{1,17},{9,25},{17,1},{25,9},{2,18},{10... | collective-permute-start | bytes 3538952 | tf_op jit(solution)/shard_map/ppermute | solution.py:414
  148.2 286.2 %reduce-scatter.4.cloned.1.call-start = ((), (), s32[]{:S(2)}) async-start(), calls=%async_computation.7 | async-start | bytes 5898240 | tf_op jit(solution)/shard_map/reduce_scatter | solution.py:522
  196.6 37.5 %collective-permute-start.16 = (bf16[512,1536]{1,0:T(8,128)(2,1)}, bf16[512,1536]{1,0:T(8,128)(2,1)}, u32[]{:S(2)}, u32[]{:S(2)}) collective-permute-start(bf16[512,1536]{1,0:T(8,128)(2,1)} %pad_maximum_fusion.10.refs_1_), channel_id=1, source_target_pairs={{0,1},{1,0},{2,3},{3,2},{4,5},{5,4},{6,7},{7,6},{8,9},{9,8},{10,11... | collective-permute-start | bytes 4718600 | tf_op jit(solution)/shard_map/ppermute | solution.py:419
  218.9 48.5 %collective-permute-start.13 = (bf16[512,1536]{1,0:T(8,128)(2,1)S(1)}, bf16[512,1536]{1,0:T(8,128)(2,1)}, u32[]{:S(2)}, u32[]{:S(2)}) collective-permute-start(bf16[512,1536]{1,0:T(8,128)(2,1)S(1)} %slice.492), channel_id=1, source_target_pairs={{0,1},{1,0},{2,3},{3,2},{4,5},{5,4},{6,7},{7,6},{8,9},{9,8},{10,11... | collective-permute-start | bytes 4718600 | tf_op jit(solution)/shard_map/ppermute | solution.py:419
  219.0 49.2 %collective-permute-start.15 = (bf16[512,1536]{1,0:T(8,128)(2,1)}, bf16[512,1536]{1,0:T(8,128)(2,1)}, u32[]{:S(2)}, u32[]{:S(2)}) collective-permute-start(bf16[512,1536]{1,0:T(8,128)(2,1)} %pad_maximum_fusion.10.refs_1_), channel_id=1, source_target_pairs={{0,8},{8,0},{16,24},{24,16},{1,9},{9,1},{17,25},{25,17},{2,10},{10... | collective-permute-start | bytes 4718600 | tf_op jit(solution)/shard_map/ppermute | solution.py:414
  234.1 45.7 %collective-permute-start.17 = (bf16[512,1536]{1,0:T(8,128)(2,1)}, bf16[512,1536]{1,0:T(8,128)(2,1)}, u32[]{:S(2)}, u32[]{:S(2)}) collective-permute-start(bf16[512,1536]{1,0:T(8,128)(2,1)} %collective-permute-done.16.refs_4_), channel_id=1, source_target_pairs={{0,8},{8,0},{16,24},{24,16},{1,9},{9,1},{17,25},{25,17},{2,10},{10... | collective-permute-start | bytes 4718600 | tf_op jit(solution)/shard_map/ppermute | solution.py:414
  317.0 251.2 %reduce-scatter.6.cloned.1.call-start = ((), (), s32[]{:S(2)}) async-start(), calls=%async_computation.8 | async-start | bytes 8847360 | tf_op jit(solution)/shard_map/reduce_scatter | solution.py:522
  385.8 20.5 %collective-permute-start.23 = (bf16[512,768]{1,0:T(8,128)(2,1)S(1)}, bf16[512,768]{1,0:T(8,128)(2,1)S(1)}, u32[]{:S(2)}, u32[]{:S(2)}) collective-permute-start(bf16[512,768]{1,0:T(8,128)(2,1)S(1)} %slice.496), channel_id=1, source_target_pairs={{0,1},{1,0},{2,3},{3,2},{4,5},{5,4},{6,7},{7,6},{8,9},{9,8},{10,11... | collective-permute-start | bytes 2359304 | tf_op jit(solution)/shard_map/ppermute | solution.py:419
  387.6 19.5 %collective-permute-start.25 = (bf16[256,768]{1,0:T(8,128)(2,1)S(1)}, bf16[256,768]{1,0:T(8,128)(2,1)S(1)}, u32[]{:S(2)}, u32[]{:S(2)}) collective-permute-start(bf16[256,768]{1,0:T(8,128)(2,1)S(1)} %split.91), channel_id=1, source_target_pairs={{0,16},{8,24},{16,0},{24,8},{1,17},{9,25},{17,1},{25,9},{2,18},{10... | collective-permute-start | bytes 1179656 | tf_op jit(solution)/shard_map/ppermute | solution.py:414
  434.4 173.9 %reduce-scatter.8.cloned.1.call-start = ((), (), s32[]{:S(2)}) async-start(), calls=%async_computation.9 | async-start | bytes 2211840 | tf_op jit(solution)/shard_map/reduce_scatter | solution.py:522
  438.4 70.6 %collective-permute-start.45 = (bf16[192,1536]{1,0:T(8,128)(2,1)}, bf16[192,1536]{1,0:T(8,128)(2,1)}, u32[]{:S(2)}, u32[]{:S(2)}) collective-permute-start(bf16[192,1536]{1,0:T(8,128)(2,1)} %get-tuple-element.136), channel_id=1, source_target_pairs={{0,0},{8,1},{2,2},{10,3},{4,4},{12,5},{6,6},{14,7},{1,8},{9,9},{3,... | collective-permute-start | bytes 1769480 | tf_op jit(solution)/shard_map/ppermute | solution.py:509
  444.4 65.2 %collective-permute-start.46 = (bf16[192,1536]{1,0:T(8,128)(2,1)}, bf16[192,1536]{1,0:T(8,128)(2,1)}, u32[]{:S(2)}, u32[]{:S(2)}) collective-permute-start(bf16[192,1536]{1,0:T(8,128)(2,1)} %get-tuple-element.137), channel_id=1, source_target_pairs={{8,0},{0,1},{10,2},{2,3},{12,4},{4,5},{14,6},{6,7},{9,8},{1,9},{11... | collective-permute-start | bytes 1769480 | tf_op jit(solution)/shard_map/ppermute | solution.py:509
  482.6 42.6 %collective-permute-start.43 = (bf16[768,768]{1,0:T(8,128)(2,1)}, bf16[768,768]{1,0:T(8,128)(2,1)}, u32[]{:S(2)}, u32[]{:S(2)}) collective-permute-start(bf16[768,768]{1,0:T(8,128)(2,1)} %bitcast.60), channel_id=1, source_target_pairs={{0,1},{1,0},{2,3},{3,2},{4,5},{5,4},{6,7},{7,6},{8,9},{9,8},{10,11... | collective-permute-start | bytes 3538952 | tf_op jit(solution)/shard_map/ppermute | solution.py:419
  491.1 33.0 %collective-permute-start.44 = (bf16[768,384]{1,0:T(8,128)(2,1)}, bf16[768,384]{1,0:T(8,128)(2,1)}, u32[]{:S(2)}, u32[]{:S(2)}) collective-permute-start(bf16[768,384]{1,0:T(8,128)(2,1)} %bitcast.65), channel_id=1, source_target_pairs={{0,1},{1,0},{2,3},{3,2},{4,5},{5,4},{6,7},{7,6},{8,9},{9,8},{10,11... | collective-permute-start | bytes 1769480 | tf_op jit(solution)/shard_map/ppermute | solution.py:419
  507.3 25.1 %collective-permute-start.34 = (bf16[512,1536]{1,0:T(8,128)(2,1)}, bf16[512,1536]{1,0:T(8,128)(2,1)S(1)}, u32[]{:S(2)}, u32[]{:S(2)}) collective-permute-start(bf16[512,1536]{1,0:T(8,128)(2,1)} %get-tuple-element.47), channel_id=1, source_target_pairs={{0,8},{8,0},{16,24},{24,16},{1,9},{9,1},{17,25},{25,17},{2,10},{10... | collective-permute-start | bytes 4718600 | tf_op jit(solution)/shard_map/ppermute | solution.py:414
  509.6 20.9 %collective-permute-start.41 = (bf16[512,1536]{1,0:T(8,128)(2,1)S(1)}, bf16[512,1536]{1,0:T(8,128)(2,1)S(1)}, u32[]{:S(2)}, u32[]{:S(2)}) collective-permute-start(bf16[512,1536]{1,0:T(8,128)(2,1)S(1)} %split.107), channel_id=1, source_target_pairs={{0,8},{8,0},{16,24},{24,16},{1,9},{9,1},{17,25},{25,17},{2,10},{10... | collective-permute-start | bytes 4718600 | tf_op jit(solution)/shard_map/ppermute | solution.py:414
  529.4 20.5 %collective-permute-start.36 = (bf16[512,768]{1,0:T(8,128)(2,1)S(1)}, bf16[512,768]{1,0:T(8,128)(2,1)S(1)}, u32[]{:S(2)}, u32[]{:S(2)}) collective-permute-start(bf16[512,768]{1,0:T(8,128)(2,1)S(1)} %slice.499), channel_id=1, source_target_pairs={{0,1},{1,0},{2,3},{3,2},{4,5},{5,4},{6,7},{7,6},{8,9},{9,8},{10,11... | collective-permute-start | bytes 2359304 | tf_op jit(solution)/shard_map/ppermute | solution.py:419
  531.3 27.5 %collective-permute-start.42 = (bf16[256,1536]{1,0:T(8,128)(2,1)S(1)}, bf16[256,1536]{1,0:T(8,128)(2,1)S(1)}, u32[]{:S(2)}, u32[]{:S(2)}) collective-permute-start(bf16[256,1536]{1,0:T(8,128)(2,1)S(1)} %split.109), channel_id=1, source_target_pairs={{0,16},{8,24},{16,0},{24,8},{1,17},{9,25},{17,1},{25,9},{2,18},{10... | collective-permute-start | bytes 2359304 | tf_op jit(solution)/shard_map/ppermute | solution.py:414
  533.1 34.2 %collective-permute-start.38 = (bf16[256,768]{1,0:T(8,128)(2,1)S(1)}, bf16[256,768]{1,0:T(8,128)(2,1)S(1)}, u32[]{:S(2)}, u32[]{:S(2)}) collective-permute-start(bf16[256,768]{1,0:T(8,128)(2,1)S(1)} %split.103), channel_id=1, source_target_pairs={{0,16},{8,24},{16,0},{24,8},{1,17},{9,25},{17,1},{25,9},{2,18},{10... | collective-permute-start | bytes 1179656 | tf_op jit(solution)/shard_map/ppermute | solution.py:414
  542.1 25.2 %collective-permute-start.40 = (bf16[256,768]{1,0:T(8,128)(2,1)S(1)}, bf16[256,768]{1,0:T(8,128)(2,1)S(1)}, u32[]{:S(2)}, u32[]{:S(2)}) collective-permute-start(bf16[256,768]{1,0:T(8,128)(2,1)S(1)} %add_convert_fusion.8), channel_id=1, source_target_pairs={{0,1},{1,0},{2,3},{3,2},{4,5},{5,4},{6,7},{7,6},{8,9},{9,8},{10,11... | collective-permute-start | bytes 1179656 | tf_op jit(solution)/shard_map/ppermute | solution.py:419
  551.1 23.1 %collective-permute-start.37 = (bf16[256,768]{1,0:T(8,128)(2,1)}, bf16[256,768]{1,0:T(8,128)(2,1)}, u32[]{:S(2)}, u32[]{:S(2)}) collective-permute-start(bf16[256,768]{1,0:T(8,128)(2,1)} %split.101), channel_id=1, source_target_pairs={{0,16},{8,24},{16,0},{24,8},{1,17},{9,25},{17,1},{25,9},{2,18},{10... | collective-permute-start | bytes 1179656 | tf_op jit(solution)/shard_map/ppermute | solution.py:414
  570.8 22.2 %collective-permute-start.48 = (bf16[192,2304]{1,0:T(8,128)(2,1)S(1)}, bf16[192,2304]{1,0:T(8,128)(2,1)S(1)}, u32[]{:S(2)}, u32[]{:S(2)}) collective-permute-start(bf16[192,2304]{1,0:T(8,128)(2,1)S(1)} %get-tuple-element.127), channel_id=1, source_target_pairs={{8,0},{0,1},{10,2},{2,3},{12,4},{4,5},{14,6},{6,7},{9,8},{1,9},{11... | collective-permute-start | bytes 2654216 | tf_op jit(solution)/shard_map/ppermute | solution.py:509
  (90 other events, 1041.0 us)
Sparse Core Ops, SparseCore 0:
  13.8 43.0 all-gather.3
  66.4 89.9 all-gather.5
  158.6 126.6 all-gather.7
  317.1 85.4 reduce-scatter.3
  434.5 124.3 reduce-scatter.5
  568.4 39.8 reduce-scatter.7
